TPU v7x, 32 devices: a whole 2x2x4 slice. The times are simulated.
32 devices in a mesh: seq: 2 (over x), fsdp: 16 (over z, y, core).
Axes of the slice: x: 2, y: 2, z: 4, core: 2. Of those that a mesh axis runs over, the one named last changes fastest.
Arguments:
- tokens: bfloat16 [16, 256, 768], P('fsdp', 'seq'), may hold values from -4 to 4
- cond: bfloat16 [16, 768], P('fsdp'), may hold values from -2.5 to 2.5
- w_ada: bfloat16 [768, 4608], P(('seq', 'fsdp')), may hold values from -0.21875 to 0.21875
- b_ada: bfloat16 [4608], P(('seq', 'fsdp')), may hold values from -1 to 1
- w_qkv: bfloat16 [768, 2304], P(('seq', 'fsdp')), may hold values from -0.3125 to 0.3125
- b_query: bfloat16 [768], P(('seq', 'fsdp')), may hold values from -1.5 to 1.5
- b_value: bfloat16 [768], P(('seq', 'fsdp')), may hold values from -1.5 to 1.5
- w_proj: bfloat16 [768, 768], P(('seq', 'fsdp')), may hold values from -0.875 to 0.875
- b_proj: bfloat16 [768], P(('seq', 'fsdp')), may hold values from -1.5 to 1.5
- w_fc1: bfloat16 [768, 3072], P(('seq', 'fsdp')), may hold values from -0.21875 to 0.21875
- b_fc1: bfloat16 [3072], P(('seq', 'fsdp')), may hold values from -1.5 to 1.5
- w_fc2: bfloat16 [3072, 768], P(('seq', 'fsdp')), may hold values from -0.15625 to 0.15625
- b_fc2: bfloat16 [768], P(('seq', 'fsdp')), may hold values from -1.5 to 1.5
- cotangent: bfloat16 [16, 256, 768], P('fsdp', 'seq'), may hold values from -4 to 4
Outputs:
- output: bfloat16 [16, 256, 768], P('fsdp', 'seq')
- grad_tokens: bfloat16 [16, 256, 768], P('fsdp', 'seq')
- grad_cond: bfloat16 [16, 768], P('fsdp')
- grad_w_ada: float32 [768, 4608], P(('seq', 'fsdp'))
- grad_b_ada: float32 [4608], P(('seq', 'fsdp'))
- grad_w_qkv: float32 [768, 2304], P(('seq', 'fsdp'))
- grad_b_query: float32 [768], P(('seq', 'fsdp'))
- grad_b_value: float32 [768], P(('seq', 'fsdp'))
- grad_w_proj: float32 [768, 768], P(('seq', 'fsdp'))
- grad_b_proj: float32 [768], P(('seq', 'fsdp'))
- grad_w_fc1: float32 [768, 3072], P(('seq', 'fsdp'))
- grad_b_fc1: float32 [3072], P(('seq', 'fsdp'))
- grad_w_fc2: float32 [3072, 768], P(('seq', 'fsdp'))
- grad_b_fc2: float32 [768], P(('seq', 'fsdp'))
All inputs are finite; a program needn't handle non-finite values.
Results may differ from a plain program's by a relative error of at most 0.017.
The roundings to bfloat16 on the way count: a program that leaves them out, or rounds other values in their place, can miss the bound.
Values may be sent and summed in bfloat16 or wider, within the bound.
No kernel may reach another device: no remote copies, remote signals or barrier semaphores. Data moves between devices by JAX's collectives and lax.ppermute only.
A program may use at most 256 MiB of HBM per device.

v0:
```python
import jax
import jax.numpy as jnp
from jax import lax
from jax.sharding import PartitionSpec as P

D = 768
HD = 64
FF = 3072


def normalize(value):
    centre = value - jnp.mean(value, axis=-1, keepdims=True)
    variance = jnp.mean(centre * centre, axis=-1, keepdims=True)
    return centre * lax.rsqrt(variance + 1e-06)


def modulate(value, shift, scale):
    return normalize(value) * (1.0 + scale) + shift


def gelu_tanh(value):
    return (
        0.5
        * value
        * (1.0 + jnp.tanh(0.7978845608028654 * (value + 0.044715 * value * value * value)))
    )


def score_table(query, key):
    scores = jnp.einsum("lqhd,lkhd->lhqk", query, key, preferred_element_type=jnp.float32)
    return scores * HD ** (-0.5)


def local(
    tokens,
    cond,
    w_ada,
    b_ada,
    w_qkv,
    b_query,
    b_value,
    w_proj,
    b_proj,
    w_fc1,
    b_fc1,
    w_fc2,
    b_fc2,
    cotangent,
):
    latents = tokens.shape[0]
    local_len = tokens.shape[1]
    width = tokens.shape[2]
    (
        full_ada,
        bias_ada,
        full_qkv,
        bias_query,
        bias_value,
        full_proj,
        bias_proj,
        full_fc1,
        bias_fc1,
        full_fc2,
        bias_fc2,
    ) = (
        lax.all_gather(w_ada, ("seq", "fsdp"), axis=0, tiled=True),
        lax.all_gather(b_ada, ("seq", "fsdp"), axis=0, tiled=True),
        lax.all_gather(w_qkv, ("seq", "fsdp"), axis=0, tiled=True),
        lax.all_gather(b_query, ("seq", "fsdp"), axis=0, tiled=True),
        lax.all_gather(b_value, ("seq", "fsdp"), axis=0, tiled=True),
        lax.all_gather(w_proj, ("seq", "fsdp"), axis=0, tiled=True),
        lax.all_gather(b_proj, ("seq", "fsdp"), axis=0, tiled=True),
        lax.all_gather(w_fc1, ("seq", "fsdp"), axis=0, tiled=True),
        lax.all_gather(b_fc1, ("seq", "fsdp"), axis=0, tiled=True),
        lax.all_gather(w_fc2, ("seq", "fsdp"), axis=0, tiled=True),
        lax.all_gather(b_fc2, ("seq", "fsdp"), axis=0, tiled=True),
    )
    cond_float = cond.astype(jnp.float32)
    silu_cond = jax.nn.silu(cond_float).astype(jnp.bfloat16)
    modulation = jnp.dot(silu_cond, full_ada, preferred_element_type=jnp.float32) + bias_ada.astype(
        jnp.float32
    )
    parts = [modulation[:, None, index * width : (index + 1) * width] for index in range(6)]
    shift_attn, scale_attn, gate_attn, shift_mlp, scale_mlp, gate_mlp = parts
    residual = tokens.astype(jnp.float32)
    h_attn = modulate(residual, shift_attn, scale_attn).astype(jnp.bfloat16)
    bias_qkv = jnp.concatenate([bias_query, jnp.zeros_like(bias_query), bias_value]).astype(
        jnp.float32
    )
    qkv = (jnp.dot(h_attn, full_qkv, preferred_element_type=jnp.float32) + bias_qkv).astype(
        jnp.bfloat16
    )
    qkv = qkv.reshape(latents, local_len, 3, width)
    heads = lax.all_to_all(qkv, "seq", split_axis=3, concat_axis=1, tiled=True)
    seq_len = heads.shape[1]
    group_width = heads.shape[3]
    head_count = group_width // HD
    query = heads[:, :, 0].reshape(latents, seq_len, head_count, HD)
    key = heads[:, :, 1].reshape(latents, seq_len, head_count, HD)
    value = heads[:, :, 2].reshape(latents, seq_len, head_count, HD)
    scores = score_table(query, key)
    top = jnp.max(scores, axis=-1, keepdims=True)
    log_total = top + jnp.log(jnp.sum(jnp.exp(scores - top), axis=-1, keepdims=True))
    probs_low = jnp.exp(scores - log_total).astype(jnp.bfloat16)
    attended = jnp.einsum("lhqk,lkhd->lqhd", probs_low, value, preferred_element_type=jnp.float32)
    attended = attended.astype(jnp.bfloat16).reshape(latents, seq_len, group_width)
    gathered_out = lax.all_to_all(attended, "seq", split_axis=1, concat_axis=2, tiled=True)
    attn = jnp.dot(gathered_out, full_proj, preferred_element_type=jnp.float32) + bias_proj.astype(
        jnp.float32
    )
    mid = residual + gate_attn * attn
    perceptron_input = modulate(mid, shift_mlp, scale_mlp).astype(jnp.bfloat16)
    up_value = jnp.dot(
        perceptron_input, full_fc1, preferred_element_type=jnp.float32
    ) + bias_fc1.astype(jnp.float32)
    activated_hidden = gelu_tanh(up_value).astype(jnp.bfloat16)
    branch = jnp.dot(
        activated_hidden, full_fc2, preferred_element_type=jnp.float32
    ) + bias_fc2.astype(jnp.float32)
    output = (mid + gate_mlp * branch).astype(jnp.bfloat16)
    back_ada, back_qkv, back_proj, first_linear_backward, second_linear_backward = (
        full_ada,
        full_qkv,
        full_proj,
        full_fc1,
        full_fc2,
    )
    grad_out = cotangent.astype(jnp.float32)
    grad_gate_mlp = jnp.sum(grad_out * branch, axis=1, keepdims=True)
    branch_output_gradient = (gate_mlp * grad_out).astype(jnp.bfloat16)
    grad_bias_fc2 = jnp.sum(branch_output_gradient.astype(jnp.float32), axis=(0, 1))
    activation_gradient = jnp.einsum(
        "yep,op->yeo",
        branch_output_gradient,
        second_linear_backward,
        preferred_element_type=jnp.float32,
    )
    gelu_value, gelu_back = jax.vjp(gelu_tanh, up_value)
    up_projection_gradient = gelu_back(activation_gradient)[0].astype(jnp.bfloat16)
    grad_bias_fc1 = jnp.sum(up_projection_gradient.astype(jnp.float32), axis=(0, 1))
    perceptron_input_gradient = jnp.einsum(
        "axq,bq->axb",
        up_projection_gradient,
        first_linear_backward,
        preferred_element_type=jnp.float32,
    )
    mlp_value, mlp_back = jax.vjp(modulate, mid, shift_mlp, scale_mlp)
    grad_mid, grad_shift_mlp, grad_scale_mlp = mlp_back(perceptron_input_gradient)
    grad_mid = grad_mid + grad_out
    grad_gate_attn = jnp.sum(grad_mid * attn, axis=1, keepdims=True)
    grad_attn = (gate_attn * grad_mid).astype(jnp.bfloat16)
    grad_bias_proj = jnp.sum(grad_attn.astype(jnp.float32), axis=(0, 1))
    grad_local_out = jnp.einsum(
        "lse,de->lsd", grad_attn, back_proj, preferred_element_type=jnp.float32
    ).astype(jnp.bfloat16)
    grad_heads = lax.all_to_all(grad_local_out, "seq", split_axis=2, concat_axis=1, tiled=True)
    grad_heads = grad_heads.reshape(latents, seq_len, head_count, HD)
    scores_again = score_table(query, key)
    probs = jnp.exp(scores_again - log_total)
    probs_again = probs.astype(jnp.bfloat16)
    grad_probs = jnp.einsum(
        "lqhd,lkhd->lhqk", grad_heads, value, preferred_element_type=jnp.float32
    )
    row_sums = jnp.sum(grad_probs * probs, axis=-1, keepdims=True)
    grad_scores = (probs * (grad_probs - row_sums)).astype(jnp.bfloat16)
    grad_value = jnp.einsum(
        "lhqk,lqhd->lkhd", probs_again, grad_heads, preferred_element_type=jnp.float32
    ).astype(jnp.bfloat16)
    grad_query = (
        jnp.einsum("lhqk,lkhd->lqhd", grad_scores, key, preferred_element_type=jnp.float32)
        * HD ** (-0.5)
    ).astype(jnp.bfloat16)
    grad_key = (
        jnp.einsum("lhqk,lqhd->lkhd", grad_scores, query, preferred_element_type=jnp.float32)
        * HD ** (-0.5)
    ).astype(jnp.bfloat16)
    grad_stack = jnp.stack([grad_query, grad_key, grad_value], axis=2).reshape(
        latents, seq_len, 3, group_width
    )
    grad_qkv_local = lax.all_to_all(grad_stack, "seq", split_axis=1, concat_axis=3, tiled=True)
    grad_qkv_local = grad_qkv_local.reshape(latents, local_len, 3 * width)
    grad_qkv_float = grad_qkv_local.astype(jnp.float32)
    grad_bias_query = jnp.sum(grad_qkv_float[..., :width], axis=(0, 1))
    grad_bias_value = jnp.sum(grad_qkv_float[..., 2 * width :], axis=(0, 1))
    grad_h_attn = jnp.einsum(
        "lse,de->lsd", grad_qkv_local, back_qkv, preferred_element_type=jnp.float32
    )
    attn_value, attn_back = jax.vjp(modulate, residual, shift_attn, scale_attn)
    grad_res, grad_shift_attn, grad_scale_attn = attn_back(grad_h_attn)
    grad_tokens = (grad_mid + grad_res).astype(jnp.bfloat16)
    grad_mod_part = jnp.concatenate(
        [
            grad_shift_attn,
            grad_scale_attn,
            grad_gate_attn,
            grad_shift_mlp,
            grad_scale_mlp,
            grad_gate_mlp,
        ],
        axis=-1,
    )[:, 0, :]
    grad_mod_total = lax.psum(grad_mod_part, "seq")
    grad_mod_low = grad_mod_total.astype(jnp.bfloat16)
    grad_mod_half = grad_mod_low * 0.5
    grad_bias_ada = jnp.sum(grad_mod_half.astype(jnp.float32), axis=0)
    grad_silu = jnp.einsum("le,de->ld", grad_mod_low, back_ada, preferred_element_type=jnp.float32)
    silu_value, silu_back = jax.vjp(jax.nn.silu, cond_float)
    grad_cond = silu_back(grad_silu)[0].astype(jnp.bfloat16)
    hidden_ratio = FF // D
    token_rows = latents * local_len
    attn_in_flat = h_attn.reshape(token_rows, width)
    qkv_grad_flat = grad_qkv_local.reshape(token_rows, 3 * width)
    attended_flat = gathered_out.reshape(token_rows, width)
    attn_grad_flat = grad_attn.reshape(token_rows, width)
    mlp_in_flat = perceptron_input.reshape(token_rows, width)
    up_grad_flat = up_projection_gradient.reshape(token_rows, FF)
    hidden_flat = activated_hidden.reshape(token_rows, FF)
    branch_grad_flat = branch_output_gradient.reshape(token_rows, width)
    owned_rows = w_ada.shape[0]
    ada_rows = jnp.einsum("lr,le->re", silu_cond, grad_mod_half, preferred_element_type=jnp.float32)
    qkv_rows = jnp.einsum(
        "tr,te->re", attn_in_flat, qkv_grad_flat, preferred_element_type=jnp.float32
    )
    proj_rows = jnp.einsum(
        "tr,te->re", attended_flat, attn_grad_flat, preferred_element_type=jnp.float32
    )
    fc1_rows = jnp.einsum(
        "tr,te->re", mlp_in_flat, up_grad_flat, preferred_element_type=jnp.float32
    )
    fc2_rows = jnp.einsum(
        "tr,te->re", hidden_flat, branch_grad_flat, preferred_element_type=jnp.float32
    )
    fc2_rows = fc2_rows.reshape(lax.axis_size(("seq", "fsdp")) * owned_rows, hidden_ratio * width)
    owned = lax.psum_scatter(
        jnp.concatenate([ada_rows, qkv_rows, proj_rows, fc1_rows, fc2_rows], axis=1),
        ("seq", "fsdp"),
        scatter_dimension=0,
        tiled=True,
    )
    (
        owned_bias_ada,
        owned_bias_query,
        owned_bias_value,
        owned_bias_proj,
        owned_bias_fc1,
        owned_bias_fc2,
    ) = (
        lax.psum_scatter(grad_bias_ada, ("seq", "fsdp"), scatter_dimension=0, tiled=True),
        lax.psum_scatter(grad_bias_query, ("seq", "fsdp"), scatter_dimension=0, tiled=True),
        lax.psum_scatter(grad_bias_value, ("seq", "fsdp"), scatter_dimension=0, tiled=True),
        lax.psum_scatter(grad_bias_proj, ("seq", "fsdp"), scatter_dimension=0, tiled=True),
        lax.psum_scatter(grad_bias_fc1, ("seq", "fsdp"), scatter_dimension=0, tiled=True),
        lax.psum_scatter(grad_bias_fc2, ("seq", "fsdp"), scatter_dimension=0, tiled=True),
    )
    offset_qkv = 6 * width
    offset_proj = 9 * width
    offset_fc1 = 10 * width
    offset_fc2 = 10 * width + FF
    owned_ada = owned[:, :offset_qkv]
    owned_qkv = owned[:, offset_qkv:offset_proj]
    owned_proj = owned[:, offset_proj:offset_fc1]
    owned_fc1 = owned[:, offset_fc1:offset_fc2]
    owned_fc2 = owned[:, offset_fc2:].reshape(owned_rows * hidden_ratio, width)
    return (
        output,
        grad_tokens,
        grad_cond,
        owned_ada,
        owned_bias_ada,
        owned_qkv,
        owned_bias_query,
        owned_bias_value,
        owned_proj,
        owned_bias_proj,
        owned_fc1,
        owned_bias_fc1,
        owned_fc2,
        owned_bias_fc2,
    )


def solution(mesh):
    in_specs = (
        P("fsdp", "seq", None),
        P("fsdp", None),
        P(("seq", "fsdp"), None),
        P(("seq", "fsdp")),
        P(("seq", "fsdp"), None),
        P(("seq", "fsdp")),
        P(("seq", "fsdp")),
        P(("seq", "fsdp"), None),
        P(("seq", "fsdp")),
        P(("seq", "fsdp"), None),
        P(("seq", "fsdp")),
        P(("seq", "fsdp"), None),
        P(("seq", "fsdp")),
        P("fsdp", "seq", None),
    )
    out_specs = (
        P("fsdp", "seq", None),
        P("fsdp", "seq", None),
        P("fsdp", None),
        P(("seq", "fsdp"), None),
        P(("seq", "fsdp")),
        P(("seq", "fsdp"), None),
        P(("seq", "fsdp")),
        P(("seq", "fsdp")),
        P(("seq", "fsdp"), None),
        P(("seq", "fsdp")),
        P(("seq", "fsdp"), None),
        P(("seq", "fsdp")),
        P(("seq", "fsdp"), None),
        P(("seq", "fsdp")),
    )
    return jax.shard_map(local, mesh=mesh, in_specs=in_specs, out_specs=out_specs, check_vma=False)
```

profile of v0, /device:TPU:0, one launch (start us, length us, event | category | flops | bytes accessed | tf_op | source)
XLA Modules:
  0.0 824.1 jit_solution(1620331633905181806)
XLA Ops:
  10.6 0.8 dynamic-update-slice.2
  11.4 0.8 dynamic-update-slice.1
  13.9 0.8 dynamic-update-slice
  14.8 0.8 dynamic-update-slice.4
  15.6 42.6 %all-reduce.13 = (bf16[768]{0:T(1024)(128)(2,1)S(1)}, bf16[768]{0:T(1024)(128)(2,1)S(1)}, bf16[4608]{0:T(1024)(128)(2,1)S(1)}, bf16[768]{0:T(1024)(128)(2,1)S(1)...) all-reduce(bf16[768]{0:T(1024)(128)(2,1)S(1)} %dynamic-update-slice, ...), channel_id=1, replica_groups=mesh['seq'=2,'fsdp'=16] {'seq','fsdp'}, use_global_device_ids=true, to_apply=%add.2 | all-reduce | flops 10752 | bytes 43008
  58.2 1.0 convert_reduce_fusion.1
  59.3 1.2 fusion.20
  60.5 26.0 %all-gather.6.cloned.1.call-done = bf16[768,4608]{1,0:T(8,128)(2,1)} async-done(((bf16[24,4608]{1,0:T(8,128)(2,1)}), bf16[768,4608]{1,0:T(8,128)(2,1)}) %all-gather.6.cloned.1.call-update) | async-done | bytes 7077904 | tf_op jit(solution)/shard_map/all_gather | solution.py:66
  86.5 4.1 convolution_reduce_fusion
  91.2 56.9 %all-gather.8.cloned.1.call-done = bf16[768,2304]{1,0:T(8,128)(2,1)} async-done(((bf16[24,2304]{1,0:T(8,128)(2,1)}), bf16[768,2304]{1,0:T(8,128)(2,1)}) %all-gather.8.cloned.1.call-update) | async-done | bytes 3538960 | tf_op jit(solution)/shard_map/all_gather | solution.py:68
  148.1 2.7 fusion
  151.6 14.2 %all_to_all.63 = bf16[1,128,3,768]{1,2,0,3:T(4,128)(2,1)S(1)} all-to-all(bf16[1,128,3,768]{1,2,0,3:T(4,128)(2,1)S(1)} %copy.83), channel_id=1, replica_groups=mesh['seq'=2,'fsdp'=16] {'seq'}, dimensions={3} | all-to-all | bytes 1179648 | tf_op jit(solution)/shard_map/all_to_all | solution.py:94
  168.8 1.8 reduce.42
  171.3 3.6 all-to-all-start.1
  175.6 4.4 all-to-all-done.1
  180.4 24.0 %all-gather.10.cloned.1.call-done = bf16[768,768]{1,0:T(8,128)(2,1)} async-done(((bf16[24,768]{1,0:T(8,128)(2,1)}), bf16[768,768]{1,0:T(8,128)(2,1)}) %all-gather.10.cloned.1.call-update) | async-done | bytes 1179664 | tf_op jit(solution)/shard_map/all_gather | solution.py:71
  204.4 2.4 fusion.64
  207.1 62.6 %all-gather.12.cloned.1.call-done = bf16[768,3072]{1,0:T(8,128)(2,1)} async-done(((bf16[24,3072]{1,0:T(8,128)(2,1)}), bf16[768,3072]{1,0:T(8,128)(2,1)}) %all-gather.12.cloned.1.call-update) | async-done | bytes 4718608 | tf_op jit(solution)/shard_map/all_gather | solution.py:73
  269.7 4.4 convolution_add_fusion.1
  274.1 60.7 %all-gather.14.cloned.1.call-done = bf16[3072,768]{1,0:T(8,128)(2,1)} async-done(((bf16[96,768]{1,0:T(8,128)(2,1)}), bf16[3072,768]{1,0:T(8,128)(2,1)}) %all-gather.14.cloned.1.call-update) | async-done | bytes 4718608 | tf_op jit(solution)/shard_map/all_gather | solution.py:75
  334.8 5.9 convert_reduce_fusion
  340.8 2.3 fusion.24
  344.0 2.5 convert_reduce_fusion.2
  347.1 1.2 fusion.10
  348.4 1.9 copy.92
  350.3 3.4 reduce.43
  353.7 1.7 reshape.495
  355.4 4.1 all-to-all-start.2
  361.4 3.3 all-to-all-done.2
  364.7 1.1 reshape.496
  366.2 1.1 convolution_convert_fusion.1
  370.0 1.1 copy.97
  371.1 3.4 pad_maximum_fusion
  374.4 3.5 all-to-all-start.3
  378.3 5.3 fusion.34
  383.5 11.5 %reshape.457 = f32[768,3072]{1,0:T(8,128)} reshape(f32[3072,768]{1,0:T(8,128)} %fusion.34) | data formatting | bytes 18874368 | tf_op jit(solution)/shard_map/reshape | solution.py:233
  395.7 3.4 fusion.21
  400.5 10.6 %psum.7 = bf16[1,4608]{1,0:T(2,128)(2,1)S(1)} all-reduce(f32[1,4608]{1,0:T(1,128)S(1)} %bitcast.169), channel_id=1, replica_groups=mesh['seq'=2,'fsdp'=16] {'seq'}, use_global_device_ids=true, to_apply=%region_17.18 | all-reduce | flops 4608 | bytes 27648 | tf_op jit(solution)/shard_map/psum | solution.py:202
  412.3 6.0 multiply_dynamic-update-slice_fusion
  418.3 4.8 convolution_dynamic-update-slice_fusion.1
  423.1 1.9 convolution_dynamic-update-slice_fusion.2
  425.1 5.1 convolution_dynamic-update-slice_fusion
  430.2 4.3 constant_dynamic-update-slice_fusion.6
  435.2 40.4 %all-reduce.12 = (f32[4608]{0:T(1024)S(1)}, f32[768]{0:T(1024)S(1)}, f32[768]{0:T(1024)S(1)}, f32[768]{0:T(1024)S(1)}, f32[3072]{0:T(1024)S(1)}, /*index=5*/f32[768]{0:T(1024)S(1)}) all-reduce(f32[4608]{0:T(1024)S(1)} %copy-done.16, f32[768]{0:T(1024)S(1)} %get-tuple-element.15, ...), channel_id=3, replica_groups=mesh['seq'=2,'fsdp'=16] {'seq','fsdp'}, use_global_device_ids=true, to_apply=%region_19.20.clone | all-reduce | flops 10752 | bytes 86016
  479.2 0.9 add_convert_fusion
  480.1 6.8 fusion.52
  486.9 325.5 %reduce-scatter.2.cloned.1.call-done = f32[24,13824]{1,0:T(8,128)} async-done(((f32[768,13824]{1,0:T(8,128)}), f32[24,13824]{1,0:T(8,128)}) %reduce-scatter.2.cloned.1.call-update) | async-done | bytes 1327120 | tf_op jit(solution)/shard_map/reduce_scatter | solution.py:234
  812.4 1.9 fusion.65
  (215 shorter events, 28.6 us)
Async XLA Ops:
  7.2 79.3 %all-gather.6.cloned.1.call-start = ((), (), s32[]{:S(2)}) async-start(), calls=%async_computation.5 | async-start | bytes 7299072 | tf_op jit(solution)/shard_map/all_gather | solution.py:66
  7.9 140.2 %all-gather.8.cloned.1.call-start = ((), (), s32[]{:S(2)}) async-start(), calls=%async_computation.6 | async-start | bytes 3649536 | tf_op jit(solution)/shard_map/all_gather | solution.py:68
  8.7 195.8 %all-gather.10.cloned.1.call-start = ((), (), s32[]{:S(2)}) async-start(), calls=%async_computation.7 | async-start | bytes 1216512 | tf_op jit(solution)/shard_map/all_gather | solution.py:71
  9.4 260.3 %all-gather.12.cloned.1.call-start = ((), (), s32[]{:S(2)}) async-start(), calls=%async_computation.8 | async-start | bytes 4866048 | tf_op jit(solution)/shard_map/all_gather | solution.py:73
  10.0 324.8 %all-gather.14.cloned.1.call-start = ((), (), s32[]{:S(2)}) async-start(), calls=%async_computation.9 | async-start | bytes 4866048 | tf_op jit(solution)/shard_map/all_gather | solution.py:75
  59.3 88.8 %copy-start.24 = (f32[128]{0:T(128)}, f32[128]{0:T(128)S(1)}, u32[]{:S(2)}) copy-start(f32[128]{0:T(128)S(1)} %broadcast_multiply_fusion.1) | copy-start | bytes 1540
  60.5 30.1 %copy-start.52 = (f32[128]{0:T(128)}, f32[128]{0:T(128)S(1)}, u32[]{:S(2)}) copy-start(f32[128]{0:T(128)S(1)} %fusion.20) | copy-start | bytes 1540
  60.5 87.6 %copy-start.26 = (f32[128]{0:T(128)}, f32[128]{0:T(128)S(1)}, u32[]{:S(2)}) copy-start(f32[128]{0:T(128)S(1)} %fusion.56) | copy-start | bytes 1540
  60.5 87.6 %copy-start.1 = (bf16[1,128,768]{2,1,0:T(8,128)(2,1)S(1)}, bf16[1,128,768]{2,1,0:T(8,128)(2,1)}, u32[]{:S(2)}) copy-start(bf16[1,128,768]{2,1,0:T(8,128)(2,1)} %param.14) | copy-start | bytes 589828
  91.2 56.9 %copy-start.21 = (f32[768]{0:T(1024)}, f32[768]{0:T(1024)S(1)}, u32[]{:S(2)}) copy-start(f32[768]{0:T(1024)S(1)} %get-tuple-element.26) | copy-start | bytes 9220
  91.2 113.2 %copy-start.35 = (f32[768]{0:T(1024)}, f32[768]{0:T(1024)S(1)}, u32[]{:S(2)}) copy-start(f32[768]{0:T(1024)S(1)} %get-tuple-element.28) | copy-start | bytes 9220
  171.3 8.6 %all-to-all-start.1 = ((bf16[2,2,24576]{2,1,0:T(2,128)(2,1)}), bf16[2,2,24576]{2,1,0:T(2,128)(2,1)S(1)}, u32[]{:S(2)}, u32[]{:S(2)}) async-start(bf16[2,2,24576]{2,1,0:T(2,128)(2,1)} %reshape.493), calls=%async_computation.1 | async-start | bytes 393216 | tf_op jit(solution)/shard_map/all_to_all | solution.py:107
  180.2 89.5 %copy-start.19 = (f32[768]{0:T(1024)S(1)}, f32[768]{0:T(1024)}, u32[]{:S(2)}) copy-start(f32[768]{0:T(1024)} %get-tuple-element.24) | copy-start | bytes 9220
  206.8 67.3 %copy-start.28 = (f32[128]{0:T(128)}, f32[128]{0:T(128)S(1)}, u32[]{:S(2)}) copy-start(f32[128]{0:T(128)S(1)} %broadcast_multiply_fusion) | copy-start | bytes 1540
  207.0 62.7 %copy-start.54 = (f32[128]{0:T(128)}, f32[128]{0:T(128)S(1)}, u32[]{:S(2)}) copy-start(f32[128]{0:T(128)S(1)} %multiply_reduce_fusion.1) | copy-start | bytes 1540
  207.0 67.1 %copy-start.39 = (f32[128]{0:T(128)}, f32[128]{0:T(128)S(1)}, u32[]{:S(2)}) copy-start(f32[128]{0:T(128)S(1)} %fusion.57) | copy-start | bytes 1540
  269.7 65.1 %copy-start.10 = (bf16[1,128,768]{2,1,0:T(8,128)(2,1)S(1)}, bf16[1,128,768]{2,1,0:T(8,128)(2,1)}, u32[]{:S(2)}) copy-start(bf16[1,128,768]{2,1,0:T(8,128)(2,1)} %param.27) | copy-start | bytes 589828
  269.7 65.1 %copy-start.32 = (f32[768]{0:T(1024)S(1)}, f32[768]{0:T(1024)}, u32[]{:S(2)}) copy-start(f32[768]{0:T(1024)} %get-tuple-element.23) | copy-start | bytes 9220
  334.8 5.9 copy-start
  334.8 5.9 copy-start.29
  334.8 5.9 copy-start.40
  340.8 3.2 copy-start.57
  343.3 3.1 copy-start.7
  343.3 3.1 copy-start.50
  344.0 3.1 copy-start.4
  355.4 9.3 %all-to-all-start.2 = ((bf16[2,2,24576]{2,1,0:T(2,128)(2,1)}), bf16[2,2,24576]{2,1,0:T(2,128)(2,1)}, u32[]{:S(2)}, u32[]{:S(2)}) async-start(bf16[2,2,24576]{2,1,0:T(2,128)(2,1)} %reshape.495), calls=%async_computation.2 | async-start | bytes 393216 | tf_op jit(solution)/shard_map/all_to_all | solution.py:156
  371.1 7.2 copy-start.3
  371.1 7.2 copy-start.34
  374.4 20.5 %all-to-all-start.3 = ((bf16[1,256,3,384]{3,2,0,1:T(4,128)(2,1)}), bf16[1,256,3,384]{3,2,0,1:T(4,128)(2,1)S(1)}, u32[]{:S(2)}, u32[]{:S(2)}) async-start(bf16[1,256,3,384]{3,2,0,1:T(4,128)(2,1)} %pad_maximum_fusion), calls=%async_computation.3 | async-start | bytes 1572864 | tf_op jit(solution)/shard_map/all_to_all | solution.py:180
  378.0 434.4 %reduce-scatter.2.cloned.1.call-start = ((), (), s32[]{:S(2)}) async-start(), calls=%async_computation.10 | async-start | bytes 43794432 | tf_op jit(solution)/shard_map/reduce_scatter | solution.py:234
  395.6 3.4 copy-start.53
  395.6 4.0 copy-start.27
  395.6 4.8 copy-start.46
  395.6 4.8 copy-start.31
  395.6 4.8 copy-start.37
  395.7 4.8 copy-start.45
  395.7 16.6 %copy-start.38 = (f32[768]{0:T(1024)S(1)}, f32[768]{0:T(1024)}, u32[]{:S(2)}) copy-start(f32[768]{0:T(1024)} %convert.10) | copy-start | bytes 9220
  412.3 6.0 copy-start.22
  418.3 4.8 copy-start.12
  418.3 11.9 %slice-start = ((s8[9437184]{0:T(1024)(128)(4,1)}), s8[4194304]{0:T(1024)(128)(4,1)S(1)}, s32[]{:S(2)}) async-start(s8[9437184]{0:T(1024)(128)(4,1)} %bitcast.141), calls=%async_computation.11 | async-start | bytes 8388608
  418.3 11.9 %slice-start.1 = ((s8[9437184]{0:T(1024)(128)(4,1)}), s8[4194304]{0:T(1024)(128)(4,1)S(1)}, s32[]{:S(2)}) async-start(s8[9437184]{0:T(1024)(128)(4,1)} %bitcast.141), calls=%async_computation.12 | async-start | bytes 8388608
  425.1 5.1 slice-start.2
  434.5 44.7 %copy-start.56 = (f32[128]{0:T(128)S(1)}, f32[128]{0:T(128)}, u32[]{:S(2)}) copy-start(f32[128]{0:T(128)} %get-tuple-element.19) | copy-start | bytes 1540
  434.5 44.7 %copy-start.8 = (f32[1,128,768]{2,1,0:T(8,128)S(1)}, f32[1,128,768]{2,1,0:T(8,128)}, u32[]{:S(2)}) copy-start(f32[1,128,768]{2,1,0:T(8,128)} %copy-done.7) | copy-start | bytes 1179652
  434.5 44.7 %copy-start.49 = (f32[128]{0:T(128)S(1)}, f32[128]{0:T(128)}, u32[]{:S(2)}) copy-start(f32[128]{0:T(128)} %copy-done.48) | copy-start | bytes 1540
  434.5 44.6 %copy-start.51 = (f32[128]{0:T(128)S(1)}, f32[128]{0:T(128)}, u32[]{:S(2)}) copy-start(f32[128]{0:T(128)} %copy-done.50) | copy-start | bytes 1540
  434.8 45.3 %copy-start.18 = (bf16[1,4608]{1,0:T(2,128)(2,1)S(1)}, bf16[1,4608]{1,0:T(2,128)(2,1)}, u32[]{:S(2)}) copy-start(bf16[1,4608]{1,0:T(2,128)(2,1)} %copy-done.17) | copy-start | bytes 27652
  434.8 45.3 %copy-start.23 = (bf16[1,768]{1,0:T(2,128)(2,1)S(1)}, bf16[1,768]{1,0:T(2,128)(2,1)}, u32[]{:S(2)}) copy-start(bf16[1,768]{1,0:T(2,128)(2,1)} %param.15) | copy-start | bytes 4612
  (22 other events, 35.3 us)
Sparse Core Ops, SparseCore 0:
  10.9 75.5 all-gather.5
  89.4 58.6 all-gather.7
  151.0 53.3 all-gather.9
  207.2 62.4 all-gather.11
  272.4 62.2 all-gather.13
  434.6 377.7 reduce-scatter.1
where the time goes:
time: 825 us; the launch traced here: 824 us
  waiting for transfers between devices  567 us (69%)
  blocking collectives  108 us (13%)
  matrix products  55.6 us (7%)
  local copies, waits for them, and re-layouts  44.4 us (5%)
  other arithmetic  23.1 us (3%)
  between operations  14.9 us (2%)
  starting transfers between devices  11.7 us (1%)
    reduce_scatter x1, waiting for transfers between devices, local(): lax.psum_scatter(jnp.concatenate([ada_rows, qkv_rows, proj_rows, fc1_rows...  326 us
    unnamed x2, blocking collectives  83 us
    all_gather x1, waiting for transfers between devices, local(): lax.all_gather(w_fc1, ('seq', 'fsdp'), axis=0, tiled=True)  62.6 us
    all_gather x1, waiting for transfers between devices, local(): lax.all_gather(w_fc2, ('seq', 'fsdp'), axis=0, tiled=True)  60.7 us
    all_gather x1, waiting for transfers between devices, local(): lax.all_gather(w_qkv, ('seq', 'fsdp'), axis=0, tiled=True)  56.9 us
    all_gather x1, waiting for transfers between devices, local(): lax.all_gather(w_ada, ('seq', 'fsdp'), axis=0, tiled=True)  26 us
    all_gather x1, waiting for transfers between devices, local(): lax.all_gather(w_proj, ('seq', 'fsdp'), axis=0, tiled=True)  24 us
    unnamed x153, local copies, waits for them, and re-layouts  16.7 us
  transfers between devices with their start and end apart: 9, of which 8 were waited for; matrix products, arithmetic and copies ran while one was open for 7% of the time, Pallas kernels for 0%

commit v1 on v0

v1 whole, which is shorter than its diff:
```python
import math

import jax
import jax.numpy as jnp
from jax import lax
from jax.sharding import PartitionSpec as P

HD = 64
AXES = ("seq", "fsdp")
F32 = jnp.float32
BF16 = jnp.bfloat16


def normalize(value):
    centre = value - jnp.mean(value, axis=-1, keepdims=True)
    variance = jnp.mean(centre * centre, axis=-1, keepdims=True)
    return centre * lax.rsqrt(variance + 1e-06)


def modulate(value, shift, scale):
    return normalize(value) * (1.0 + scale) + shift


def gelu_tanh(value):
    return (
        0.5
        * value
        * (1.0 + jnp.tanh(0.7978845608028654 * (value + 0.044715 * value * value * value)))
    )


def dot(left, right):
    return jnp.dot(left, right, preferred_element_type=F32)


def dot_rt(left, right):
    return lax.dot_general(left, right, (((1,), (1,)), ((), ())), preferred_element_type=F32)


def dot_lt(left, right):
    return lax.dot_general(left, right, (((0,), (0,)), ((), ())), preferred_element_type=F32)


class Links:
    def __init__(self, devices):
        self.devices = devices
        self.index = lax.axis_index(AXES)

    def place(self, bits):
        spot = jnp.int32(0)
        for bit in bits:
            spot = spot * 2 + ((self.index >> bit) & 1)
        return spot

    def mask(self, bits, step):
        total = 0
        for at, bit in enumerate(reversed(bits)):
            total |= ((step >> at) & 1) << bit
        return total

    def send(self, value, bits, step=1):
        mask = self.mask(bits, step)
        return lax.ppermute(value, AXES, [(i, i ^ mask) for i in range(self.devices)])

    def gather(self, value, bits, axis):
        count = 1 << len(bits)
        spot = self.place(bits)
        arrived = [value] + [self.send(value, bits, step) for step in range(1, count)]
        if count == 2:
            first = jnp.stack(arrived, axis)
            second = jnp.stack(arrived[::-1], axis)
            return jnp.where(spot == 0, first, second)
        shape = value.shape[:axis] + (count,) + value.shape[axis:]
        out = jnp.zeros(shape, value.dtype)
        for step, part in enumerate(arrived):
            out = lax.dynamic_update_index_in_dim(out, part, spot ^ step, axis)
        return out

    def pick(self, value, spot, axis=0):
        return lax.dynamic_index_in_dim(value, spot, axis, keepdims=False)

    def exchange(self, value, bits):
        spot = self.place(bits)
        out = value
        for step in range(1, 1 << len(bits)):
            part = self.send(self.pick(value, spot ^ step), bits, step)
            out = lax.dynamic_update_index_in_dim(out, part, spot ^ step, 0)
        return out

    def scatter(self, value, bits, axis):
        spot = self.place(bits)
        total = self.pick(value, spot, axis).astype(F32)
        for step in range(1, 1 << len(bits)):
            part = self.pick(value, spot ^ step, axis).astype(BF16)
            total = total + self.send(part, bits, step).astype(F32)
        return total


def bit_groups(bits):
    high = list(reversed(bits))
    return [high[at : at + 2] for at in range(0, len(high), 2)]


def local(
    shards,
    split,
    tokens,
    cond,
    w_ada,
    b_ada,
    w_qkv,
    b_query,
    b_value,
    w_proj,
    b_proj,
    w_fc1,
    b_fc1,
    w_fc2,
    b_fc2,
    cotangent,
):
    seq, fsdp = split
    link = Links(shards)
    low_bits = int(math.log2(fsdp))
    core_bit = [0]
    seq_bits = list(range(low_bits, int(math.log2(shards))))[::-1]
    rest_bits = list(range(1, low_bits))
    rest = fsdp // 2
    team = seq * 2
    team_bits = seq_bits + core_bit
    core = link.place(core_bit)
    half = link.place(seq_bits)
    me = link.place(team_bits)
    latents, local_len, width = tokens.shape
    seq_len = seq * local_len
    rows = w_qkv.shape[0]
    hidden_rows = w_fc2.shape[0]
    hidden = hidden_rows * rest
    group = width // team
    heads = group // HD
    count = 2 * latents

    def gather_rest(value):
        first, last = value.shape[0], value.shape[1:]
        value = value[:, None]
        for bits in bit_groups(rest_bits):
            value = link.gather(value, bits, 2)
            value = value.reshape((first, -1) + last)
        return value

    def scatter_rest(value):
        first, last = value.shape[0], value.shape[2:]
        for bits in bit_groups(rest_bits)[::-1]:
            value = value.reshape((first, -1, 1 << len(bits)) + last)
            value = link.scatter(value, bits, 2)
        return value[:, 0]

    def both_halves(value):
        value = link.gather(value, seq_bits, 1).reshape(latents, seq_len, -1)
        return link.gather(value, core_bit, 0).reshape(count, seq_len, -1)

    cond_float = cond.astype(F32)
    silu_cond = jax.nn.silu(cond_float).astype(BF16)
    cond_blocks = silu_cond.reshape(latents, shards, rows).swapaxes(0, 1).reshape(shards, -1)
    small = jnp.concatenate([b_query, b_value, b_proj, b_fc2, b_fc1])
    small = jnp.concatenate(
        [cond_blocks, jnp.broadcast_to(small, (shards, small.shape[0]))], axis=1
    )
    small = lax.all_to_all(small, AXES, 0, 0, tiled=True)
    mine = latents * rows
    all_cond = small[:fsdp, :mine].reshape(fsdp * latents, rows)
    full_query = small[:, mine : mine + rows].reshape(-1)
    full_value = small[:, mine + rows : mine + 2 * rows].reshape(-1)
    bias_proj = small[:, mine + 2 * rows : mine + 3 * rows].reshape(-1).astype(F32)
    bias_fc2 = small[:, mine + 3 * rows : mine + 4 * rows].reshape(-1).astype(F32)
    bias_fc1 = small[:, mine + 4 * rows :].reshape(seq, rest, 2, hidden_rows)
    bias_fc1 = link.pick(link.pick(bias_fc1, half, 0), core, 1).reshape(-1).astype(F32)

    team_qkv = w_qkv.reshape(rows, 3, team, group).transpose(2, 0, 1, 3)
    team_qkv = link.exchange(team_qkv.reshape(team, rows, 3 * group), team_bits)
    my_qkv = gather_rest(team_qkv.reshape(seq, 2 * rows, 3 * group)).reshape(width, 3 * group)
    full_proj = gather_rest(w_proj[None])[0]
    full_proj = link.gather(full_proj, seq_bits, 0)
    full_proj = link.gather(full_proj, core_bit, 2).reshape(width, width)
    team_fc1 = w_fc1.reshape(rows, seq, rest, 2, hidden_rows).transpose(1, 3, 0, 2, 4)
    team_fc1 = link.exchange(team_fc1.reshape(team, rows, hidden), team_bits)
    my_fc1 = gather_rest(team_fc1.reshape(seq, 2 * rows, hidden)).reshape(width, hidden)
    my_fc2 = gather_rest(w_fc2[None]).reshape(hidden, width)
    all_tokens = both_halves(tokens).astype(F32)
    all_cotangent = both_halves(cotangent).astype(F32)

    part = dot(all_cond, w_ada)
    own_columns = (jnp.arange(shards) == link.index)[:, None] * b_ada.astype(F32)[None, :]
    part = part + own_columns.reshape(-1)
    part = part.reshape(1, fsdp, latents * 6 * width)
    part = jnp.broadcast_to(part, (seq, fsdp, latents * 6 * width)).reshape(shards, -1)
    part = lax.all_to_all(part, AXES, 0, 0, tiled=True)
    modulation = jnp.sum(part, axis=0).reshape(latents, 1, 6 * width)
    modulation = link.gather(modulation, core_bit, 0).reshape(count, 1, 6 * width)
    parts = [modulation[..., at * width : (at + 1) * width] for at in range(6)]
    shift_attn, scale_attn, gate_attn, shift_mlp, scale_mlp, gate_mlp = parts

    def own(value):
        return lax.dynamic_slice_in_dim(value, core * latents, latents, 0)

    def own_rows(value):
        return lax.dynamic_slice_in_dim(value, half * local_len, local_len, 1)

    def sum_team(value):
        value = link.scatter(value.reshape(2, latents, seq_len, width), core_bit, 0)
        value = value.astype(BF16)
        return value.astype(F32) + link.send(value, seq_bits).astype(F32)

    def flat(value):
        return value.reshape(count * seq_len, -1)

    h_attn = modulate(all_tokens, shift_attn, scale_attn).astype(BF16)
    bias_q = lax.dynamic_slice_in_dim(full_query, me * group, group, 0)
    bias_v = lax.dynamic_slice_in_dim(full_value, me * group, group, 0)
    bias_qkv = jnp.concatenate([bias_q, jnp.zeros_like(bias_q), bias_v]).astype(F32)
    qkv = (dot(flat(h_attn), my_qkv) + bias_qkv).astype(BF16)
    qkv = qkv.reshape(count, seq_len, 3, heads, HD)
    query, key, value = qkv[:, :, 0], qkv[:, :, 1], qkv[:, :, 2]
    scores = jnp.einsum("lqhd,lkhd->lhqk", query, key, preferred_element_type=F32) * HD ** (-0.5)
    top = jnp.max(scores, axis=-1, keepdims=True)
    log_total = top + jnp.log(jnp.sum(jnp.exp(scores - top), axis=-1, keepdims=True))
    probs = jnp.exp(scores - log_total)
    probs_low = probs.astype(BF16)
    attended = jnp.einsum("lhqk,lkhd->lqhd", probs_low, value, preferred_element_type=F32)
    attended = attended.astype(BF16).reshape(count * seq_len, group)
    all_attended = link.gather(link.gather(attended, seq_bits, 0), core_bit, 1)
    all_attended = all_attended.reshape(team, count * seq_len, group)
    attn = jnp.einsum(
        "tnd,tde->ne",
        all_attended,
        full_proj.reshape(team, group, width),
        preferred_element_type=F32,
    )
    attn = (attn + bias_proj).reshape(count, seq_len, width)
    mid = all_tokens + gate_attn * attn

    h_mlp = flat(modulate(mid, shift_mlp, scale_mlp).astype(BF16))
    up = dot(h_mlp, my_fc1) + bias_fc1
    activated, gelu_back = jax.vjp(gelu_tanh, up)
    activated = activated.astype(BF16)
    grad_branch = flat((gate_mlp * all_cotangent).astype(BF16))
    grad_up = gelu_back(dot_rt(grad_branch, my_fc2))[0].astype(BF16)
    grad_h_mlp = sum_team(dot_rt(grad_up, my_fc1).reshape(count, seq_len, width))

    own_tokens = own(all_tokens)
    own_cotangent = own(all_cotangent)
    own_mid = own(mid)
    mlp_back = jax.vjp(modulate, own_mid, own(shift_mlp), own(scale_mlp))[1]
    grad_mid, grad_shift_mlp, grad_scale_mlp = mlp_back(grad_h_mlp)
    grad_mid = grad_mid + own_cotangent
    grad_gate_attn = jnp.sum(grad_mid * own(attn), axis=1, keepdims=True)
    grad_attn = (own(gate_attn) * grad_mid).astype(BF16)
    grad_attn = link.gather(grad_attn, core_bit, 0).reshape(count * seq_len, width)

    grad_fc2 = dot_lt(activated, grad_branch).astype(BF16)
    grad_fc2 = scatter_rest(grad_fc2.reshape(1, rest, hidden_rows, width))[0]
    grad_fc1 = dot_lt(h_mlp, grad_up).astype(BF16)
    grad_fc1 = scatter_rest(grad_fc1.reshape(seq, rest, 2 * rows, hidden)).astype(BF16)
    grad_fc1 = link.exchange(grad_fc1.reshape(team, rows, hidden), team_bits)
    grad_fc1 = grad_fc1.reshape(seq, 2, rows, rest, hidden_rows).transpose(2, 0, 3, 1, 4)
    grad_fc1 = grad_fc1.reshape(rows, -1).astype(F32)

    branch = dot(activated, my_fc2).reshape(2, latents, seq_len, width)
    branch = link.scatter(branch, core_bit, 0).reshape(latents, seq, local_len, width)
    branch = link.scatter(branch, seq_bits, 1) + bias_fc2
    output = (own_rows(own_mid) + own(gate_mlp) * branch).astype(BF16)
    grad_gate_mlp = jnp.sum(cotangent.astype(F32) * branch, axis=1, keepdims=True)
    grad_gate_mlp = grad_gate_mlp + link.send(grad_gate_mlp, seq_bits)

    my_proj = lax.dynamic_slice_in_dim(full_proj, me * group, group, 0)
    grad_heads = dot_rt(grad_attn, my_proj).astype(BF16).reshape(count, seq_len, heads, HD)
    grad_probs = jnp.einsum("lqhd,lkhd->lhqk", grad_heads, value, preferred_element_type=F32)
    row_sums = jnp.sum(grad_probs * probs, axis=-1, keepdims=True)
    grad_scores = (probs * (grad_probs - row_sums)).astype(BF16)
    grad_value = jnp.einsum(
        "lhqk,lqhd->lkhd", probs_low, grad_heads, preferred_element_type=F32
    ).astype(BF16)
    grad_query = (
        jnp.einsum("lhqk,lkhd->lqhd", grad_scores, key, preferred_element_type=F32) * HD ** (-0.5)
    ).astype(BF16)
    grad_key = (
        jnp.einsum("lhqk,lqhd->lkhd", grad_scores, query, preferred_element_type=F32)
        * HD ** (-0.5)
    ).astype(BF16)
    grad_qkv = jnp.stack([grad_query, grad_key, grad_value], axis=2)
    grad_qkv = grad_qkv.reshape(count * seq_len, 3 * group)
    grad_h_attn = sum_team(dot_rt(grad_qkv, my_qkv).reshape(count, seq_len, width))
    grad_w_qkv = dot_lt(flat(h_attn), grad_qkv).astype(BF16)
    grad_w_qkv = scatter_rest(grad_w_qkv.reshape(seq, rest, 2 * rows, 3 * group)).astype(BF16)
    grad_w_qkv = link.exchange(grad_w_qkv.reshape(team, rows, 3 * group), team_bits)
    grad_w_qkv = grad_w_qkv.reshape(team, rows, 3, group).transpose(1, 2, 0, 3)
    grad_w_qkv = grad_w_qkv.reshape(rows, -1).astype(F32)

    grad_proj = dot_lt(attended, grad_attn).astype(BF16)
    grad_proj = grad_proj.reshape(rest // 2, 2, rows, width).swapaxes(0, 1)
    grad_proj = link.exchange(grad_proj, core_bit).reshape(1, rest, rows, width)
    grad_proj = scatter_rest(grad_proj)[0]

    attn_back = jax.vjp(modulate, own_tokens, own(shift_attn), own(scale_attn))[1]
    grad_res, grad_shift_attn, grad_scale_attn = attn_back(grad_h_attn)
    grad_tokens = own_rows(grad_mid + grad_res).astype(BF16)

    grad_mod = jnp.concatenate(
        [
            grad_shift_attn,
            grad_scale_attn,
            grad_gate_attn,
            grad_shift_mlp,
            grad_scale_mlp,
            grad_gate_mlp,
        ],
        axis=-1,
    ).astype(BF16)
    grad_mod = gather_rest(grad_mod.reshape(1, latents, 6 * width))[0]
    grad_mod = link.gather(grad_mod, core_bit, 1).reshape(fsdp * latents, 6 * width)
    grad_ada = dot_lt(all_cond, grad_mod)
    own_ada = b_ada.shape[0]
    grad_b_ada = lax.dynamic_slice_in_dim(grad_mod, link.index * own_ada, own_ada, 1)
    grad_b_ada = jnp.sum(grad_b_ada.astype(F32), axis=0)
    grad_silu = dot_rt(grad_mod, w_ada).reshape(1, fsdp, latents * rows)
    grad_silu = jnp.broadcast_to(grad_silu, (seq, fsdp, latents * rows)).reshape(shards, -1)

    def column_sums(value):
        return jnp.sum(value.astype(F32), axis=0)

    everyone = 1.0 / team
    by_owner = [
        (column_sums(grad_branch) * everyone).reshape(shards, rows),
        (column_sums(grad_attn) * everyone).reshape(shards, rows),
    ]
    sums_qkv = column_sums(grad_qkv)
    in_team = (jnp.arange(team) == me)[:, None]
    for sums in (sums_qkv[:group], sums_qkv[2 * group :]):
        by_owner.append(jnp.where(in_team, sums[None, :], 0.0).reshape(shards, rows))
    sums_up = column_sums(grad_up).reshape(1, rest, 1, hidden_rows)
    in_seq = jnp.arange(seq).reshape(seq, 1, 1, 1) == half
    in_core = jnp.arange(2).reshape(1, 1, 2, 1) == core
    by_owner.append(jnp.where(in_seq & in_core, sums_up, 0.0).reshape(shards, hidden_rows))
    tail = jnp.concatenate([grad_silu] + by_owner, axis=1)
    tail = lax.all_to_all(tail, AXES, 0, 0, tiled=True)
    grad_silu = tail[:, :mine].reshape(shards, latents, rows).swapaxes(0, 1)
    grad_silu = grad_silu.reshape(latents, width)
    silu_back = jax.vjp(jax.nn.silu, cond_float)[1]
    grad_cond = silu_back(grad_silu)[0].astype(BF16)
    sums = jnp.sum(tail[:, mine:], axis=0)
    return (
        output,
        grad_tokens,
        grad_cond,
        grad_ada,
        grad_b_ada,
        grad_w_qkv,
        sums[2 * rows : 3 * rows],
        sums[3 * rows : 4 * rows],
        grad_proj,
        sums[rows : 2 * rows],
        grad_fc1,
        sums[4 * rows :],
        grad_fc2,
        sums[:rows],
    )


def solution(mesh):
    seq, fsdp = mesh.shape["seq"], mesh.shape["fsdp"]
    act = P("fsdp", "seq", None)
    matrix = P(AXES, None)
    vector = P(AXES)
    cond = P("fsdp", None)
    in_specs = (
        act, cond, matrix, vector, matrix, vector, vector, matrix, vector, matrix, vector, matrix,
        vector, act,
    )
    out_specs = (
        act, act, cond, matrix, vector, matrix, vector, vector, matrix, vector, matrix, vector,
        matrix, vector,
    )

    def layer(*args):
        return local(seq * fsdp, (seq, fsdp), *args)

    return jax.shard_map(layer, mesh=mesh, in_specs=in_specs, out_specs=out_specs, check_vma=False)
```

time: 825 us -> 299 us (0.36)
  waiting for transfers between devices: 567 us -> 107 us
  blocking collectives: 108 us -> 0 us
  starting transfers between devices: 11.7 us -> 84 us
  matrix products: 55.6 us -> 18.2 us
  other arithmetic: 23.1 us -> 43.3 us
  between operations: 14.9 us -> 2.38 us
    reduce_scatter x1 -> x0, waiting for transfers between devices: 326 us -> none  [local(): lax.psum_scatter(jnp.concatenate([ada_rows, qkv_rows, proj_rows, fc1_rows...]
    all_gather x5 -> x0, waiting for transfers between devices: 230 us -> none  [the longest x1 62.6 us: local(): lax.all_gather(w_fc1, ('seq', 'fsdp'), axis=0, tiled=True)]
    ppermute x0 -> x67, waiting for transfers between devices: none -> 96.1 us  [send(): lax.ppermute(value, AXES, [(i, i ^ mask) for i in range(self.devices)])]
    unnamed x2 -> x0, blocking collectives: 83 us -> none
    ppermute x0 -> x67, starting transfers between devices: none -> 70.8 us  [send(): lax.ppermute(value, AXES, [(i, i ^ mask) for i in range(self.devices)])]
    dot_general x19 -> x20, matrix products: 55.3 us -> 17.9 us  [the longest x5 5.43 us: dot_lt(): lax.dot_general(left, right, (((0,), (0,)), ((), ())), preferred_element_...]
    select_n x0 -> x17, other arithmetic: none -> 14.2 us  [the longest x15 12.9 us: gather(): return jnp.where(spot == 0, first, second)]
    all_to_all x1 -> x0, blocking collectives: 14.2 us -> none  [local(): heads = lax.all_to_all(qkv, 'seq', split_axis=3, concat_axis=1, tiled=True)]
  transfers between devices with their start and end apart: 9 -> 70, of which waited for: 8 -> 27; matrix products, arithmetic and copies ran while one was open for 7% -> 27% of each run, Pallas kernels for 0% -> 0%
where the time goes in v1:
time: 299 us; the launch traced here: 298 us
  waiting for transfers between devices  107 us (36%)
  starting transfers between devices  84 us (28%)
  other arithmetic  43.3 us (14%)
  local copies, waits for them, and re-layouts  43.1 us (14%)
  matrix products  18.2 us (6%)
    ppermute x67, waiting for transfers between devices, send(): lax.ppermute(value, AXES, [(i, i ^ mask) for i in range(self.devices)])  96.1 us
    ppermute x67, starting transfers between devices, send(): lax.ppermute(value, AXES, [(i, i ^ mask) for i in range(self.devices)])  70.8 us
    select_n x15, other arithmetic, gather(): return jnp.where(spot == 0, first, second)  12.9 us
    unnamed x146, local copies, waits for them, and re-layouts  10.6 us
    all_to_all x1, starting transfers between devices, local(): small = lax.all_to_all(small, AXES, 0, 0, tiled=True)  6.07 us
  transfers between devices with their start and end apart: 70, of which 27 were waited for; matrix products, arithmetic and copies ran while one was open for 27% of the time, Pallas kernels for 0%

profile of v1, /device:TPU:0, one launch (start us, length us, event | category | flops | bytes accessed | tf_op | source)
XLA Modules:
  0.0 298.3 jit_solution(8178881902981826514)
XLA Ops:
  0.7 3.1 %collective-permute-start.12 = (bf16[1,1,24,768]{3,2,1,0:T(8,128)(2,1)}, bf16[1,1,24,768]{3,2,1,0:T(8,128)(2,1)S(1)}, u32[]{:S(2)}, u32[]{:S(2)}) collective-permute-start(bf16[1,1,24,768]{3,2,1,0:T(8,128)(2,1)} %bitcast.458), channel_id=1, source_target_pairs={{0,4},{1,5},{2,6},{3,7},{4,0},{5,1},{6,2},{7,3},{8,12},{9,13},{10,... | collective-permute-start | bytes 110600 | tf_op jit(solution)/shard_map/ppermute | solution.py:63
  3.8 2.6 collective-permute-start.13
  11.4 6.1 %all-to-all-start = ((bf16[32,1,216]{2,1,0:T(2,128)(2,1)}), bf16[32,1,216]{2,1,0:T(2,128)(2,1)S(1)}, u32[]{:S(2)}, u32[]{:S(2)}) async-start(bf16[32,1,216]{2,1,0:T(2,128)(2,1)} %copy.159), calls=%async_computation | async-start | bytes 65536 | tf_op jit(solution)/shard_map/all_to_all | solution.py:169
  19.2 5.5 %all-to-all-done = bf16[32,1,216]{2,1,0:T(2,128)(2,1)S(1)} async-done(((bf16[32,1,216]{2,1,0:T(2,128)(2,1)}), bf16[32,1,216]{2,1,0:T(2,128)(2,1)S(1)}, u32[]{:S(2)}, u32[]{:S(2)}) %all-to-all-start) | async-done | bytes 13856 | tf_op jit(solution)/shard_map/all_to_all | solution.py:169
  27.1 3.6 %all-to-all-start.1 = ((f32[32,1,4608]{2,1,0:T(1,128)}), f32[32,1,4608]{2,1,0:T(1,128)}, u32[]{:S(2)}, u32[]{:S(2)}) async-start(f32[32,1,4608]{2,1,0:T(1,128)} %all_to_all.25), calls=%async_computation.1 | async-start | bytes 1179648 | tf_op jit(solution)/shard_map/all_to_all | solution.py:197
  33.9 2.6 collective-permute-start.26
  36.8 1.6 collective-permute-start
  39.0 6.7 %collective-permute-done.4 = bf16[24,576]{1,0:T(8,128)(2,1)S(1)} collective-permute-done((bf16[24,576]{1,0:T(8,128)(2,1)S(1)}, bf16[24,576]{1,0:T(8,128)(2,1)S(1)}, u32[]{:S(2)}, u32[]{:S(2)}) %collective-permute-start.4) | collective-permute-done | bytes 27680 | tf_op jit(solution)/shard_map/ppermute | solution.py:63
  45.7 3.3 %collective-permute-done.5 = bf16[24,576]{1,0:T(8,128)(2,1)S(1)} collective-permute-done((bf16[24,576]{1,0:T(8,128)(2,1)S(1)}, bf16[24,576]{1,0:T(8,128)(2,1)S(1)}, u32[]{:S(2)}, u32[]{:S(2)}) %collective-permute-start.5) | collective-permute-done | bytes 27680 | tf_op jit(solution)/shard_map/ppermute | solution.py:63
  50.2 2.8 collective-permute-done.19
  53.0 3.4 %collective-permute-done.20 = bf16[24,768]{1,0:T(8,128)(2,1)S(1)} collective-permute-done((bf16[24,768]{1,0:T(8,128)(2,1)S(1)}, bf16[24,768]{1,0:T(8,128)(2,1)S(1)}, u32[]{:S(2)}, u32[]{:S(2)}) %collective-permute-start.20) | collective-permute-done | bytes 36896 | tf_op jit(solution)/shard_map/ppermute | solution.py:63
  59.1 1.9 collective-permute-start.15
  61.9 2.6 collective-permute-start.7
  64.5 2.3 collective-permute-done.6
  66.8 3.0 collective-permute-start.8
  69.8 2.1 collective-permute-done.7
  71.9 2.0 collective-permute-done.8
  73.9 3.5 %collective-permute-start.22 = (bf16[2,1,48,768]{3,2,0,1:T(8,128)(2,1)S(1)}, bf16[2,1,48,768]{3,2,0,1:T(8,128)(2,1)S(1)}, u32[]{:S(2)}, u32[]{:S(2)}) collective-permute-start(bf16[2,1,48,768]{3,2,0,1:T(8,128)(2,1)S(1)} %bitcast.418), channel_id=1, source_target_pairs={{0,8},{1,9},{2,10},{3,11},{4,12},{5,13},{6,14},{7,15},{8,0},{9,1},... | collective-permute-start | bytes 442376 | tf_op jit(solution)/shard_map/ppermute | solution.py:63
  82.3 3.9 %collective-permute-done.22 = bf16[2,1,48,768]{3,2,0,1:T(8,128)(2,1)S(1)} collective-permute-done((bf16[2,1,48,768]{3,2,0,1:T(8,128)(2,1)S(1)}, bf16[2,1,48,768]{3,2,0,1:T(8,128)(2,1)S(1)}, u32[]{:S(2)}, u32[]{:S(2)}) %collective-permute-start.22) | collective-permute-done | bytes 147488 | tf_op jit(solution)/shard_map/ppermute | solution.py:63
  88.0 1.9 collective-permute-start.24
  94.8 10.0 %collective-permute-done.9 = bf16[2,4,48,576]{3,2,1,0:T(8,128)(2,1)S(1)} collective-permute-done((bf16[2,4,48,576]{3,2,1,0:T(8,128)(2,1)S(1)}, bf16[2,4,48,576]{3,2,1,0:T(8,128)(2,1)S(1)}, u32[]{:S(2)}, u32[]{:S(2)}) %collective-permute-start.9) | collective-permute-done | bytes 442400 | tf_op jit(solution)/shard_map/ppermute | solution.py:63
  105.2 1.8 reduce_sum.259
  107.1 2.7 maximum_select_fusion.2
  115.8 2.9 maximum_select_fusion.1
  128.4 2.8 fusion.19
  134.5 1.9 convert_reduce_fusion
  156.3 10.6 %collective-permute-done.56 = bf16[2,4,48,768]{3,2,1,0:T(8,128)(2,1)} collective-permute-done((bf16[2,4,48,768]{3,2,1,0:T(8,128)(2,1)}, bf16[2,4,48,768]{3,2,1,0:T(8,128)(2,1)}, u32[]{:S(2)}, u32[]{:S(2)}) %collective-permute-start.56) | collective-permute-done | bytes 589856 | tf_op jit(solution)/shard_map/ppermute | solution.py:63
  168.4 3.8 %collective-permute-start.58 = (bf16[2,1,48,768]{3,2,1,0:T(8,128)(2,1)S(1)}, bf16[2,1,48,768]{3,2,1,0:T(8,128)(2,1)S(1)}, u32[]{:S(2)}, u32[]{:S(2)}) collective-permute-start(bf16[2,1,48,768]{3,2,1,0:T(8,128)(2,1)S(1)} %get-tuple-element.42), channel_id=1, source_target_pairs={{0,8},{1,9},{2,10},{3,11},{4,12},{5,13},{6,14},{7,15},{8,0},{9,1},... | collective-permute-start | bytes 442376 | tf_op jit(solution)/shard_map/ppermute | solution.py:63
  174.1 1.9 collective-permute-done.57
  176.9 9.5 %collective-permute-done.58 = bf16[2,1,48,768]{3,2,1,0:T(8,128)(2,1)S(1)} collective-permute-done((bf16[2,1,48,768]{3,2,1,0:T(8,128)(2,1)S(1)}, bf16[2,1,48,768]{3,2,1,0:T(8,128)(2,1)S(1)}, u32[]{:S(2)}, u32[]{:S(2)}) %collective-permute-start.58) | collective-permute-done | bytes 147488 | tf_op jit(solution)/shard_map/ppermute | solution.py:63
  186.4 2.4 collective-permute-start.66
  190.3 5.6 %collective-permute-done.65 = bf16[1,1,96,768]{3,2,1,0:T(8,128)(2,1)S(1)} collective-permute-done((bf16[1,1,96,768]{3,2,1,0:T(8,128)(2,1)S(1)}, bf16[1,1,96,768]{3,2,1,0:T(8,128)(2,1)S(1)}, u32[]{:S(2)}, u32[]{:S(2)}) %collective-permute-start.65) | collective-permute-done | bytes 147488 | tf_op jit(solution)/shard_map/ppermute | solution.py:63
  220.3 1.8 collective-permute-start.52
  222.8 10.0 %collective-permute-done.52 = bf16[1,4,24,768]{3,2,1,0:T(8,128)(2,1)S(1)} collective-permute-done((bf16[1,4,24,768]{3,2,1,0:T(8,128)(2,1)S(1)}, bf16[1,4,24,768]{3,2,1,0:T(8,128)(2,1)S(1)}, u32[]{:S(2)}, u32[]{:S(2)}) %collective-permute-start.52) | collective-permute-done | bytes 147488 | tf_op jit(solution)/shard_map/ppermute | solution.py:63
  234.1 2.5 collective-permute-start.45
  239.1 1.7 collective-permute-done.45
  240.8 2.0 collective-permute-start.53
  242.8 5.8 %collective-permute-done.46 = bf16[2,1,48,576]{3,2,1,0:T(8,128)(2,1)S(1)} collective-permute-done((bf16[2,1,48,576]{3,2,1,0:T(8,128)(2,1)S(1)}, bf16[2,1,48,576]{3,2,1,0:T(8,128)(2,1)S(1)}, u32[]{:S(2)}, u32[]{:S(2)}) %collective-permute-start.46) | collective-permute-done | bytes 110624 | tf_op jit(solution)/shard_map/ppermute | solution.py:63
  248.7 2.3 collective-permute-start.55
  251.1 2.4 collective-permute-done.54
  257.4 2.1 collective-permute-done.49
  259.5 4.6 %collective-permute-done.50 = bf16[24,576]{1,0:T(8,128)(2,1)S(1)} collective-permute-done((bf16[24,576]{1,0:T(8,128)(2,1)S(1)}, bf16[24,576]{1,0:T(8,128)(2,1)S(1)}, u32[]{:S(2)}, u32[]{:S(2)}) %collective-permute-start.50) | collective-permute-done | bytes 27680 | tf_op jit(solution)/shard_map/ppermute | solution.py:63
  270.0 2.2 collective-permute-start.39
  272.3 2.4 collective-permute-start.41
  279.5 2.8 collective-permute-done.42
  282.5 1.8 fusion.20
  285.6 3.5 %all-to-all-start.2 = ((f32[32,1,216]{2,1,0:T(1,128)}), f32[32,1,216]{2,1,0:T(1,128)S(1)}, u32[]{:S(2)}, u32[]{:S(2)}) async-start(f32[32,1,216]{2,1,0:T(1,128)} %all_to_all.27), calls=%async_computation.2 | async-start | bytes 65536 | tf_op jit(solution)/shard_map/all_to_all | solution.py:345
  290.7 5.6 %all-to-all-done.2 = f32[32,1,216]{2,1,0:T(1,128)S(1)} async-done(((f32[32,1,216]{2,1,0:T(1,128)}), f32[32,1,216]{2,1,0:T(1,128)S(1)}, u32[]{:S(2)}, u32[]{:S(2)}) %all-to-all-start.2) | async-done | bytes 27680 | tf_op jit(solution)/shard_map/all_to_all | solution.py:345
  (472 shorter events, 122.1 us)
Async XLA Ops:
  0.7 35.7 %collective-permute-start.12 = (bf16[1,1,24,768]{3,2,1,0:T(8,128)(2,1)}, bf16[1,1,24,768]{3,2,1,0:T(8,128)(2,1)S(1)}, u32[]{:S(2)}, u32[]{:S(2)}) collective-permute-start(bf16[1,1,24,768]{3,2,1,0:T(8,128)(2,1)} %bitcast.458), channel_id=1, source_target_pairs={{0,4},{1,5},{2,6},{3,7},{4,0},{5,1},{6,2},{7,3},{8,12},{9,13},{10,... | collective-permute-start | bytes 110600 | tf_op jit(solution)/shard_map/ppermute | solution.py:63
  3.8 33.0 %collective-permute-start.13 = (bf16[1,1,24,768]{3,2,1,0:T(8,128)(2,1)}, bf16[1,1,24,768]{3,2,1,0:T(8,128)(2,1)S(1)}, u32[]{:S(2)}, u32[]{:S(2)}) collective-permute-start(bf16[1,1,24,768]{3,2,1,0:T(8,128)(2,1)} %bitcast.459), channel_id=1, source_target_pairs={{0,8},{1,9},{2,10},{3,11},{4,12},{5,13},{6,14},{7,15},{8,0},{9,1},... | collective-permute-start | bytes 110600 | tf_op jit(solution)/shard_map/ppermute | solution.py:63
  6.4 32.0 %collective-permute-start.14 = (bf16[1,1,24,768]{3,2,1,0:T(8,128)(2,1)}, bf16[1,1,24,768]{3,2,1,0:T(8,128)(2,1)S(1)}, u32[]{:S(2)}, u32[]{:S(2)}) collective-permute-start(bf16[1,1,24,768]{3,2,1,0:T(8,128)(2,1)} %bitcast.460), channel_id=1, source_target_pairs={{0,12},{1,13},{2,14},{3,15},{4,8},{5,9},{6,10},{7,11},{8,4},{9,5},... | collective-permute-start | bytes 110600 | tf_op jit(solution)/shard_map/ppermute | solution.py:63
  7.8 26.0 %collective-permute-start.18 = (bf16[24,768]{1,0:T(8,128)(2,1)S(1)}, bf16[24,768]{1,0:T(8,128)(2,1)S(1)}, u32[]{:S(2)}, u32[]{:S(2)}) collective-permute-start(bf16[24,768]{1,0:T(8,128)(2,1)S(1)} %dynamic-slice_bitcast_fusion.10), channel_id=1, source_target_pairs={{0,1},{1,0},{2,3},{3,2},{4,5},{5,4},{6,7},{7,6},{8,9},{9,8},{10,11... | collective-permute-start | bytes 110600 | tf_op jit(solution)/shard_map/ppermute | solution.py:63
  9.3 23.0 %collective-permute-start.3 = (bf16[24,576]{1,0:T(8,128)(2,1)S(1)}, bf16[24,576]{1,0:T(8,128)(2,1)S(1)}, u32[]{:S(2)}, u32[]{:S(2)}) collective-permute-start(bf16[24,576]{1,0:T(8,128)(2,1)S(1)} %dynamic-slice_bitcast_fusion.16), channel_id=1, source_target_pairs={{0,1},{1,0},{2,3},{3,2},{4,5},{5,4},{6,7},{7,6},{8,9},{9,8},{10,11... | collective-permute-start | bytes 82952 | tf_op jit(solution)/shard_map/ppermute | solution.py:63
  11.4 13.3 %all-to-all-start = ((bf16[32,1,216]{2,1,0:T(2,128)(2,1)}), bf16[32,1,216]{2,1,0:T(2,128)(2,1)S(1)}, u32[]{:S(2)}, u32[]{:S(2)}) async-start(bf16[32,1,216]{2,1,0:T(2,128)(2,1)} %copy.159), calls=%async_computation | async-start | bytes 65536 | tf_op jit(solution)/shard_map/all_to_all | solution.py:169
  27.1 78.1 %all-to-all-start.1 = ((f32[32,1,4608]{2,1,0:T(1,128)}), f32[32,1,4608]{2,1,0:T(1,128)}, u32[]{:S(2)}, u32[]{:S(2)}) async-start(f32[32,1,4608]{2,1,0:T(1,128)} %all_to_all.25), calls=%async_computation.1 | async-start | bytes 1179648 | tf_op jit(solution)/shard_map/all_to_all | solution.py:197
  32.2 26.9 %collective-permute-start.25 = (bf16[1,1,96,768]{3,2,1,0:T(8,128)(2,1)S(1)}, bf16[1,1,96,768]{3,2,1,0:T(8,128)(2,1)S(1)}, u32[]{:S(2)}, u32[]{:S(2)}) collective-permute-start(bf16[1,1,96,768]{3,2,1,0:T(8,128)(2,1)S(1)} %bitcast.449), channel_id=1, source_target_pairs={{0,4},{1,5},{2,6},{3,7},{4,0},{5,1},{6,2},{7,3},{8,12},{9,13},{10,... | collective-permute-start | bytes 442376 | tf_op jit(solution)/shard_map/ppermute | solution.py:63
  33.9 27.2 %collective-permute-start.26 = (bf16[1,1,96,768]{3,2,1,0:T(8,128)(2,1)S(1)}, bf16[1,1,96,768]{3,2,1,0:T(8,128)(2,1)S(1)}, u32[]{:S(2)}, u32[]{:S(2)}) collective-permute-start(bf16[1,1,96,768]{3,2,1,0:T(8,128)(2,1)S(1)} %bitcast.450), channel_id=1, source_target_pairs={{0,8},{1,9},{2,10},{3,11},{4,12},{5,13},{6,14},{7,15},{8,0},{9,1},... | collective-permute-start | bytes 442376 | tf_op jit(solution)/shard_map/ppermute | solution.py:63
  36.4 25.4 %collective-permute-start.27 = (bf16[1,1,96,768]{3,2,1,0:T(8,128)(2,1)S(1)}, bf16[1,1,96,768]{3,2,1,0:T(8,128)(2,1)S(1)}, u32[]{:S(2)}, u32[]{:S(2)}) collective-permute-start(bf16[1,1,96,768]{3,2,1,0:T(8,128)(2,1)S(1)} %bitcast.451), channel_id=1, source_target_pairs={{0,12},{1,13},{2,14},{3,15},{4,8},{5,9},{6,10},{7,11},{8,4},{9,5},... | collective-permute-start | bytes 442376 | tf_op jit(solution)/shard_map/ppermute | solution.py:63
  36.8 41.1 %collective-permute-start = (bf16[1,128,768]{2,1,0:T(8,128)(2,1)S(1)}, bf16[1,128,768]{2,1,0:T(8,128)(2,1)S(1)}, u32[]{:S(2)}, u32[]{:S(2)}) collective-permute-start(bf16[1,128,768]{2,1,0:T(8,128)(2,1)S(1)} %copy-done.37), channel_id=1, source_target_pairs={{0,16},{1,17},{2,18},{3,19},{4,20},{5,21},{6,22},{7,23},{8,24},{9,... | collective-permute-start | bytes 589832 | tf_op jit(solution)/shard_map/ppermute | solution.py:63
  38.4 7.2 %collective-permute-start.4 = (bf16[24,576]{1,0:T(8,128)(2,1)S(1)}, bf16[24,576]{1,0:T(8,128)(2,1)S(1)}, u32[]{:S(2)}, u32[]{:S(2)}) collective-permute-start(bf16[24,576]{1,0:T(8,128)(2,1)S(1)} %get-tuple-element.64), channel_id=1, source_target_pairs={{0,16},{1,17},{2,18},{3,19},{4,20},{5,21},{6,22},{7,23},{8,24},{9,... | collective-permute-start | bytes 82952 | tf_op jit(solution)/shard_map/ppermute | solution.py:63
  56.4 22.6 %collective-permute-start.31 = (bf16[1,128,768]{2,1,0:T(8,128)(2,1)S(1)}, bf16[1,128,768]{2,1,0:T(8,128)(2,1)S(1)}, u32[]{:S(2)}, u32[]{:S(2)}) collective-permute-start(bf16[1,128,768]{2,1,0:T(8,128)(2,1)S(1)} %copy-done.35), channel_id=1, source_target_pairs={{0,16},{1,17},{2,18},{3,19},{4,20},{5,21},{6,22},{7,23},{8,24},{9,... | collective-permute-start | bytes 589832 | tf_op jit(solution)/shard_map/ppermute | solution.py:63
  59.1 18.3 %collective-permute-start.15 = (bf16[1,4,24,768]{3,2,1,0:T(8,128)(2,1)S(1)}, bf16[1,4,24,768]{3,2,1,0:T(8,128)(2,1)S(1)}, u32[]{:S(2)}, u32[]{:S(2)}) collective-permute-start(bf16[1,4,24,768]{3,2,1,0:T(8,128)(2,1)S(1)} %bitcast.436), channel_id=1, source_target_pairs={{0,2},{1,3},{2,0},{3,1},{4,6},{5,7},{6,4},{7,5},{8,10},{9,11},{10,... | collective-permute-start | bytes 442376 | tf_op jit(solution)/shard_map/ppermute | solution.py:63
  61.9 10.0 %collective-permute-start.7 = (bf16[2,1,48,576]{3,2,0,1:T(8,128)(2,1)S(1)}, bf16[2,1,48,576]{3,2,0,1:T(8,128)(2,1)S(1)}, u32[]{:S(2)}, u32[]{:S(2)}) collective-permute-start(bf16[2,1,48,576]{3,2,0,1:T(8,128)(2,1)S(1)} %bitcast.426), channel_id=1, source_target_pairs={{0,8},{1,9},{2,10},{3,11},{4,12},{5,13},{6,14},{7,15},{8,0},{9,1},... | collective-permute-start | bytes 331784 | tf_op jit(solution)/shard_map/ppermute | solution.py:63
  66.8 7.1 %collective-permute-start.8 = (bf16[2,1,48,576]{3,2,0,1:T(8,128)(2,1)S(1)}, bf16[2,1,48,576]{3,2,0,1:T(8,128)(2,1)S(1)}, u32[]{:S(2)}, u32[]{:S(2)}) collective-permute-start(bf16[2,1,48,576]{3,2,0,1:T(8,128)(2,1)S(1)} %bitcast.427), channel_id=1, source_target_pairs={{0,12},{1,13},{2,14},{3,15},{4,8},{5,9},{6,10},{7,11},{8,4},{9,5},... | collective-permute-start | bytes 331784 | tf_op jit(solution)/shard_map/ppermute | solution.py:63
  71.9 8.4 %collective-permute-start.21 = (bf16[2,1,48,768]{3,2,0,1:T(8,128)(2,1)S(1)}, bf16[2,1,48,768]{3,2,0,1:T(8,128)(2,1)S(1)}, u32[]{:S(2)}, u32[]{:S(2)}) collective-permute-start(bf16[2,1,48,768]{3,2,0,1:T(8,128)(2,1)S(1)} %bitcast.417), channel_id=1, source_target_pairs={{0,4},{1,5},{2,6},{3,7},{4,0},{5,1},{6,2},{7,3},{8,12},{9,13},{10,... | collective-permute-start | bytes 442376 | tf_op jit(solution)/shard_map/ppermute | solution.py:63
  73.9 12.3 %collective-permute-start.22 = (bf16[2,1,48,768]{3,2,0,1:T(8,128)(2,1)S(1)}, bf16[2,1,48,768]{3,2,0,1:T(8,128)(2,1)S(1)}, u32[]{:S(2)}, u32[]{:S(2)}) collective-permute-start(bf16[2,1,48,768]{3,2,0,1:T(8,128)(2,1)S(1)} %bitcast.418), channel_id=1, source_target_pairs={{0,8},{1,9},{2,10},{3,11},{4,12},{5,13},{6,14},{7,15},{8,0},{9,1},... | collective-permute-start | bytes 442376 | tf_op jit(solution)/shard_map/ppermute | solution.py:63
  77.4 9.5 %collective-permute-start.23 = (bf16[2,1,48,768]{3,2,0,1:T(8,128)(2,1)S(1)}, bf16[2,1,48,768]{3,2,0,1:T(8,128)(2,1)S(1)}, u32[]{:S(2)}, u32[]{:S(2)}) collective-permute-start(bf16[2,1,48,768]{3,2,0,1:T(8,128)(2,1)S(1)} %bitcast.419), channel_id=1, source_target_pairs={{0,12},{1,13},{2,14},{3,15},{4,8},{5,9},{6,10},{7,11},{8,4},{9,5},... | collective-permute-start | bytes 442376 | tf_op jit(solution)/shard_map/ppermute | solution.py:63
  78.0 29.1 %collective-permute-start.28 = (bf16[1,4,96,768]{3,2,1,0:T(8,128)(2,1)S(1)}, bf16[1,4,96,768]{3,2,1,0:T(8,128)(2,1)}, u32[]{:S(2)}, u32[]{:S(2)}) collective-permute-start(bf16[1,4,96,768]{3,2,1,0:T(8,128)(2,1)S(1)} %bitcast.378), channel_id=1, source_target_pairs={{0,2},{1,3},{2,0},{3,1},{4,6},{5,7},{6,4},{7,5},{8,10},{9,11},{10,... | collective-permute-start | bytes 1769480 | tf_op jit(solution)/shard_map/ppermute | solution.py:63
  79.0 25.8 %collective-permute-start.9 = (bf16[2,4,48,576]{3,2,1,0:T(8,128)(2,1)S(1)}, bf16[2,4,48,576]{3,2,1,0:T(8,128)(2,1)S(1)}, u32[]{:S(2)}, u32[]{:S(2)}) collective-permute-start(bf16[2,4,48,576]{3,2,1,0:T(8,128)(2,1)S(1)} %bitcast.397), channel_id=1, source_target_pairs={{0,2},{1,3},{2,0},{3,1},{4,6},{5,7},{6,4},{7,5},{8,10},{9,11},{10,... | collective-permute-start | bytes 1327112 | tf_op jit(solution)/shard_map/ppermute | solution.py:63
  80.2 7.8 %collective-permute-start.16 = (bf16[8,24,768]{2,1,0:T(8,128)(2,1)S(1)}, bf16[8,24,768]{2,1,0:T(8,128)(2,1)S(1)}, u32[]{:S(2)}, u32[]{:S(2)}) collective-permute-start(bf16[8,24,768]{2,1,0:T(8,128)(2,1)S(1)} %bitcast.390), channel_id=1, source_target_pairs={{0,16},{1,17},{2,18},{3,19},{4,20},{5,21},{6,22},{7,23},{8,24},{9,... | collective-permute-start | bytes 884744 | tf_op jit(solution)/shard_map/ppermute | solution.py:63
  88.0 27.8 %collective-permute-start.24 = (bf16[2,4,48,768]{3,2,1,0:T(8,128)(2,1)}, bf16[2,4,48,768]{3,2,1,0:T(8,128)(2,1)}, u32[]{:S(2)}, u32[]{:S(2)}) collective-permute-start(bf16[2,4,48,768]{3,2,1,0:T(8,128)(2,1)} %bitcast.76), channel_id=1, source_target_pairs={{0,2},{1,3},{2,0},{3,1},{4,6},{5,7},{6,4},{7,5},{8,10},{9,11},{10,... | collective-permute-start | bytes 1769480 | tf_op jit(solution)/shard_map/ppermute | solution.py:63
  91.7 27.0 %collective-permute-start.17 = (bf16[2,8,24,768]{3,2,1,0:T(8,128)(2,1)}, bf16[2,8,24,768]{3,2,1,0:T(8,128)(2,1)}, u32[]{:S(2)}, u32[]{:S(2)}) collective-permute-start(bf16[2,8,24,768]{3,2,1,0:T(8,128)(2,1)} %maximum_select_fusion.9), channel_id=1, source_target_pairs={{0,1},{1,0},{2,3},{3,2},{4,5},{5,4},{6,7},{7,6},{8,9},{9,8},{10,11... | collective-permute-start | bytes 1769480 | tf_op jit(solution)/shard_map/ppermute | solution.py:63
  114.5 7.6 %collective-permute-start.10 = (bf16[512,192]{0,1:T(8,128)(2,1)}, bf16[512,192]{0,1:T(8,128)(2,1)}, u32[]{:S(2)}, u32[]{:S(2)}) collective-permute-start(bf16[512,192]{0,1:T(8,128)(2,1)} %bitcast.192), channel_id=1, source_target_pairs={{0,16},{1,17},{2,18},{3,19},{4,20},{5,21},{6,22},{7,23},{8,24},{9,... | collective-permute-start | bytes 589832 | tf_op jit(solution)/shard_map/ppermute | solution.py:63
  138.2 16.5 %collective-permute-start.63 = (bf16[1,4,96,768]{3,2,1,0:T(8,128)(2,1)}, bf16[1,4,96,768]{3,2,1,0:T(8,128)(2,1)}, u32[]{:S(2)}, u32[]{:S(2)}) collective-permute-start(bf16[1,4,96,768]{3,2,1,0:T(8,128)(2,1)} %dynamic-slice_bitcast_fusion), channel_id=1, source_target_pairs={{0,2},{1,3},{2,0},{3,1},{4,6},{5,7},{6,4},{7,5},{8,10},{9,11},{10,... | collective-permute-start | bytes 1769480 | tf_op jit(solution)/shard_map/ppermute | solution.py:63
  141.2 25.7 %collective-permute-start.56 = (bf16[2,4,48,768]{3,2,1,0:T(8,128)(2,1)}, bf16[2,4,48,768]{3,2,1,0:T(8,128)(2,1)}, u32[]{:S(2)}, u32[]{:S(2)}) collective-permute-start(bf16[2,4,48,768]{3,2,1,0:T(8,128)(2,1)} %dynamic-slice_bitcast_fusion.1), channel_id=1, source_target_pairs={{0,2},{1,3},{2,0},{3,1},{4,6},{5,7},{6,4},{7,5},{8,10},{9,11},{10,... | collective-permute-start | bytes 1769480 | tf_op jit(solution)/shard_map/ppermute | solution.py:63
  151.5 46.6 %collective-permute-start.34 = (bf16[1,256,768]{2,1,0:T(8,128)(2,1)S(1)}, bf16[1,256,768]{2,1,0:T(8,128)(2,1)S(1)}, u32[]{:S(2)}, u32[]{:S(2)}) collective-permute-start(bf16[1,256,768]{2,1,0:T(8,128)(2,1)S(1)} %add_convert_fusion.2), channel_id=1, source_target_pairs={{0,16},{1,17},{2,18},{3,19},{4,20},{5,21},{6,22},{7,23},{8,24},{9,... | collective-permute-start | bytes 1179656 | tf_op jit(solution)/shard_map/ppermute | solution.py:63
  154.0 18.2 %collective-permute-start.30 = (bf16[1,128,768]{2,1,0:T(8,128)(2,1)S(1)}, bf16[1,128,768]{2,1,0:T(8,128)(2,1)S(1)}, u32[]{:S(2)}, u32[]{:S(2)}) collective-permute-start(bf16[1,128,768]{2,1,0:T(8,128)(2,1)S(1)} %fusion.25), channel_id=1, source_target_pairs={{0,16},{1,17},{2,18},{3,19},{4,20},{5,21},{6,22},{7,23},{8,24},{9,... | collective-permute-start | bytes 589832 | tf_op jit(solution)/shard_map/ppermute | solution.py:63
  156.2 34.0 %collective-permute-start.64 = (bf16[1,1,96,768]{3,2,1,0:T(8,128)(2,1)S(1)}, bf16[1,1,96,768]{3,2,1,0:T(8,128)(2,1)S(1)}, u32[]{:S(2)}, u32[]{:S(2)}) collective-permute-start(bf16[1,1,96,768]{3,2,1,0:T(8,128)(2,1)S(1)} %get-tuple-element.37), channel_id=1, source_target_pairs={{0,4},{1,5},{2,6},{3,7},{4,0},{5,1},{6,2},{7,3},{8,12},{9,13},{10,... | collective-permute-start | bytes 442376 | tf_op jit(solution)/shard_map/ppermute | solution.py:63
  168.2 7.8 %collective-permute-start.57 = (bf16[2,1,48,768]{3,2,1,0:T(8,128)(2,1)S(1)}, bf16[2,1,48,768]{3,2,1,0:T(8,128)(2,1)S(1)}, u32[]{:S(2)}, u32[]{:S(2)}) collective-permute-start(bf16[2,1,48,768]{3,2,1,0:T(8,128)(2,1)S(1)} %get-tuple-element.40), channel_id=1, source_target_pairs={{0,4},{1,5},{2,6},{3,7},{4,0},{5,1},{6,2},{7,3},{8,12},{9,13},{10,... | collective-permute-start | bytes 442376 | tf_op jit(solution)/shard_map/ppermute | solution.py:63
  168.4 18.0 %collective-permute-start.58 = (bf16[2,1,48,768]{3,2,1,0:T(8,128)(2,1)S(1)}, bf16[2,1,48,768]{3,2,1,0:T(8,128)(2,1)S(1)}, u32[]{:S(2)}, u32[]{:S(2)}) collective-permute-start(bf16[2,1,48,768]{3,2,1,0:T(8,128)(2,1)S(1)} %get-tuple-element.42), channel_id=1, source_target_pairs={{0,8},{1,9},{2,10},{3,11},{4,12},{5,13},{6,14},{7,15},{8,0},{9,1},... | collective-permute-start | bytes 442376 | tf_op jit(solution)/shard_map/ppermute | solution.py:63
  172.2 16.6 %collective-permute-start.59 = (bf16[2,1,48,768]{3,2,1,0:T(8,128)(2,1)S(1)}, bf16[2,1,48,768]{3,2,1,0:T(8,128)(2,1)S(1)}, u32[]{:S(2)}, u32[]{:S(2)}) collective-permute-start(bf16[2,1,48,768]{3,2,1,0:T(8,128)(2,1)S(1)} %get-tuple-element.41), channel_id=1, source_target_pairs={{0,12},{1,13},{2,14},{3,15},{4,8},{5,9},{6,10},{7,11},{8,4},{9,5},... | collective-permute-start | bytes 442376 | tf_op jit(solution)/shard_map/ppermute | solution.py:63
  176.0 19.9 %collective-permute-start.65 = (bf16[1,1,96,768]{3,2,1,0:T(8,128)(2,1)S(1)}, bf16[1,1,96,768]{3,2,1,0:T(8,128)(2,1)S(1)}, u32[]{:S(2)}, u32[]{:S(2)}) collective-permute-start(bf16[1,1,96,768]{3,2,1,0:T(8,128)(2,1)S(1)} %get-tuple-element.39), channel_id=1, source_target_pairs={{0,8},{1,9},{2,10},{3,11},{4,12},{5,13},{6,14},{7,15},{8,0},{9,1},... | collective-permute-start | bytes 442376 | tf_op jit(solution)/shard_map/ppermute | solution.py:63
  186.4 9.5 %collective-permute-start.66 = (bf16[1,1,96,768]{3,2,1,0:T(8,128)(2,1)S(1)}, bf16[1,1,96,768]{3,2,1,0:T(8,128)(2,1)S(1)}, u32[]{:S(2)}, u32[]{:S(2)}) collective-permute-start(bf16[1,1,96,768]{3,2,1,0:T(8,128)(2,1)S(1)} %get-tuple-element.38), channel_id=1, source_target_pairs={{0,12},{1,13},{2,14},{3,15},{4,8},{5,9},{6,10},{7,11},{8,4},{9,5},... | collective-permute-start | bytes 442376 | tf_op jit(solution)/shard_map/ppermute | solution.py:63
  188.8 80.0 %collective-permute-start.38 = (f32[1,1,768]{2,1,0:T(1,128)}, f32[1,1,768]{2,1,0:T(1,128)}, u32[]{:S(2)}, u32[]{:S(2)}) collective-permute-start(f32[1,1,768]{2,1,0:T(1,128)} %broadcast_in_dim.280), channel_id=1, source_target_pairs={{0,16},{1,17},{2,18},{3,19},{4,20},{5,21},{6,22},{7,23},{8,24},{9,... | collective-permute-start | bytes 9224 | tf_op jit(solution)/shard_map/ppermute | solution.py:63
  211.6 7.7 %collective-permute-start.51 = (bf16[4,24,768]{2,1,0:T(8,128)(2,1)}, bf16[4,24,768]{2,1,0:T(8,128)(2,1)}, u32[]{:S(2)}, u32[]{:S(2)}) collective-permute-start(bf16[4,24,768]{2,1,0:T(8,128)(2,1)} %dynamic-slice_bitcast_fusion.4), channel_id=1, source_target_pairs={{0,1},{1,0},{2,3},{3,2},{4,5},{5,4},{6,7},{7,6},{8,9},{9,8},{10,11... | collective-permute-start | bytes 442376 | tf_op jit(solution)/shard_map/ppermute | solution.py:63
  215.9 16.9 %collective-permute-start.44 = (bf16[2,4,48,576]{3,2,1,0:T(8,128)(2,1)}, bf16[2,4,48,576]{3,2,1,0:T(8,128)(2,1)}, u32[]{:S(2)}, u32[]{:S(2)}) collective-permute-start(bf16[2,4,48,576]{3,2,1,0:T(8,128)(2,1)} %dynamic-slice_bitcast_fusion.2), channel_id=1, source_target_pairs={{0,2},{1,3},{2,0},{3,1},{4,6},{5,7},{6,4},{7,5},{8,10},{9,11},{10,... | collective-permute-start | bytes 1327112 | tf_op jit(solution)/shard_map/ppermute | solution.py:63
  218.9 37.5 %collective-permute-start.36 = (bf16[1,256,768]{2,1,0:T(8,128)(2,1)}, bf16[1,256,768]{2,1,0:T(8,128)(2,1)S(1)}, u32[]{:S(2)}, u32[]{:S(2)}) collective-permute-start(bf16[1,256,768]{2,1,0:T(8,128)(2,1)} %dynamic-slice_convert_fusion), channel_id=1, source_target_pairs={{0,1},{1,0},{2,3},{3,2},{4,5},{5,4},{6,7},{7,6},{8,9},{9,8},{10,11... | collective-permute-start | bytes 1179656 | tf_op jit(solution)/shard_map/ppermute | solution.py:63
  220.3 12.5 %collective-permute-start.52 = (bf16[1,4,24,768]{3,2,1,0:T(8,128)(2,1)S(1)}, bf16[1,4,24,768]{3,2,1,0:T(8,128)(2,1)S(1)}, u32[]{:S(2)}, u32[]{:S(2)}) collective-permute-start(bf16[1,4,24,768]{3,2,1,0:T(8,128)(2,1)S(1)} %dynamic-slice_bitcast_fusion.3), channel_id=1, source_target_pairs={{0,2},{1,3},{2,0},{3,1},{4,6},{5,7},{6,4},{7,5},{8,10},{9,11},{10,... | collective-permute-start | bytes 442376 | tf_op jit(solution)/shard_map/ppermute | solution.py:63
  234.1 6.7 %collective-permute-start.45 = (bf16[2,1,48,576]{3,2,1,0:T(8,128)(2,1)S(1)}, bf16[2,1,48,576]{3,2,1,0:T(8,128)(2,1)S(1)}, u32[]{:S(2)}, u32[]{:S(2)}) collective-permute-start(bf16[2,1,48,576]{3,2,1,0:T(8,128)(2,1)S(1)} %get-tuple-element.45), channel_id=1, source_target_pairs={{0,4},{1,5},{2,6},{3,7},{4,0},{5,1},{6,2},{7,3},{8,12},{9,13},{10,... | collective-permute-start | bytes 331784 | tf_op jit(solution)/shard_map/ppermute | solution.py:63
  236.6 12.1 %collective-permute-start.46 = (bf16[2,1,48,576]{3,2,1,0:T(8,128)(2,1)S(1)}, bf16[2,1,48,576]{3,2,1,0:T(8,128)(2,1)S(1)}, u32[]{:S(2)}, u32[]{:S(2)}) collective-permute-start(bf16[2,1,48,576]{3,2,1,0:T(8,128)(2,1)S(1)} %get-tuple-element.47), channel_id=1, source_target_pairs={{0,8},{1,9},{2,10},{3,11},{4,12},{5,13},{6,14},{7,15},{8,0},{9,1},... | collective-permute-start | bytes 331784 | tf_op jit(solution)/shard_map/ppermute | solution.py:63
  237.6 11.0 %collective-permute-start.47 = (bf16[2,1,48,576]{3,2,1,0:T(8,128)(2,1)S(1)}, bf16[2,1,48,576]{3,2,1,0:T(8,128)(2,1)S(1)}, u32[]{:S(2)}, u32[]{:S(2)}) collective-permute-start(bf16[2,1,48,576]{3,2,1,0:T(8,128)(2,1)S(1)} %get-tuple-element.46), channel_id=1, source_target_pairs={{0,12},{1,13},{2,14},{3,15},{4,8},{5,9},{6,10},{7,11},{8,4},{9,5},... | collective-permute-start | bytes 331784 | tf_op jit(solution)/shard_map/ppermute | solution.py:63
  240.8 10.3 %collective-permute-start.53 = (bf16[1,1,24,768]{3,2,1,0:T(8,128)(2,1)S(1)}, bf16[1,1,24,768]{3,2,1,0:T(8,128)(2,1)S(1)}, u32[]{:S(2)}, u32[]{:S(2)}) collective-permute-start(bf16[1,1,24,768]{3,2,1,0:T(8,128)(2,1)S(1)} %get-tuple-element.51), channel_id=1, source_target_pairs={{0,4},{1,5},{2,6},{3,7},{4,0},{5,1},{6,2},{7,3},{8,12},{9,13},{10,... | collective-permute-start | bytes 110600 | tf_op jit(solution)/shard_map/ppermute | solution.py:63
  256.6 8.9 %collective-permute-start.37 = (bf16[1,256,768]{2,1,0:T(8,128)(2,1)S(1)}, bf16[1,256,768]{2,1,0:T(8,128)(2,1)S(1)}, u32[]{:S(2)}, u32[]{:S(2)}) collective-permute-start(bf16[1,256,768]{2,1,0:T(8,128)(2,1)S(1)} %add_convert_fusion.1), channel_id=1, source_target_pairs={{0,16},{1,17},{2,18},{3,19},{4,20},{5,21},{6,22},{7,23},{8,24},{9,... | collective-permute-start | bytes 1179656 | tf_op jit(solution)/shard_map/ppermute | solution.py:63
  257.4 6.7 %collective-permute-start.50 = (bf16[24,576]{1,0:T(8,128)(2,1)S(1)}, bf16[24,576]{1,0:T(8,128)(2,1)S(1)}, u32[]{:S(2)}, u32[]{:S(2)}) collective-permute-start(bf16[24,576]{1,0:T(8,128)(2,1)S(1)} %get-tuple-element.60), channel_id=1, source_target_pairs={{0,17},{1,16},{2,19},{3,18},{4,21},{5,20},{6,23},{7,22},{8,25},{9,... | collective-permute-start | bytes 82952 | tf_op jit(solution)/shard_map/ppermute | solution.py:63
  270.0 6.8 %collective-permute-start.39 = (bf16[1,1,1,4608]{3,2,1,0:T(2,128)(2,1)}, bf16[1,1,1,4608]{3,2,1,0:T(2,128)(2,1)S(1)}, u32[]{:S(2)}, u32[]{:S(2)}) collective-permute-start(bf16[1,1,1,4608]{3,2,1,0:T(2,128)(2,1)} %constant_dynamic-update-slice_fusion.6), channel_id=1, source_target_pairs={{0,4},{1,5},{2,6},{3,7},{4,0},{5,1},{6,2},{7,3},{8,12},{9,13},{10,... | collective-permute-start | bytes 27656 | tf_op jit(solution)/shard_map/ppermute | solution.py:63
  285.6 10.7 %all-to-all-start.2 = ((f32[32,1,216]{2,1,0:T(1,128)}), f32[32,1,216]{2,1,0:T(1,128)S(1)}, u32[]{:S(2)}, u32[]{:S(2)}) async-start(f32[32,1,216]{2,1,0:T(1,128)} %all_to_all.27), calls=%async_computation.2 | async-start | bytes 65536 | tf_op jit(solution)/shard_map/all_to_all | solution.py:345
  (88 other events, 630.7 us)

commit v2 on v1

--- a/solution.py
+++ b/solution.py
@@ -41,6 +41,10 @@
     return lax.dot_general(left, right, (((0,), (0,)), ((), ())), preferred_element_type=F32)
 
 
+def after(value, *earlier):
+    return lax.optimization_barrier((value,) + earlier)[0]
+
+
 class Links:
     def __init__(self, devices):
         self.devices = devices
@@ -61,6 +65,10 @@
     def send(self, value, bits, step=1):
         mask = self.mask(bits, step)
         return lax.ppermute(value, AXES, [(i, i ^ mask) for i in range(self.devices)])
+
+    def own_first(self, value, bits, axis):
+        arrived = [value] + [self.send(value, bits, step) for step in range(1, 1 << len(bits))]
+        return jnp.stack(arrived, axis)
 
     def gather(self, value, bits, axis):
         count = 1 << len(bits)
@@ -87,12 +95,18 @@
             out = lax.dynamic_update_index_in_dim(out, part, spot ^ step, 0)
         return out
 
-    def scatter(self, value, bits, axis):
+    def scatter(self, value, bits, axis, earlier=()):
         spot = self.place(bits)
-        total = self.pick(value, spot, axis).astype(F32)
+        arrived = []
         for step in range(1, 1 << len(bits)):
             part = self.pick(value, spot ^ step, axis).astype(BF16)
-            total = total + self.send(part, bits, step).astype(F32)
+            arrived.append(self.send(part, bits, step))
+        total = self.pick(value, spot, axis)
+        if earlier:
+            total = after(total, *earlier)
+        total = total.astype(F32)
+        for part in arrived:
+            total = total + part.astype(F32)
         return total
 
 
@@ -139,25 +153,42 @@
     group = width // team
     heads = group // HD
     count = 2 * latents
-
-    def gather_rest(value):
+    own_flat = latents * seq_len
+
+    def gather_rest(value, earlier=()):
         first, last = value.shape[0], value.shape[1:]
         value = value[:, None]
+        if earlier:
+            value = after(value, *earlier)
+        begun = None
         for bits in bit_groups(rest_bits):
             value = link.gather(value, bits, 2)
             value = value.reshape((first, -1) + last)
-        return value
-
-    def scatter_rest(value):
+            begun = value if begun is None else begun
+        return value, begun
+
+    def scatter_rest(value, earlier=()):
         first, last = value.shape[0], value.shape[2:]
-        for bits in bit_groups(rest_bits)[::-1]:
+        for at, bits in enumerate(bit_groups(rest_bits)[::-1]):
             value = value.reshape((first, -1, 1 << len(bits)) + last)
-            value = link.scatter(value, bits, 2)
+            value = link.scatter(value, bits, 2, earlier[at] if at < len(earlier) else ())
         return value[:, 0]
 
-    def both_halves(value):
-        value = link.gather(value, seq_bits, 1).reshape(latents, seq_len, -1)
-        return link.gather(value, core_bit, 0).reshape(count, seq_len, -1)
+    def all_rest(value):
+        for bits in bit_groups(rest_bits) + [core_bit]:
+            lead = value.shape[:-2]
+            value = link.own_first(value, bits, len(lead))
+            value = value.reshape((-1,) + value.shape[-2:])
+        there = link.index % fsdp ^ jnp.arange(fsdp)
+        order = (jnp.arange(fsdp)[:, None] == there[None, :]).astype(value.dtype)
+        value = dot(order, value.reshape(fsdp, -1)).astype(value.dtype)
+        return value.reshape(fsdp * latents, -1)
+
+    def halves(value):
+        return link.gather(value, seq_bits, 1).reshape(latents, seq_len, -1)
+
+    def cores(value):
+        return link.own_first(value, core_bit, 0).reshape((count,) + value.shape[1:])
 
     cond_float = cond.astype(F32)
     silu_cond = jax.nn.silu(cond_float).astype(BF16)
@@ -176,19 +207,6 @@
     bias_fc1 = small[:, mine + 4 * rows :].reshape(seq, rest, 2, hidden_rows)
     bias_fc1 = link.pick(link.pick(bias_fc1, half, 0), core, 1).reshape(-1).astype(F32)
 
-    team_qkv = w_qkv.reshape(rows, 3, team, group).transpose(2, 0, 1, 3)
-    team_qkv = link.exchange(team_qkv.reshape(team, rows, 3 * group), team_bits)
-    my_qkv = gather_rest(team_qkv.reshape(seq, 2 * rows, 3 * group)).reshape(width, 3 * group)
-    full_proj = gather_rest(w_proj[None])[0]
-    full_proj = link.gather(full_proj, seq_bits, 0)
-    full_proj = link.gather(full_proj, core_bit, 2).reshape(width, width)
-    team_fc1 = w_fc1.reshape(rows, seq, rest, 2, hidden_rows).transpose(1, 3, 0, 2, 4)
-    team_fc1 = link.exchange(team_fc1.reshape(team, rows, hidden), team_bits)
-    my_fc1 = gather_rest(team_fc1.reshape(seq, 2 * rows, hidden)).reshape(width, hidden)
-    my_fc2 = gather_rest(w_fc2[None]).reshape(hidden, width)
-    all_tokens = both_halves(tokens).astype(F32)
-    all_cotangent = both_halves(cotangent).astype(F32)
-
     part = dot(all_cond, w_ada)
     own_columns = (jnp.arange(shards) == link.index)[:, None] * b_ada.astype(F32)[None, :]
     part = part + own_columns.reshape(-1)
@@ -196,29 +214,49 @@
     part = jnp.broadcast_to(part, (seq, fsdp, latents * 6 * width)).reshape(shards, -1)
     part = lax.all_to_all(part, AXES, 0, 0, tiled=True)
     modulation = jnp.sum(part, axis=0).reshape(latents, 1, 6 * width)
-    modulation = link.gather(modulation, core_bit, 0).reshape(count, 1, 6 * width)
+    modulation = cores(modulation)
     parts = [modulation[..., at * width : (at + 1) * width] for at in range(6)]
     shift_attn, scale_attn, gate_attn, shift_mlp, scale_mlp, gate_mlp = parts
 
+    team_qkv = w_qkv.reshape(rows, 3, team, group).transpose(2, 0, 1, 3)
+    team_qkv = link.exchange(team_qkv.reshape(team, rows, 3 * group), team_bits)
+    half_tokens = halves(after(tokens, team_qkv))
+    all_tokens = cores(half_tokens).astype(F32)
+    my_qkv, begun = gather_rest(team_qkv.reshape(seq, 2 * rows, 3 * group))
+    my_qkv = my_qkv.reshape(width, 3 * group)
+    fc2_proj = jnp.concatenate([w_fc2, w_proj], axis=0)[None]
+    fc2_proj, begun = gather_rest(fc2_proj, (begun,))
+    my_fc2 = fc2_proj[0, :, :hidden_rows].reshape(hidden, width)
+    full_proj = fc2_proj[0, :, hidden_rows:]
+    full_proj = link.gather(full_proj, seq_bits, 0)
+    full_proj = link.gather(full_proj, core_bit, 2).reshape(team, group, width)
+    team_fc1 = w_fc1.reshape(rows, seq, rest, 2, hidden_rows).transpose(1, 3, 0, 2, 4)
+    team_fc1 = after(team_fc1.reshape(team, rows, hidden), team_qkv)
+    team_fc1 = link.exchange(team_fc1, team_bits)
+    my_fc1, begun = gather_rest(team_fc1.reshape(seq, 2 * rows, hidden), (begun,))
+    my_fc1 = my_fc1.reshape(width, hidden)
+    all_cotangent = cores(halves(after(cotangent, half_tokens))).astype(F32)
+
     def own(value):
-        return lax.dynamic_slice_in_dim(value, core * latents, latents, 0)
+        return value[:latents]
 
     def own_rows(value):
         return lax.dynamic_slice_in_dim(value, half * local_len, local_len, 1)
 
-    def sum_team(value):
-        value = link.scatter(value.reshape(2, latents, seq_len, width), core_bit, 0)
-        value = value.astype(BF16)
-        return value.astype(F32) + link.send(value, seq_bits).astype(F32)
+    def team_part(left, right):
+        other = dot_rt(left[own_flat:], right).astype(BF16)
+        other = link.send(other, core_bit)
+        total = dot_rt(left[:own_flat], right) + other.astype(F32)
+        return total.reshape(latents, seq_len, width)
 
     def flat(value):
         return value.reshape(count * seq_len, -1)
 
-    h_attn = modulate(all_tokens, shift_attn, scale_attn).astype(BF16)
+    h_attn = flat(modulate(all_tokens, shift_attn, scale_attn).astype(BF16))
     bias_q = lax.dynamic_slice_in_dim(full_query, me * group, group, 0)
     bias_v = lax.dynamic_slice_in_dim(full_value, me * group, group, 0)
     bias_qkv = jnp.concatenate([bias_q, jnp.zeros_like(bias_q), bias_v]).astype(F32)
-    qkv = (dot(flat(h_attn), my_qkv) + bias_qkv).astype(BF16)
+    qkv = (dot(h_attn, my_qkv) + bias_qkv).astype(BF16)
     qkv = qkv.reshape(count, seq_len, 3, heads, HD)
     query, key, value = qkv[:, :, 0], qkv[:, :, 1], qkv[:, :, 2]
     scores = jnp.einsum("lqhd,lkhd->lhqk", query, key, preferred_element_type=F32) * HD ** (-0.5)
@@ -228,15 +266,15 @@
     probs_low = probs.astype(BF16)
     attended = jnp.einsum("lhqk,lkhd->lqhd", probs_low, value, preferred_element_type=F32)
     attended = attended.astype(BF16).reshape(count * seq_len, group)
-    all_attended = link.gather(link.gather(attended, seq_bits, 0), core_bit, 1)
-    all_attended = all_attended.reshape(team, count * seq_len, group)
-    attn = jnp.einsum(
-        "tnd,tde->ne",
-        all_attended,
-        full_proj.reshape(team, group, width),
-        preferred_element_type=F32,
-    )
-    attn = (attn + bias_proj).reshape(count, seq_len, width)
+    near = link.send(attended, core_bit)
+    far = link.send(attended, seq_bits)
+    across = link.send(far, core_bit)
+    attn = bias_proj
+    for step, piece in ((0, attended), (1, near), (2, far), (3, across)):
+        if step % 2:
+            piece = jnp.concatenate([piece[own_flat:], piece[:own_flat]], axis=0)
+        attn = attn + dot(piece, link.pick(full_proj, me ^ step))
+    attn = attn.reshape(count, seq_len, width)
     mid = all_tokens + gate_attn * attn
 
     h_mlp = flat(modulate(mid, shift_mlp, scale_mlp).astype(BF16))
@@ -245,7 +283,9 @@
     activated = activated.astype(BF16)
     grad_branch = flat((gate_mlp * all_cotangent).astype(BF16))
     grad_up = gelu_back(dot_rt(grad_branch, my_fc2))[0].astype(BF16)
-    grad_h_mlp = sum_team(dot_rt(grad_up, my_fc1).reshape(count, seq_len, width))
+    grad_h_mlp = team_part(grad_up, my_fc1).astype(BF16)
+    sent_h_mlp = grad_h_mlp
+    grad_h_mlp = grad_h_mlp.astype(F32) + link.send(grad_h_mlp, seq_bits).astype(F32)
 
     own_tokens = own(all_tokens)
     own_cotangent = own(all_cotangent)
@@ -254,25 +294,10 @@
     grad_mid, grad_shift_mlp, grad_scale_mlp = mlp_back(grad_h_mlp)
     grad_mid = grad_mid + own_cotangent
     grad_gate_attn = jnp.sum(grad_mid * own(attn), axis=1, keepdims=True)
-    grad_attn = (own(gate_attn) * grad_mid).astype(BF16)
-    grad_attn = link.gather(grad_attn, core_bit, 0).reshape(count * seq_len, width)
-
-    grad_fc2 = dot_lt(activated, grad_branch).astype(BF16)
-    grad_fc2 = scatter_rest(grad_fc2.reshape(1, rest, hidden_rows, width))[0]
-    grad_fc1 = dot_lt(h_mlp, grad_up).astype(BF16)
-    grad_fc1 = scatter_rest(grad_fc1.reshape(seq, rest, 2 * rows, hidden)).astype(BF16)
-    grad_fc1 = link.exchange(grad_fc1.reshape(team, rows, hidden), team_bits)
-    grad_fc1 = grad_fc1.reshape(seq, 2, rows, rest, hidden_rows).transpose(2, 0, 3, 1, 4)
-    grad_fc1 = grad_fc1.reshape(rows, -1).astype(F32)
-
-    branch = dot(activated, my_fc2).reshape(2, latents, seq_len, width)
-    branch = link.scatter(branch, core_bit, 0).reshape(latents, seq, local_len, width)
-    branch = link.scatter(branch, seq_bits, 1) + bias_fc2
-    output = (own_rows(own_mid) + own(gate_mlp) * branch).astype(BF16)
-    grad_gate_mlp = jnp.sum(cotangent.astype(F32) * branch, axis=1, keepdims=True)
-    grad_gate_mlp = grad_gate_mlp + link.send(grad_gate_mlp, seq_bits)
-
-    my_proj = lax.dynamic_slice_in_dim(full_proj, me * group, group, 0)
+    own_grad_attn = (own(gate_attn) * grad_mid).astype(BF16)
+    grad_attn = flat(cores(own_grad_attn))
+
+    my_proj = link.pick(full_proj, me)
     grad_heads = dot_rt(grad_attn, my_proj).astype(BF16).reshape(count, seq_len, heads, HD)
     grad_probs = jnp.einsum("lqhd,lkhd->lhqk", grad_heads, value, preferred_element_type=F32)
     row_sums = jnp.sum(grad_probs * probs, axis=-1, keepdims=True)
@@ -289,41 +314,72 @@
     ).astype(BF16)
     grad_qkv = jnp.stack([grad_query, grad_key, grad_value], axis=2)
     grad_qkv = grad_qkv.reshape(count * seq_len, 3 * group)
-    grad_h_attn = sum_team(dot_rt(grad_qkv, my_qkv).reshape(count, seq_len, width))
-    grad_w_qkv = dot_lt(flat(h_attn), grad_qkv).astype(BF16)
+    grad_h_attn = dot_rt(grad_qkv, my_qkv).reshape(count, seq_len, width)
+
+    late = jnp.concatenate(
+        [
+            jnp.sum(grad_h_attn, axis=1),
+            jnp.sum(grad_h_attn * normalize(all_tokens), axis=1),
+        ],
+        axis=-1,
+    )
+    late = late[:latents] + link.send(late[latents:], core_bit)
+    late = late + link.send(late, seq_bits)
+    late = all_rest(late.astype(BF16))
+
+    activated, h_mlp = after((activated, h_mlp), sent_h_mlp)
+    grad_fc2 = dot_lt(activated, grad_branch).astype(BF16)
+    grad_fc2 = scatter_rest(
+        grad_fc2.reshape(1, rest, hidden_rows, width), ((own_grad_attn,), (grad_qkv,))
+    )[0]
+    grad_fc1 = dot_lt(h_mlp, grad_up).astype(BF16)
+    grad_fc1 = scatter_rest(
+        grad_fc1.reshape(seq, rest, 2 * rows, hidden), ((own_grad_attn,), (grad_qkv,))
+    ).astype(BF16)
+    grad_fc1 = link.exchange(grad_fc1.reshape(team, rows, hidden), team_bits)
+    grad_fc1 = grad_fc1.reshape(seq, 2, rows, rest, hidden_rows).transpose(2, 0, 3, 1, 4)
+    grad_fc1 = grad_fc1.reshape(rows, -1).astype(F32)
+
+    branch = dot(activated, my_fc2).reshape(2, latents, seq_len, width)
+    branch = branch[0] + link.send(branch[1].astype(BF16), core_bit).astype(F32)
+    branch = branch.reshape(latents, seq, local_len, width)
+    branch = link.scatter(branch, seq_bits, 1, (own_grad_attn,)) + bias_fc2
+    output = (own_rows(own_mid) + own(gate_mlp) * branch).astype(BF16)
+    grad_gate_mlp = jnp.sum(cotangent.astype(F32) * branch, axis=1, keepdims=True)
+    grad_gate_mlp = grad_gate_mlp + link.send(grad_gate_mlp, seq_bits)
+
+    grad_w_qkv = dot_lt(h_attn, grad_qkv).astype(BF16)
     grad_w_qkv = scatter_rest(grad_w_qkv.reshape(seq, rest, 2 * rows, 3 * group)).astype(BF16)
     grad_w_qkv = link.exchange(grad_w_qkv.reshape(team, rows, 3 * group), team_bits)
     grad_w_qkv = grad_w_qkv.reshape(team, rows, 3, group).transpose(1, 2, 0, 3)
     grad_w_qkv = grad_w_qkv.reshape(rows, -1).astype(F32)
-
     grad_proj = dot_lt(attended, grad_attn).astype(BF16)
     grad_proj = grad_proj.reshape(rest // 2, 2, rows, width).swapaxes(0, 1)
     grad_proj = link.exchange(grad_proj, core_bit).reshape(1, rest, rows, width)
     grad_proj = scatter_rest(grad_proj)[0]
 
-    attn_back = jax.vjp(modulate, own_tokens, own(shift_attn), own(scale_attn))[1]
-    grad_res, grad_shift_attn, grad_scale_attn = attn_back(grad_h_attn)
-    grad_tokens = own_rows(grad_mid + grad_res).astype(BF16)
-
-    grad_mod = jnp.concatenate(
-        [
-            grad_shift_attn,
-            grad_scale_attn,
-            grad_gate_attn,
-            grad_shift_mlp,
-            grad_scale_mlp,
-            grad_gate_mlp,
-        ],
-        axis=-1,
-    ).astype(BF16)
-    grad_mod = gather_rest(grad_mod.reshape(1, latents, 6 * width))[0]
-    grad_mod = link.gather(grad_mod, core_bit, 1).reshape(fsdp * latents, 6 * width)
+    other = link.send(grad_h_attn[latents:].astype(BF16), core_bit)
+    grad_h_attn = grad_h_attn[:latents] + other.astype(F32)
+    grad_h_attn = grad_h_attn.reshape(latents, seq, local_len, width)
+    grad_h_attn = link.scatter(grad_h_attn, seq_bits, 1)
+    attn_back = jax.vjp(
+        modulate, tokens.astype(F32), own(shift_attn), own(scale_attn)
+    )[1]
+    grad_tokens = (own_rows(grad_mid) + attn_back(grad_h_attn)[0]).astype(BF16)
+
+    early = jnp.concatenate(
+        [grad_gate_attn, grad_shift_mlp, grad_scale_mlp, grad_gate_mlp], axis=-1
+    )
+    early = all_rest(early.reshape(latents, 4 * width).astype(BF16))
+    grad_silu = dot_rt(early, w_ada[:, 2 * width :])
+    grad_silu = grad_silu + dot_rt(late, w_ada[:, : 2 * width])
+    grad_silu = grad_silu.reshape(1, fsdp, latents * rows)
+    grad_silu = jnp.broadcast_to(grad_silu, (seq, fsdp, latents * rows)).reshape(shards, -1)
+    grad_mod = jnp.concatenate([late, early], axis=1)
     grad_ada = dot_lt(all_cond, grad_mod)
     own_ada = b_ada.shape[0]
     grad_b_ada = lax.dynamic_slice_in_dim(grad_mod, link.index * own_ada, own_ada, 1)
     grad_b_ada = jnp.sum(grad_b_ada.astype(F32), axis=0)
-    grad_silu = dot_rt(grad_mod, w_ada).reshape(1, fsdp, latents * rows)
-    grad_silu = jnp.broadcast_to(grad_silu, (seq, fsdp, latents * rows)).reshape(shards, -1)
 
     def column_sums(value):
         return jnp.sum(value.astype(F32), axis=0)

time: 299 us -> 317 us (1.060)
  local copies, waits for them, and re-layouts: 43.1 us -> 66.1 us
  waiting for transfers between devices: 107 us -> 87.8 us
  matrix products: 18.2 us -> 28.4 us
  starting transfers between devices: 84 us -> 88.5 us
    ppermute x67 -> x71, waiting for transfers between devices: 96.1 us -> 87.8 us  [send(): lax.ppermute(value, AXES, [(i, i ^ mask) for i in range(self.devices)])]
    dot_general x5 -> x7, matrix products: 5.11 us -> 13 us  [dot_rt(): lax.dot_general(left, right, (((1,), (1,)), ((), ())), preferred_element_...]
    select_n x15 -> x8, other arithmetic: 12.9 us -> 5.78 us  [gather(): return jnp.where(spot == 0, first, second)]
    all_to_all x1, waiting for transfers between devices: 5.59 us -> 0.01 us  [local(): tail = lax.all_to_all(tail, AXES, 0, 0, tiled=True)]
    all_to_all x1, waiting for transfers between devices: 5.5 us -> 0.01 us  [local(): small = lax.all_to_all(small, AXES, 0, 0, tiled=True)]
    another operation x2 -> x12, other arithmetic: 0.83 us -> 5.71 us  [the longest x10 3 us: own_first(): return jnp.stack(arrived, axis)]
    squeeze x13 -> x16, local copies, waits for them, and re-layouts: 3.53 us -> 7.18 us  [pick(): return lax.dynamic_index_in_dim(value, spot, axis, keepdims=False)]
    convert_element_type x3, local copies, waits for them, and re-layouts: 1.75 us -> 5.22 us  [local(): grad_fc1 = grad_fc1.reshape(rows, -1).astype(F32)]
  transfers between devices with their start and end apart: 70 -> 74, of which waited for: 27 -> 24; matrix products, arithmetic and copies ran while one was open for 27% -> 34% of each run, Pallas kernels for 0% -> 0%
where the time goes in v2:
time: 317 us; the launch traced here: 315 us
  starting transfers between devices  88.5 us (28%)
  waiting for transfers between devices  87.8 us (28%)
  local copies, waits for them, and re-layouts  66.1 us (21%)
  other arithmetic  41.7 us (13%)
  matrix products  28.4 us (9%)
    ppermute x71, waiting for transfers between devices, send(): lax.ppermute(value, AXES, [(i, i ^ mask) for i in range(self.devices)])  87.8 us
    ppermute x71, starting transfers between devices, send(): lax.ppermute(value, AXES, [(i, i ^ mask) for i in range(self.devices)])  73 us
    dot_general x7, matrix products, dot_rt(): lax.dot_general(left, right, (((1,), (1,)), ((), ())), preferred_element_...  13 us
    unnamed x156, local copies, waits for them, and re-layouts  9.47 us
    all_to_all x1, starting transfers between devices, local(): small = lax.all_to_all(small, AXES, 0, 0, tiled=True)  7.3 us
    squeeze x16, local copies, waits for them, and re-layouts, pick(): return lax.dynamic_index_in_dim(value, spot, axis, keepdims=False)  7.18 us
  transfers between devices with their start and end apart: 74, of which 24 were waited for; matrix products, arithmetic and copies ran while one was open for 34% of the time, Pallas kernels for 0%

profile of v2, /device:TPU:0, one launch (start us, length us, event | category | flops | bytes accessed | tf_op | source)
XLA Modules:
  0.0 314.7 jit_solution(12363569910907703218)
XLA Ops:
  2.1 3.5 %concatenate.78 = bf16[192]{0:T(256)(128)(2,1)S(1)} concatenate(bf16[24]{0:T(256)(128)(2,1)} %param.19, bf16[24]{0:T(256)(128)(2,1)} %param.20, bf16[24]{0:T(256)(128)(2,1)} %param.22, bf16[24]{0:T(256)(128)(2,1)} %param.26, bf16[96]{0:T(256)(128)(2,1)} %param.24), dimensions={0} | concatenate | bytes 768 | tf_op jit(solution)/shard_map/concatenate | solution.py:196
  6.3 7.3 %all-to-all-start = ((bf16[32,1,216]{2,1,0:T(2,128)(2,1)}), bf16[32,1,216]{2,1,0:T(2,128)(2,1)S(1)}, u32[]{:S(2)}, u32[]{:S(2)}) async-start(bf16[32,1,216]{2,1,0:T(2,128)(2,1)} %copy.131), calls=%async_computation | async-start | bytes 65536 | tf_op jit(solution)/shard_map/all_to_all | solution.py:200
  21.3 1.7 collective-permute-start.1
  24.7 4.7 %all-to-all-start.1 = ((f32[32,1,4608]{2,1,0:T(1,128)}), f32[32,1,4608]{2,1,0:T(1,128)}, u32[]{:S(2)}, u32[]{:S(2)}) async-start(f32[32,1,4608]{2,1,0:T(1,128)} %all_to_all.25), calls=%async_computation.1 | async-start | bytes 1179648 | tf_op jit(solution)/shard_map/all_to_all | solution.py:215
  31.3 3.3 %collective-permute-done.2 = bf16[24,576]{1,0:T(8,128)(2,1)S(1)} collective-permute-done((bf16[24,576]{1,0:T(8,128)(2,1)S(1)}, bf16[24,576]{1,0:T(8,128)(2,1)S(1)}, u32[]{:S(2)}, u32[]{:S(2)}) %collective-permute-start.2) | collective-permute-done | bytes 27680 | tf_op jit(solution)/shard_map/ppermute | solution.py:67
  39.9 3.8 %collective-permute-start.7 = (bf16[2,1,48,576]{3,2,0,1:T(8,128)(2,1)S(1)}, bf16[2,1,48,576]{3,2,0,1:T(8,128)(2,1)S(1)}, u32[]{:S(2)}, u32[]{:S(2)}) collective-permute-start(bf16[2,1,48,576]{3,2,0,1:T(8,128)(2,1)S(1)} %bitcast.500), channel_id=1, source_target_pairs={{0,8},{1,9},{2,10},{3,11},{4,12},{5,13},{6,14},{7,15},{8,0},{9,1},... | collective-permute-start | bytes 331784 | tf_op jit(solution)/shard_map/ppermute | solution.py:67
  44.1 1.7 collective-permute-start.20
  45.9 5.3 %collective-permute-done.20 = bf16[24,768]{1,0:T(8,128)(2,1)S(1)} collective-permute-done((bf16[24,768]{1,0:T(8,128)(2,1)S(1)}, bf16[24,768]{1,0:T(8,128)(2,1)S(1)}, u32[]{:S(2)}, u32[]{:S(2)}) %collective-permute-start.20) | collective-permute-done | bytes 36896 | tf_op jit(solution)/shard_map/ppermute | solution.py:67
  51.1 3.4 %collective-permute-done.21 = bf16[24,768]{1,0:T(8,128)(2,1)S(1)} collective-permute-done((bf16[24,768]{1,0:T(8,128)(2,1)S(1)}, bf16[24,768]{1,0:T(8,128)(2,1)S(1)}, u32[]{:S(2)}, u32[]{:S(2)}) %collective-permute-start.21) | collective-permute-done | bytes 36896 | tf_op jit(solution)/shard_map/ppermute | solution.py:67
  56.0 2.5 collective-permute-start.10
  61.0 4.1 %collective-permute-done.10 = bf16[1,1,120,768]{3,2,1,0:T(8,128)(2,1)S(1)} collective-permute-done((bf16[1,1,120,768]{3,2,1,0:T(8,128)(2,1)S(1)}, bf16[1,1,120,768]{3,2,1,0:T(8,128)(2,1)S(1)}, u32[]{:S(2)}, u32[]{:S(2)}) %collective-permute-start.10) | collective-permute-done | bytes 184352 | tf_op jit(solution)/shard_map/ppermute | solution.py:67
  66.6 7.9 %collective-permute-done.11 = bf16[1,1,120,768]{3,2,1,0:T(8,128)(2,1)S(1)} collective-permute-done((bf16[1,1,120,768]{3,2,1,0:T(8,128)(2,1)S(1)}, bf16[1,1,120,768]{3,2,1,0:T(8,128)(2,1)S(1)}, u32[]{:S(2)}, u32[]{:S(2)}) %collective-permute-start.11) | collective-permute-done | bytes 184352 | tf_op jit(solution)/shard_map/ppermute | solution.py:67
  75.1 3.0 collective-permute-start.22
  79.7 2.6 collective-permute-done.22
  84.3 7.6 %collective-permute-done.23 = bf16[2,1,48,768]{3,2,0,1:T(8,128)(2,1)S(1)} collective-permute-done((bf16[2,1,48,768]{3,2,0,1:T(8,128)(2,1)S(1)}, bf16[2,1,48,768]{3,2,0,1:T(8,128)(2,1)S(1)}, u32[]{:S(2)}, u32[]{:S(2)}) %collective-permute-start.23) | collective-permute-done | bytes 147488 | tf_op jit(solution)/shard_map/ppermute | solution.py:67
  101.2 8.2 %collective-permute-done.25 = bf16[2,4,48,768]{3,2,1,0:T(8,128)(2,1)} collective-permute-done((bf16[2,4,48,768]{3,2,1,0:T(8,128)(2,1)}, bf16[2,4,48,768]{3,2,1,0:T(8,128)(2,1)}, u32[]{:S(2)}, u32[]{:S(2)}) %collective-permute-start.25) | collective-permute-done | bytes 589856 | tf_op jit(solution)/shard_map/ppermute | solution.py:67
  109.4 2.8 maximum_select_fusion.2
  115.7 2.1 reshape.1046
  134.9 3.4 %convert_reduce_fusion.1 = (f32[768]{0:T(1024)}, bf16[512,768]{1,0:T(8,128)(2,1)S(1)}, bf16[512,768]{1,0:T(8,128)(2,1)}) fusion(f32[512,768]{1,0:T(8,128)S(1)} %convolution_add_fusion.1, bf16[512,768]{1,0:T(8,128)(2,1)S(1)} %bitcast.503, bf16[768,768]{1,0:T(8,128)(2,1)S(1)} %bitcast.484), kind=kOutput, calls=%fused_computation.36 | convolution fusion | flops 614989056 | bytes 5114880 | tf_op jit(solution)/shard_map/dot_general | solution.py:37
  147.3 2.0 fusion.38
  152.5 1.7 collective-permute-start.60
  156.3 4.4 %collective-permute-done.30 = bf16[1,256,768]{2,1,0:T(8,128)(2,1)S(1)} collective-permute-done((bf16[1,256,768]{2,1,0:T(8,128)(2,1)S(1)}, bf16[1,256,768]{2,1,0:T(8,128)(2,1)S(1)}, u32[]{:S(2)}, u32[]{:S(2)}) %collective-permute-start.30) | collective-permute-done | bytes 393248 | tf_op jit(solution)/shard_map/ppermute | solution.py:67
  166.2 5.6 %collective-permute-done.31 = bf16[1,128,768]{2,1,0:T(8,128)(2,1)S(1)} collective-permute-done((bf16[1,128,768]{2,1,0:T(8,128)(2,1)S(1)}, bf16[1,128,768]{2,1,0:T(8,128)(2,1)S(1)}, u32[]{:S(2)}, u32[]{:S(2)}) %collective-permute-start.31) | collective-permute-done | bytes 196640 | tf_op jit(solution)/shard_map/ppermute | solution.py:67
  174.4 6.1 %collective-permute-done.67 = bf16[1,4,96,768]{3,2,1,0:T(8,128)(2,1)S(1)} collective-permute-done((bf16[1,4,96,768]{3,2,1,0:T(8,128)(2,1)S(1)}, bf16[1,4,96,768]{3,2,1,0:T(8,128)(2,1)S(1)}, u32[]{:S(2)}, u32[]{:S(2)}) %collective-permute-start.67) | collective-permute-done | bytes 589856 | tf_op jit(solution)/shard_map/ppermute | solution.py:67
  181.6 1.9 dynamic-slice_convert_fusion.4
  184.3 2.3 collective-permute-start.38
  186.6 2.1 collective-permute-start.36
  192.9 2.3 collective-permute-done.39
  195.4 1.7 constant_dynamic-slice_fusion
  203.5 1.7 fusion.74
  207.2 2.1 convolution_convert_fusion.8
  223.0 2.1 collective-permute-start.68
  230.5 1.8 add_bitcast_fusion
  233.9 2.1 collective-permute-done.42
  236.0 1.9 collective-permute-start.45
  237.9 2.6 collective-permute-start.43
  243.8 3.0 collective-permute-done.46
  254.6 1.9 fusion.73
  260.4 3.5 %all-to-all-start.2 = ((f32[32,1,216]{2,1,0:T(1,128)}), f32[32,1,216]{2,1,0:T(1,128)}, u32[]{:S(2)}, u32[]{:S(2)}) async-start(f32[32,1,216]{2,1,0:T(1,128)} %all_to_all.27), calls=%async_computation.2 | async-start | bytes 65536 | tf_op jit(solution)/shard_map/all_to_all | solution.py:401
  267.1 2.0 copy.162
  269.2 2.2 reshape.1070
  276.9 3.8 %collective-permute-done.56 = bf16[1,4,24,768]{3,2,1,0:T(8,128)(2,1)S(1)} collective-permute-done((bf16[1,4,24,768]{3,2,1,0:T(8,128)(2,1)S(1)}, bf16[1,4,24,768]{3,2,1,0:T(8,128)(2,1)S(1)}, u32[]{:S(2)}, u32[]{:S(2)}) %collective-permute-start.56) | collective-permute-done | bytes 147488 | tf_op jit(solution)/shard_map/ppermute | solution.py:67
  281.6 4.2 %collective-permute-start.59 = (bf16[1,1,24,768]{3,2,1,0:T(8,128)(2,1)S(1)}, bf16[1,1,24,768]{3,2,1,0:T(8,128)(2,1)S(1)}, u32[]{:S(2)}, u32[]{:S(2)}) collective-permute-start(bf16[1,1,24,768]{3,2,1,0:T(8,128)(2,1)S(1)} %get-tuple-element.89), channel_id=1, source_target_pairs={{0,12},{1,13},{2,14},{3,15},{4,8},{5,9},{6,10},{7,11},{8,4},{9,5},... | collective-permute-start | bytes 110600 | tf_op jit(solution)/shard_map/ppermute | solution.py:67
  287.8 2.9 collective-permute-done.58
  294.7 2.3 collective-permute-start.49
  298.0 2.2 collective-permute-done.51
  300.2 3.9 %collective-permute-done.50 = bf16[2,1,48,576]{3,2,1,0:T(8,128)(2,1)S(1)} collective-permute-done((bf16[2,1,48,576]{3,2,1,0:T(8,128)(2,1)S(1)}, bf16[2,1,48,576]{3,2,1,0:T(8,128)(2,1)S(1)}, u32[]{:S(2)}, u32[]{:S(2)}) %collective-permute-start.50) | collective-permute-done | bytes 110624 | tf_op jit(solution)/shard_map/ppermute | solution.py:67
  307.5 4.6 %collective-permute-done.34 = bf16[1,128,768]{2,1,0:T(8,128)(2,1)S(1)} collective-permute-done((bf16[1,128,768]{2,1,0:T(8,128)(2,1)S(1)}, bf16[1,128,768]{2,1,0:T(8,128)(2,1)S(1)}, u32[]{:S(2)}, u32[]{:S(2)}) %collective-permute-start.34) | collective-permute-done | bytes 196640 | tf_op jit(solution)/shard_map/ppermute | solution.py:67
  (500 shorter events, 152.7 us)
Async XLA Ops:
  6.3 14.8 %all-to-all-start = ((bf16[32,1,216]{2,1,0:T(2,128)(2,1)}), bf16[32,1,216]{2,1,0:T(2,128)(2,1)S(1)}, u32[]{:S(2)}, u32[]{:S(2)}) async-start(bf16[32,1,216]{2,1,0:T(2,128)(2,1)} %copy.131), calls=%async_computation | async-start | bytes 65536 | tf_op jit(solution)/shard_map/all_to_all | solution.py:200
  21.3 10.0 %collective-permute-start.1 = (bf16[24,576]{1,0:T(8,128)(2,1)S(1)}, bf16[24,576]{1,0:T(8,128)(2,1)S(1)}, u32[]{:S(2)}, u32[]{:S(2)}) collective-permute-start(bf16[24,576]{1,0:T(8,128)(2,1)S(1)} %get-tuple-element.105), channel_id=1, source_target_pairs={{0,16},{1,17},{2,18},{3,19},{4,20},{5,21},{6,22},{7,23},{8,24},{9,... | collective-permute-start | bytes 82952 | tf_op jit(solution)/shard_map/ppermute | solution.py:67
  24.7 74.9 %all-to-all-start.1 = ((f32[32,1,4608]{2,1,0:T(1,128)}), f32[32,1,4608]{2,1,0:T(1,128)}, u32[]{:S(2)}, u32[]{:S(2)}) async-start(f32[32,1,4608]{2,1,0:T(1,128)} %all_to_all.25), calls=%async_computation.1 | async-start | bytes 1179648 | tf_op jit(solution)/shard_map/all_to_all | solution.py:215
  34.6 9.5 %collective-permute-start.19 = (bf16[24,768]{1,0:T(8,128)(2,1)S(1)}, bf16[24,768]{1,0:T(8,128)(2,1)S(1)}, u32[]{:S(2)}, u32[]{:S(2)}) collective-permute-start(bf16[24,768]{1,0:T(8,128)(2,1)S(1)} %dynamic-slice_bitcast_fusion.13), channel_id=1, source_target_pairs={{0,1},{1,0},{2,3},{3,2},{4,5},{5,4},{6,7},{7,6},{8,9},{9,8},{10,11... | collective-permute-start | bytes 110600 | tf_op jit(solution)/shard_map/ppermute | solution.py:67
  38.6 15.9 %collective-permute-start.6 = (bf16[2,1,48,576]{3,2,0,1:T(8,128)(2,1)S(1)}, bf16[2,1,48,576]{3,2,0,1:T(8,128)(2,1)S(1)}, u32[]{:S(2)}, u32[]{:S(2)}) collective-permute-start(bf16[2,1,48,576]{3,2,0,1:T(8,128)(2,1)S(1)} %bitcast.499), channel_id=1, source_target_pairs={{0,4},{1,5},{2,6},{3,7},{4,0},{5,1},{6,2},{7,3},{8,12},{9,13},{10,... | collective-permute-start | bytes 331784 | tf_op jit(solution)/shard_map/ppermute | solution.py:67
  39.9 14.6 %collective-permute-start.7 = (bf16[2,1,48,576]{3,2,0,1:T(8,128)(2,1)S(1)}, bf16[2,1,48,576]{3,2,0,1:T(8,128)(2,1)S(1)}, u32[]{:S(2)}, u32[]{:S(2)}) collective-permute-start(bf16[2,1,48,576]{3,2,0,1:T(8,128)(2,1)S(1)} %bitcast.500), channel_id=1, source_target_pairs={{0,8},{1,9},{2,10},{3,11},{4,12},{5,13},{6,14},{7,15},{8,0},{9,1},... | collective-permute-start | bytes 331784 | tf_op jit(solution)/shard_map/ppermute | solution.py:67
  43.7 10.9 %collective-permute-start.8 = (bf16[2,1,48,576]{3,2,0,1:T(8,128)(2,1)S(1)}, bf16[2,1,48,576]{3,2,0,1:T(8,128)(2,1)S(1)}, u32[]{:S(2)}, u32[]{:S(2)}) collective-permute-start(bf16[2,1,48,576]{3,2,0,1:T(8,128)(2,1)S(1)} %bitcast.501), channel_id=1, source_target_pairs={{0,12},{1,13},{2,14},{3,15},{4,8},{5,9},{6,10},{7,11},{8,4},{9,5},... | collective-permute-start | bytes 331784 | tf_op jit(solution)/shard_map/ppermute | solution.py:67
  43.7 17.2 %collective-permute-start.3 = (bf16[1,128,768]{2,1,0:T(8,128)(2,1)S(1)}, bf16[1,128,768]{2,1,0:T(8,128)(2,1)S(1)}, u32[]{:S(2)}, u32[]{:S(2)}) collective-permute-start(bf16[1,128,768]{2,1,0:T(8,128)(2,1)S(1)} %copy-done.13), channel_id=1, source_target_pairs={{0,16},{1,17},{2,18},{3,19},{4,20},{5,21},{6,22},{7,23},{8,24},{9,... | collective-permute-start | bytes 589832 | tf_op jit(solution)/shard_map/ppermute | solution.py:67
  44.1 7.0 %collective-permute-start.20 = (bf16[24,768]{1,0:T(8,128)(2,1)S(1)}, bf16[24,768]{1,0:T(8,128)(2,1)S(1)}, u32[]{:S(2)}, u32[]{:S(2)}) collective-permute-start(bf16[24,768]{1,0:T(8,128)(2,1)S(1)} %get-tuple-element.99), channel_id=1, source_target_pairs={{0,16},{1,17},{2,18},{3,19},{4,20},{5,21},{6,22},{7,23},{8,24},{9,... | collective-permute-start | bytes 110600 | tf_op jit(solution)/shard_map/ppermute | solution.py:67
  54.6 40.0 %collective-permute-start.9 = (bf16[2,4,48,576]{3,2,1,0:T(8,128)(2,1)S(1)}, bf16[2,4,48,576]{3,2,1,0:T(8,128)(2,1)S(1)}, u32[]{:S(2)}, u32[]{:S(2)}) collective-permute-start(bf16[2,4,48,576]{3,2,1,0:T(8,128)(2,1)S(1)} %bitcast.470), channel_id=1, source_target_pairs={{0,2},{1,3},{2,0},{3,1},{4,6},{5,7},{6,4},{7,5},{8,10},{9,11},{10,... | collective-permute-start | bytes 1327112 | tf_op jit(solution)/shard_map/ppermute | solution.py:67
  56.0 9.1 %collective-permute-start.10 = (bf16[1,1,120,768]{3,2,1,0:T(8,128)(2,1)S(1)}, bf16[1,1,120,768]{3,2,1,0:T(8,128)(2,1)S(1)}, u32[]{:S(2)}, u32[]{:S(2)}) collective-permute-start(bf16[1,1,120,768]{3,2,1,0:T(8,128)(2,1)S(1)} %maximum_bitcast_fusion), channel_id=1, source_target_pairs={{0,4},{1,5},{2,6},{3,7},{4,0},{5,1},{6,2},{7,3},{8,12},{9,13},{10,... | collective-permute-start | bytes 552968 | tf_op jit(solution)/shard_map/ppermute | solution.py:67
  58.4 16.1 %collective-permute-start.11 = (bf16[1,1,120,768]{3,2,1,0:T(8,128)(2,1)S(1)}, bf16[1,1,120,768]{3,2,1,0:T(8,128)(2,1)S(1)}, u32[]{:S(2)}, u32[]{:S(2)}) collective-permute-start(bf16[1,1,120,768]{3,2,1,0:T(8,128)(2,1)S(1)} %maximum_bitcast_fusion), channel_id=1, source_target_pairs={{0,8},{1,9},{2,10},{3,11},{4,12},{5,13},{6,14},{7,15},{8,0},{9,1},... | collective-permute-start | bytes 552968 | tf_op jit(solution)/shard_map/ppermute | solution.py:67
  59.8 14.8 %collective-permute-start.12 = (bf16[1,1,120,768]{3,2,1,0:T(8,128)(2,1)S(1)}, bf16[1,1,120,768]{3,2,1,0:T(8,128)(2,1)S(1)}, u32[]{:S(2)}, u32[]{:S(2)}) collective-permute-start(bf16[1,1,120,768]{3,2,1,0:T(8,128)(2,1)S(1)} %maximum_bitcast_fusion), channel_id=1, source_target_pairs={{0,12},{1,13},{2,14},{3,15},{4,8},{5,9},{6,10},{7,11},{8,4},{9,5},... | collective-permute-start | bytes 552968 | tf_op jit(solution)/shard_map/ppermute | solution.py:67
  61.0 33.9 %collective-permute-start.4 = (bf16[1,256,768]{2,1,0:T(8,128)(2,1)S(1)}, bf16[1,256,768]{2,1,0:T(8,128)(2,1)S(1)}, u32[]{:S(2)}, u32[]{:S(2)}) collective-permute-start(bf16[1,256,768]{2,1,0:T(8,128)(2,1)S(1)} %bitcast.427), channel_id=1, source_target_pairs={{0,1},{1,0},{2,3},{3,2},{4,5},{5,4},{6,7},{7,6},{8,9},{9,8},{10,11... | collective-permute-start | bytes 1179656 | tf_op jit(solution)/shard_map/ppermute | solution.py:67
  65.1 14.5 %collective-permute-start.26 = (bf16[1,128,768]{2,1,0:T(8,128)(2,1)S(1)}, bf16[1,128,768]{2,1,0:T(8,128)(2,1)S(1)}, u32[]{:S(2)}, u32[]{:S(2)}) collective-permute-start(bf16[1,128,768]{2,1,0:T(8,128)(2,1)S(1)} %copy-done.36), channel_id=1, source_target_pairs={{0,16},{1,17},{2,18},{3,19},{4,20},{5,21},{6,22},{7,23},{8,24},{9,... | collective-permute-start | bytes 589832 | tf_op jit(solution)/shard_map/ppermute | solution.py:67
  74.6 21.1 %collective-permute-start.13 = (bf16[1,4,120,768]{3,2,1,0:T(8,128)(2,1)S(1)}, bf16[1,4,120,768]{3,2,1,0:T(8,128)(2,1)S(1)}, u32[]{:S(2)}, u32[]{:S(2)}) collective-permute-start(bf16[1,4,120,768]{3,2,1,0:T(8,128)(2,1)S(1)} %bitcast.463), channel_id=1, source_target_pairs={{0,2},{1,3},{2,0},{3,1},{4,6},{5,7},{6,4},{7,5},{8,10},{9,11},{10,... | collective-permute-start | bytes 2211848 | tf_op jit(solution)/shard_map/ppermute | solution.py:67
  75.1 7.2 %collective-permute-start.22 = (bf16[2,1,48,768]{3,2,0,1:T(8,128)(2,1)S(1)}, bf16[2,1,48,768]{3,2,0,1:T(8,128)(2,1)S(1)}, u32[]{:S(2)}, u32[]{:S(2)}) collective-permute-start(bf16[2,1,48,768]{3,2,0,1:T(8,128)(2,1)S(1)} %bitcast.493), channel_id=1, source_target_pairs={{0,4},{1,5},{2,6},{3,7},{4,0},{5,1},{6,2},{7,3},{8,12},{9,13},{10,... | collective-permute-start | bytes 442376 | tf_op jit(solution)/shard_map/ppermute | solution.py:67
  79.6 12.4 %collective-permute-start.23 = (bf16[2,1,48,768]{3,2,0,1:T(8,128)(2,1)S(1)}, bf16[2,1,48,768]{3,2,0,1:T(8,128)(2,1)S(1)}, u32[]{:S(2)}, u32[]{:S(2)}) collective-permute-start(bf16[2,1,48,768]{3,2,0,1:T(8,128)(2,1)S(1)} %bitcast.495), channel_id=1, source_target_pairs={{0,8},{1,9},{2,10},{3,11},{4,12},{5,13},{6,14},{7,15},{8,0},{9,1},... | collective-permute-start | bytes 442376 | tf_op jit(solution)/shard_map/ppermute | solution.py:67
  82.3 10.3 %collective-permute-start.24 = (bf16[2,1,48,768]{3,2,0,1:T(8,128)(2,1)S(1)}, bf16[2,1,48,768]{3,2,0,1:T(8,128)(2,1)S(1)}, u32[]{:S(2)}, u32[]{:S(2)}) collective-permute-start(bf16[2,1,48,768]{3,2,0,1:T(8,128)(2,1)S(1)} %bitcast.496), channel_id=1, source_target_pairs={{0,12},{1,13},{2,14},{3,15},{4,8},{5,9},{6,10},{7,11},{8,4},{9,5},... | collective-permute-start | bytes 442376 | tf_op jit(solution)/shard_map/ppermute | solution.py:67
  93.3 16.1 %collective-permute-start.25 = (bf16[2,4,48,768]{3,2,1,0:T(8,128)(2,1)}, bf16[2,4,48,768]{3,2,1,0:T(8,128)(2,1)}, u32[]{:S(2)}, u32[]{:S(2)}) collective-permute-start(bf16[2,4,48,768]{3,2,1,0:T(8,128)(2,1)} %bitcast.78), channel_id=1, source_target_pairs={{0,2},{1,3},{2,0},{3,1},{4,6},{5,7},{6,4},{7,5},{8,10},{9,11},{10,... | collective-permute-start | bytes 1769480 | tf_op jit(solution)/shard_map/ppermute | solution.py:67
  98.5 25.1 %collective-permute-start.14 = (bf16[8,24,768]{2,1,0:T(8,128)(2,1)}, bf16[8,24,768]{2,1,0:T(8,128)(2,1)}, u32[]{:S(2)}, u32[]{:S(2)}) collective-permute-start(bf16[8,24,768]{2,1,0:T(8,128)(2,1)} %get-tuple-element.68), channel_id=1, source_target_pairs={{0,16},{1,17},{2,18},{3,19},{4,20},{5,21},{6,22},{7,23},{8,24},{9,... | collective-permute-start | bytes 884744 | tf_op jit(solution)/shard_map/ppermute | solution.py:67
  101.1 11.1 %collective-permute-start.5 = (f32[1,1,4608]{2,1,0:T(1,128)S(1)}, f32[1,1,4608]{2,1,0:T(1,128)S(1)}, u32[]{:S(2)}, u32[]{:S(2)}) collective-permute-start(f32[1,1,4608]{2,1,0:T(1,128)S(1)} %reshape.1041), channel_id=1, source_target_pairs={{0,1},{1,0},{2,3},{3,2},{4,5},{5,4},{6,7},{7,6},{8,9},{9,8},{10,11... | collective-permute-start | bytes 55304 | tf_op jit(solution)/shard_map/ppermute | solution.py:67
  120.3 6.6 %collective-permute-start.17 = (bf16[512,192]{0,1:T(8,128)(2,1)S(1)}, bf16[512,192]{0,1:T(8,128)(2,1)S(1)}, u32[]{:S(2)}, u32[]{:S(2)}) collective-permute-start(bf16[512,192]{0,1:T(8,128)(2,1)S(1)} %bitcast.474), channel_id=1, source_target_pairs={{0,16},{1,17},{2,18},{3,19},{4,20},{5,21},{6,22},{7,23},{8,24},{9,... | collective-permute-start | bytes 589832 | tf_op jit(solution)/shard_map/ppermute | solution.py:67
  139.6 7.7 %collective-permute-start.28 = (bf16[256,768]{1,0:T(8,128)(2,1)}, bf16[256,768]{1,0:T(8,128)(2,1)}, u32[]{:S(2)}, u32[]{:S(2)}) collective-permute-start(bf16[256,768]{1,0:T(8,128)(2,1)} %convolution_convert_fusion.5), channel_id=1, source_target_pairs={{0,1},{1,0},{2,3},{3,2},{4,5},{5,4},{6,7},{7,6},{8,9},{9,8},{10,11... | collective-permute-start | bytes 1179656 | tf_op jit(solution)/shard_map/ppermute | solution.py:67
  149.2 11.5 %collective-permute-start.30 = (bf16[1,256,768]{2,1,0:T(8,128)(2,1)S(1)}, bf16[1,256,768]{2,1,0:T(8,128)(2,1)S(1)}, u32[]{:S(2)}, u32[]{:S(2)}) collective-permute-start(bf16[1,256,768]{2,1,0:T(8,128)(2,1)S(1)} %fusion.38), channel_id=1, source_target_pairs={{0,16},{1,17},{2,18},{3,19},{4,20},{5,21},{6,22},{7,23},{8,24},{9,... | collective-permute-start | bytes 1179656 | tf_op jit(solution)/shard_map/ppermute | solution.py:67
  152.5 21.1 %collective-permute-start.60 = (bf16[2,4,48,768]{3,2,1,0:T(8,128)(2,1)S(1)}, bf16[2,4,48,768]{3,2,1,0:T(8,128)(2,1)S(1)}, u32[]{:S(2)}, u32[]{:S(2)}) collective-permute-start(bf16[2,4,48,768]{3,2,1,0:T(8,128)(2,1)S(1)} %get-tuple-element.79), channel_id=1, source_target_pairs={{0,2},{1,3},{2,0},{3,1},{4,6},{5,7},{6,4},{7,5},{8,10},{9,11},{10,... | collective-permute-start | bytes 1769480 | tf_op jit(solution)/shard_map/ppermute | solution.py:67
  155.1 25.4 %collective-permute-start.67 = (bf16[1,4,96,768]{3,2,1,0:T(8,128)(2,1)S(1)}, bf16[1,4,96,768]{3,2,1,0:T(8,128)(2,1)S(1)}, u32[]{:S(2)}, u32[]{:S(2)}) collective-permute-start(bf16[1,4,96,768]{3,2,1,0:T(8,128)(2,1)S(1)} %get-tuple-element.74), channel_id=1, source_target_pairs={{0,2},{1,3},{2,0},{3,1},{4,6},{5,7},{6,4},{7,5},{8,10},{9,11},{10,... | collective-permute-start | bytes 1769480 | tf_op jit(solution)/shard_map/ppermute | solution.py:67
  164.4 40.8 %collective-permute-start.32 = (bf16[1,256,768]{2,1,0:T(8,128)(2,1)}, bf16[1,256,768]{2,1,0:T(8,128)(2,1)S(1)}, u32[]{:S(2)}, u32[]{:S(2)}) collective-permute-start(bf16[1,256,768]{2,1,0:T(8,128)(2,1)} %multiply_convert_fusion.2), channel_id=1, source_target_pairs={{0,1},{1,0},{2,3},{3,2},{4,5},{5,4},{6,7},{7,6},{8,9},{9,8},{10,11... | collective-permute-start | bytes 1179656 | tf_op jit(solution)/shard_map/ppermute | solution.py:67
  164.5 7.4 %collective-permute-start.31 = (bf16[1,128,768]{2,1,0:T(8,128)(2,1)S(1)}, bf16[1,128,768]{2,1,0:T(8,128)(2,1)S(1)}, u32[]{:S(2)}, u32[]{:S(2)}) collective-permute-start(bf16[1,128,768]{2,1,0:T(8,128)(2,1)S(1)} %fusion.62), channel_id=1, source_target_pairs={{0,16},{1,17},{2,18},{3,19},{4,20},{5,21},{6,22},{7,23},{8,24},{9,... | collective-permute-start | bytes 589832 | tf_op jit(solution)/shard_map/ppermute | solution.py:67
  172.7 11.6 %collective-permute-start.35 = (f32[1,1,768]{2,0,1:T(1,128)S(1)}, f32[1,1,768]{2,0,1:T(1,128)S(1)}, u32[]{:S(2)}, u32[]{:S(2)}) collective-permute-start(f32[1,1,768]{2,0,1:T(1,128)S(1)} %broadcast_in_dim.249), channel_id=1, source_target_pairs={{0,16},{1,17},{2,18},{3,19},{4,20},{5,21},{6,22},{7,23},{8,24},{9,... | collective-permute-start | bytes 9224 | tf_op jit(solution)/shard_map/ppermute | solution.py:67
  197.1 25.9 %collective-permute-start.63 = (bf16[2,1,48,768]{3,2,1,0:T(8,128)(2,1)}, bf16[2,1,48,768]{3,2,1,0:T(8,128)(2,1)}, u32[]{:S(2)}, u32[]{:S(2)}) collective-permute-start(bf16[2,1,48,768]{3,2,1,0:T(8,128)(2,1)} %get-tuple-element.76), channel_id=1, source_target_pairs={{0,12},{1,13},{2,14},{3,15},{4,8},{5,9},{6,10},{7,11},{8,4},{9,5},... | collective-permute-start | bytes 442376 | tf_op jit(solution)/shard_map/ppermute | solution.py:67
  198.7 26.5 %collective-permute-start.62 = (bf16[2,1,48,768]{3,2,1,0:T(8,128)(2,1)}, bf16[2,1,48,768]{3,2,1,0:T(8,128)(2,1)}, u32[]{:S(2)}, u32[]{:S(2)}) collective-permute-start(bf16[2,1,48,768]{3,2,1,0:T(8,128)(2,1)} %get-tuple-element.77), channel_id=1, source_target_pairs={{0,8},{1,9},{2,10},{3,11},{4,12},{5,13},{6,14},{7,15},{8,0},{9,1},... | collective-permute-start | bytes 442376 | tf_op jit(solution)/shard_map/ppermute | solution.py:67
  199.8 25.4 %collective-permute-start.61 = (bf16[2,1,48,768]{3,2,1,0:T(8,128)(2,1)}, bf16[2,1,48,768]{3,2,1,0:T(8,128)(2,1)}, u32[]{:S(2)}, u32[]{:S(2)}) collective-permute-start(bf16[2,1,48,768]{3,2,1,0:T(8,128)(2,1)} %get-tuple-element.75), channel_id=1, source_target_pairs={{0,4},{1,5},{2,6},{3,7},{4,0},{5,1},{6,2},{7,3},{8,12},{9,13},{10,... | collective-permute-start | bytes 442376 | tf_op jit(solution)/shard_map/ppermute | solution.py:67
  201.5 27.5 %collective-permute-start.70 = (bf16[1,1,96,768]{3,2,1,0:T(8,128)(2,1)}, bf16[1,1,96,768]{3,2,1,0:T(8,128)(2,1)}, u32[]{:S(2)}, u32[]{:S(2)}) collective-permute-start(bf16[1,1,96,768]{3,2,1,0:T(8,128)(2,1)} %get-tuple-element.71), channel_id=1, source_target_pairs={{0,12},{1,13},{2,14},{3,15},{4,8},{5,9},{6,10},{7,11},{8,4},{9,5},... | collective-permute-start | bytes 442376 | tf_op jit(solution)/shard_map/ppermute | solution.py:67
  205.3 25.2 %collective-permute-start.69 = (bf16[1,1,96,768]{3,2,1,0:T(8,128)(2,1)}, bf16[1,1,96,768]{3,2,1,0:T(8,128)(2,1)}, u32[]{:S(2)}, u32[]{:S(2)}) collective-permute-start(bf16[1,1,96,768]{3,2,1,0:T(8,128)(2,1)} %get-tuple-element.72), channel_id=1, source_target_pairs={{0,8},{1,9},{2,10},{3,11},{4,12},{5,13},{6,14},{7,15},{8,0},{9,1},... | collective-permute-start | bytes 442376 | tf_op jit(solution)/shard_map/ppermute | solution.py:67
  223.0 7.5 %collective-permute-start.68 = (bf16[1,1,96,768]{3,2,1,0:T(8,128)(2,1)}, bf16[1,1,96,768]{3,2,1,0:T(8,128)(2,1)S(1)}, u32[]{:S(2)}, u32[]{:S(2)}) collective-permute-start(bf16[1,1,96,768]{3,2,1,0:T(8,128)(2,1)} %get-tuple-element.70), channel_id=1, source_target_pairs={{0,4},{1,5},{2,6},{3,7},{4,0},{5,1},{6,2},{7,3},{8,12},{9,13},{10,... | collective-permute-start | bytes 442376 | tf_op jit(solution)/shard_map/ppermute | solution.py:67
  225.2 71.8 %collective-permute-start.33 = (bf16[1,256,768]{2,1,0:T(8,128)(2,1)}, bf16[1,256,768]{2,1,0:T(8,128)(2,1)}, u32[]{:S(2)}, u32[]{:S(2)}) collective-permute-start(bf16[1,256,768]{2,1,0:T(8,128)(2,1)} %fusion.40), channel_id=1, source_target_pairs={{0,1},{1,0},{2,3},{3,2},{4,5},{5,4},{6,7},{7,6},{8,9},{9,8},{10,11... | collective-permute-start | bytes 1179656 | tf_op jit(solution)/shard_map/ppermute | solution.py:67
  225.2 7.1 %collective-permute-start.41 = (f32[1,1536]{1,0:T(1,128)S(1)}, f32[1,1536]{1,0:T(1,128)S(1)}, u32[]{:S(2)}, u32[]{:S(2)}) collective-permute-start(f32[1,1536]{1,0:T(1,128)S(1)} %pad_maximum_fusion.11), channel_id=1, source_target_pairs={{0,1},{1,0},{2,3},{3,2},{4,5},{5,4},{6,7},{7,6},{8,9},{9,8},{10,11... | collective-permute-start | bytes 18440 | tf_op jit(solution)/shard_map/ppermute | solution.py:67
  229.1 62.3 %collective-permute-start.48 = (bf16[2,4,48,576]{3,2,1,0:T(8,128)(2,1)}, bf16[2,4,48,576]{3,2,1,0:T(8,128)(2,1)}, u32[]{:S(2)}, u32[]{:S(2)}) collective-permute-start(bf16[2,4,48,576]{3,2,1,0:T(8,128)(2,1)} %dynamic-slice_bitcast_fusion.4), channel_id=1, source_target_pairs={{0,2},{1,3},{2,0},{3,1},{4,6},{5,7},{6,4},{7,5},{8,10},{9,11},{10,... | collective-permute-start | bytes 1327112 | tf_op jit(solution)/shard_map/ppermute | solution.py:67
  242.5 29.8 %collective-permute-start.55 = (bf16[4,24,768]{2,1,0:T(8,128)(2,1)}, bf16[4,24,768]{2,1,0:T(8,128)(2,1)}, u32[]{:S(2)}, u32[]{:S(2)}) collective-permute-start(bf16[4,24,768]{2,1,0:T(8,128)(2,1)} %dynamic-slice_bitcast_fusion.7), channel_id=1, source_target_pairs={{0,1},{1,0},{2,3},{3,2},{4,5},{5,4},{6,7},{7,6},{8,9},{9,8},{10,11... | collective-permute-start | bytes 442376 | tf_op jit(solution)/shard_map/ppermute | solution.py:67
  248.9 15.7 %collective-permute-start.65 = (bf16[24,768]{1,0:T(8,128)(2,1)}, bf16[24,768]{1,0:T(8,128)(2,1)}, u32[]{:S(2)}, u32[]{:S(2)}) collective-permute-start(bf16[24,768]{1,0:T(8,128)(2,1)} %get-tuple-element.96), channel_id=1, source_target_pairs={{0,16},{1,17},{2,18},{3,19},{4,20},{5,21},{6,22},{7,23},{8,24},{9,... | collective-permute-start | bytes 110600 | tf_op jit(solution)/shard_map/ppermute | solution.py:67
  249.7 15.7 %collective-permute-start.66 = (bf16[24,768]{1,0:T(8,128)(2,1)}, bf16[24,768]{1,0:T(8,128)(2,1)}, u32[]{:S(2)}, u32[]{:S(2)}) collective-permute-start(bf16[24,768]{1,0:T(8,128)(2,1)} %get-tuple-element.95), channel_id=1, source_target_pairs={{0,17},{1,16},{2,19},{3,18},{4,21},{5,20},{6,23},{7,22},{8,25},{9,... | collective-permute-start | bytes 110600 | tf_op jit(solution)/shard_map/ppermute | solution.py:67
  260.4 11.0 %all-to-all-start.2 = ((f32[32,1,216]{2,1,0:T(1,128)}), f32[32,1,216]{2,1,0:T(1,128)}, u32[]{:S(2)}, u32[]{:S(2)}) async-start(f32[32,1,216]{2,1,0:T(1,128)} %all_to_all.27), calls=%async_computation.2 | async-start | bytes 65536 | tf_op jit(solution)/shard_map/all_to_all | solution.py:401
  292.5 7.7 %collective-permute-start.51 = (bf16[2,1,48,576]{3,2,1,0:T(8,128)(2,1)S(1)}, bf16[2,1,48,576]{3,2,1,0:T(8,128)(2,1)S(1)}, u32[]{:S(2)}, u32[]{:S(2)}) collective-permute-start(bf16[2,1,48,576]{3,2,1,0:T(8,128)(2,1)S(1)} %get-tuple-element.81), channel_id=1, source_target_pairs={{0,12},{1,13},{2,14},{3,15},{4,8},{5,9},{6,10},{7,11},{8,4},{9,5},... | collective-permute-start | bytes 331784 | tf_op jit(solution)/shard_map/ppermute | solution.py:67
  294.0 10.0 %collective-permute-start.50 = (bf16[2,1,48,576]{3,2,1,0:T(8,128)(2,1)S(1)}, bf16[2,1,48,576]{3,2,1,0:T(8,128)(2,1)S(1)}, u32[]{:S(2)}, u32[]{:S(2)}) collective-permute-start(bf16[2,1,48,576]{3,2,1,0:T(8,128)(2,1)S(1)} %get-tuple-element.82), channel_id=1, source_target_pairs={{0,8},{1,9},{2,10},{3,11},{4,12},{5,13},{6,14},{7,15},{8,0},{9,1},... | collective-permute-start | bytes 331784 | tf_op jit(solution)/shard_map/ppermute | solution.py:67
  294.7 9.4 %collective-permute-start.49 = (bf16[2,1,48,576]{3,2,1,0:T(8,128)(2,1)S(1)}, bf16[2,1,48,576]{3,2,1,0:T(8,128)(2,1)S(1)}, u32[]{:S(2)}, u32[]{:S(2)}) collective-permute-start(bf16[2,1,48,576]{3,2,1,0:T(8,128)(2,1)S(1)} %get-tuple-element.80), channel_id=1, source_target_pairs={{0,4},{1,5},{2,6},{3,7},{4,0},{5,1},{6,2},{7,3},{8,12},{9,13},{10,... | collective-permute-start | bytes 331784 | tf_op jit(solution)/shard_map/ppermute | solution.py:67
  304.3 7.8 %collective-permute-start.34 = (bf16[1,128,768]{2,1,0:T(8,128)(2,1)S(1)}, bf16[1,128,768]{2,1,0:T(8,128)(2,1)S(1)}, u32[]{:S(2)}, u32[]{:S(2)}) collective-permute-start(bf16[1,128,768]{2,1,0:T(8,128)(2,1)S(1)} %fusion.63), channel_id=1, source_target_pairs={{0,16},{1,17},{2,18},{3,19},{4,20},{5,21},{6,22},{7,23},{8,24},{9,... | collective-permute-start | bytes 589832 | tf_op jit(solution)/shard_map/ppermute | solution.py:67
  305.9 7.5 %collective-permute-start.53 = (bf16[24,576]{1,0:T(8,128)(2,1)S(1)}, bf16[24,576]{1,0:T(8,128)(2,1)S(1)}, u32[]{:S(2)}, u32[]{:S(2)}) collective-permute-start(bf16[24,576]{1,0:T(8,128)(2,1)S(1)} %get-tuple-element.102), channel_id=1, source_target_pairs={{0,16},{1,17},{2,18},{3,19},{4,20},{5,21},{6,22},{7,23},{8,24},{9,... | collective-permute-start | bytes 82952 | tf_op jit(solution)/shard_map/ppermute | solution.py:67
  (101 other events, 569.9 us)

commit v3 on v1

v3 whole, which is shorter than its diff:
```python
import math

import jax
import jax.numpy as jnp
from jax import lax
from jax.experimental import pallas as pl
from jax.experimental.pallas import tpu as pltpu
from jax.sharding import PartitionSpec as P

HD = 64
AXES = ("seq", "fsdp")
F32 = jnp.float32
BF16 = jnp.bfloat16
VMEM_SPEC = pl.BlockSpec(memory_space=pltpu.VMEM)
SMEM_SPEC = pl.BlockSpec(memory_space=pltpu.SMEM)


def contract(left, right, left_dim, right_dim):
    return lax.dot_general(
        left, right, (((left_dim,), (right_dim,)), ((), ())), preferred_element_type=F32
    )


def dot(left, right):
    return contract(left, right, 1, 0)


def dot_rt(left, right):
    return contract(left, right, 1, 1)


def dot_lt(left, right):
    return contract(left, right, 0, 0)


def norm_parts(value):
    centre = value - jnp.mean(value, axis=-1, keepdims=True)
    variance = jnp.mean(centre * centre, axis=-1, keepdims=True)
    scale = lax.rsqrt(variance + 1e-06)
    return centre * scale, scale


def norm_back(norm, rate, grad):
    inner = jnp.mean(grad * norm, axis=-1, keepdims=True)
    return rate * (grad - jnp.mean(grad, axis=-1, keepdims=True) - norm * inner)


def after(value, *earlier):
    return lax.optimization_barrier((value,) + earlier)[0]


class Links:
    def __init__(self, devices):
        self.devices = devices
        self.index = lax.axis_index(AXES)

    def place(self, bits):
        spot = jnp.int32(0)
        for bit in bits:
            spot = spot * 2 + ((self.index >> bit) & 1)
        return spot

    def mask(self, bits, step):
        total = 0
        for at, bit in enumerate(reversed(bits)):
            total |= ((step >> at) & 1) << bit
        return total

    def groups(self, bits):
        steps = [self.mask(bits, step) for step in range(1 << len(bits))]
        return [
            [base | step for step in steps] for base in range(self.devices) if not base & steps[-1]
        ]

    def send(self, value, bits, step=1):
        mask = self.mask(bits, step)
        return lax.ppermute(value, AXES, [(i, i ^ mask) for i in range(self.devices)])

    def all_to_all(self, value, bits):
        return lax.all_to_all(
            value, AXES, 0, 0, tiled=True, axis_index_groups=self.groups(bits)
        )

    def flip(self, value, bits):
        shape = value.shape
        value = value.reshape((2,) * len(bits) + shape[1:])
        for axis, bit in enumerate(bits):
            first, second = jnp.split(value, 2, axis)
            turned = jnp.concatenate([second, first], axis)
            value = jnp.where(self.place([bit]) == 0, value, turned)
        return value.reshape(shape)

    def gather_step(self, value, bit, earlier=()):
        part = self.send(value, [bit])
        if earlier:
            value = after(value, *earlier)
        return jnp.concatenate([value, part], 0)

    def exchange(self, value, bits):
        value = self.flip(value, bits)
        parts = [value[:1]]
        for step in range(1, 1 << len(bits)):
            parts.append(self.send(value[step : step + 1], bits, step))
        return self.flip(jnp.concatenate(parts, 0), bits)

    def exchange_pieces(self, value, bits):
        spot = self.place(bits)
        parts = [self.pick(value, spot)]
        for step in range(1, 1 << len(bits)):
            parts.append(self.send(self.pick(value, spot ^ step), bits, step))
        return parts

    def gather(self, value, bits, axis):
        spot = self.place(bits)
        part = self.send(value, bits)
        shape = value.shape[:axis] + (2,) + value.shape[axis:]
        out = jnp.zeros(shape, value.dtype)
        out = lax.dynamic_update_index_in_dim(out, value, spot, axis)
        return lax.dynamic_update_index_in_dim(out, part, 1 - spot, axis)

    def pick(self, value, spot, axis=0):
        return lax.dynamic_index_in_dim(value, spot, axis, keepdims=False)

    def scatter(self, value, bits, earlier=()):
        spot = self.place(bits)
        arrived = []
        for step in range(1, 1 << len(bits)):
            arrived.append(self.send(self.pick(value, spot ^ step).astype(BF16), bits, step))
        total = self.pick(value, spot)
        if earlier:
            total = after(total, *earlier)
        total = total.astype(F32)
        for part in arrived:
            total = total + part.astype(F32)
        return total


def call(kernel, outs, *args, scalars=0, scratch=(), us=5):
    arrays = [jnp.reshape(arg, 1) for arg in args[:scalars]] + list(args[scalars:])
    return pl.pallas_call(
        kernel,
        out_shape=[jax.ShapeDtypeStruct(shape, dtype) for shape, dtype in outs],
        in_specs=[SMEM_SPEC] * scalars + [VMEM_SPEC] * (len(args) - scalars),
        out_specs=[VMEM_SPEC] * len(outs),
        scratch_shapes=[pltpu.VMEM(shape, dtype) for shape, dtype in scratch],
        compiler_params=pltpu.CompilerParams(vmem_limit_bytes=48 * 2**20),
        cost_estimate=pl.CostEstimate(
            flops=us * 10**9, bytes_accessed=us * 3 * 10**6, transcendentals=0
        ),
    )(*arrays)


def step_order(count):
    order = [0]
    while count > 1:
        count //= 2
        order = order + [at ^ count for at in order]
    return order


def interleave(own_ref, other_ref, out_ref, pair, high, swap=False):
    outer, inner, rows, cols = own_ref.shape
    for first, away in enumerate(step_order(outer)):
        to = jnp.bitwise_xor(high, away)
        for second in range(inner):
            out_ref[second, to, pair] = own_ref[first, second]
            piece = other_ref[first, second]
            if swap:
                piece = jnp.concatenate([piece[:, cols // 2 :], piece[:, : cols // 2]], axis=1)
            out_ref[second, to, 1 - pair] = piece


def interleave_call(own, other, pair, high):
    outer, inner, rows, cols = own.shape

    def kernel(pair_ref, high_ref, own_ref, other_ref, out_ref):
        interleave(own_ref, other_ref, out_ref, pair_ref[0], high_ref[0])

    shape = (inner, outer, 2, rows, cols)
    return call(kernel, [(shape, own.dtype)], pair, high, own, other, scalars=2, us=2)[0]


def attend(core, pair, high, mine, there, own_x, other_x, own_w, other_w, bias):
    latents, seq_len, width = own_x.shape[1:]
    count = 2 * latents
    columns = own_w.shape[3]
    group = columns // 3
    total = count * seq_len

    def kernel(
        core_ref, pair_ref, high_ref, mine_ref, there_ref, own_ref, other_ref, own_w_ref,
        other_w_ref, b_ref, mod_ref, h_ref, qkv_ref, out_ref, w_out_ref, w_ref,
    ):
        interleave(own_w_ref, other_w_ref, w_ref, pair_ref[0], high_ref[0])
        weight = w_ref[...].reshape(width, columns)
        w_out_ref[...] = weight
        core_at = core_ref[0]
        for side in range(2):
            row = jnp.bitwise_xor(core_at, side)
            for latent in range(latents):
                one, two = mine_ref[row, latent], there_ref[row, latent]
                first = jnp.where(core_at == 0, one, two)
                second = jnp.where(core_at == 0, two, one)
                mod_ref[side * latents + latent, 0:3] = first
                mod_ref[side * latents + latent, 3:6] = second
        for at in range(count):
            where = slice(at * seq_len, (at + 1) * seq_len)
            x = own_ref[0, at] if at < latents else other_ref[0, at - latents]
            norm = norm_parts(x.astype(F32))[0]
            shift, scale = mod_ref[at, 0:1], mod_ref[at, 1:2]
            h_low = (norm * (1.0 + scale) + shift).astype(BF16)
            h_ref[where] = h_low
            qkv = (dot(h_low, weight) + b_ref[...]).astype(BF16)
            qkv_ref[where] = qkv
            pieces = []
            for head in range(group // HD):
                query, key, value = (
                    qkv[:, part * group + head * HD : part * group + (head + 1) * HD]
                    for part in range(3)
                )
                probs = softmax(query, key).astype(BF16)
                pieces.append(dot(probs, value).astype(BF16))
            out_ref[where] = jnp.concatenate(pieces, axis=1)

    outs = [
        ((count, 6, width), F32),
        ((total, width), BF16),
        ((total, columns), BF16),
        ((total, group), BF16),
        ((width, columns), BF16),
    ]
    placed = (own_w.shape[1], own_w.shape[0], 2) + own_w.shape[2:]
    return call(
        kernel, outs, core, pair, high, mine, there, own_x, other_x, own_w, other_w, bias,
        scalars=3, scratch=[(placed, BF16)], us=6,
    )


def softmax(query, key):
    scores = dot_rt(query, key) * HD ** (-0.5)
    top = jnp.max(scores, axis=-1, keepdims=True)
    log_total = top + jnp.log(jnp.sum(jnp.exp(scores - top), axis=-1, keepdims=True))
    return jnp.exp(scores - log_total)


def feed(me, pair, high, pieces, proj, biases, own_x, other_x, mod, own_1, other_1, own_2, other_2):
    latents, seq_len, width = own_x.shape[1:]
    count = 2 * latents
    total = count * seq_len
    members = len(pieces)
    outer, seq, block, hidden = own_1.shape
    front = hidden // 2
    hidden_rows = hidden // (2 * outer)

    def kernel(me_ref, pair_ref, high_ref, *refs):
        piece_refs, refs = refs[:members], refs[members:]
        (
            proj_ref, bias_ref, own_ref, other_ref, mod_ref, own_1_ref, other_1_ref, own_2_ref,
            other_2_ref, attn_ref, mid_ref, h_own_ref, h_other_ref, keep_1_ref, send_1_ref,
            keep_2_ref, send_2_ref, out_own_ref, out_other_ref, gate_ref, sums_ref,
            fc1_ref, fc2_ref, h_ref, act_ref, up_ref, branch_ref, whole_ref,
        ) = refs
        interleave(own_1_ref, other_1_ref, fc1_ref, pair_ref[0], high_ref[0], swap=True)
        for at, away in enumerate(step_order(outer)):
            to = jnp.bitwise_xor(high_ref[0], away)
            fc2_ref[0, to] = own_2_ref[at, :hidden_rows]
            fc2_ref[1, to] = other_2_ref[at, :hidden_rows]
        fc1 = fc1_ref[...].reshape(width, hidden)
        fc2 = fc2_ref[...].reshape(hidden, width)
        sums_up, sums_branch = 0.0, 0.0
        for at in range(count):
            where = slice(at * seq_len, (at + 1) * seq_len)
            near = at % latents
            lane = slice(near * seq_len, (near + 1) * seq_len)
            away = (at + latents) % count
            away = slice(away * seq_len, (away + 1) * seq_len)
            x_ref = own_ref if at < latents else other_ref
            x, cotangent = x_ref[0, near].astype(F32), x_ref[1, near].astype(F32)
            mods = [mod_ref[at, part : part + 1] for part in range(6)]
            attn = bias_ref[0:1, :width]
            for step, piece_ref in enumerate(piece_refs):
                piece = piece_ref[away if step % 2 else where]
                attn = attn + dot(piece, proj_ref[jnp.bitwise_xor(me_ref[0], step)])
            mid = x + mods[2] * attn
            if at < latents:
                attn_ref[where] = attn
                mid_ref[where] = mid
            h_low = (norm_parts(mid)[0] * (1.0 + mods[4]) + mods[3]).astype(BF16)
            h_ref[where] = h_low
            up = dot(h_low, fc1) + bias_ref[1:2, :hidden]
            square = up * up
            bend = jnp.tanh(0.7978845608028654 * up * (1.0 + 0.044715 * square))
            act = (0.5 * up * (1.0 + bend)).astype(BF16)
            act_ref[where] = act
            slope = 0.7978845608028654 * (1.0 + 0.134145 * square)
            slope = 0.5 * (1.0 + bend) + 0.5 * up * (1.0 - bend * bend) * slope
            grad_branch = (mods[5] * cotangent).astype(BF16)
            branch_ref[where] = grad_branch
            grad_up = (slope * dot_rt(grad_branch, fc2)).astype(BF16)
            up_ref[where] = grad_up
            grad_h = dot_rt(grad_up, fc1)
            out = dot(act, fc2) + bias_ref[2:3, :width]
            gate_ref[at] = jnp.sum(cotangent * out, axis=0, keepdims=True)
            if at < latents:
                h_own_ref[lane] = grad_h
                out_own_ref[lane] = out
            else:
                h_other_ref[lane] = grad_h.astype(BF16)
                out_other_ref[lane] = out.astype(BF16)
            sums_branch = sums_branch + jnp.sum(
                grad_branch.astype(F32), axis=0, keepdims=True
            )
            sums_up = sums_up + jnp.sum(grad_up.astype(F32), axis=0, keepdims=True)
        sums_ref[0:1, :width] = sums_branch
        sums_ref[1:2, :hidden] = sums_up
        grad_2 = dot_lt(act_ref[...], branch_ref[...]).astype(BF16)
        keep_2_ref[...] = grad_2[:front]
        send_2_ref[...] = grad_2[front:]
        whole_ref[...] = dot_lt(h_ref[...], up_ref[...]).astype(BF16).reshape(whole_ref.shape)
        for first in range(seq):
            for second in range(outer):
                lane = slice(first * block, (first + 1) * block)
                at = first * outer + second
                keep_1_ref[second, lane] = whole_ref[at, pair_ref[0]]
                piece = whole_ref[at, 1 - pair_ref[0]]
                send_1_ref[second, lane] = jnp.concatenate(
                    [piece[:, front:], piece[:, :front]], axis=1
                )

    own_total = latents * seq_len
    wide = max(width, hidden)
    outs = [
        ((own_total, width), F32),
        ((own_total, width), F32),
        ((own_total, width), F32),
        ((own_total, width), BF16),
        ((outer, seq * block, hidden), BF16),
        ((outer, seq * block, hidden), BF16),
        ((front, width), BF16),
        ((front, width), BF16),
        ((own_total, width), F32),
        ((own_total, width), BF16),
        ((count, 1, width), F32),
        ((2, wide), F32),
    ]
    scratch = [
        ((seq, outer, 2, block, hidden), BF16),
        ((2, outer, hidden_rows, width), BF16),
        ((total, width), BF16),
        ((total, hidden), BF16),
        ((total, hidden), BF16),
        ((total, width), BF16),
        ((seq * outer, 2, block, hidden), BF16),
    ]
    args = pieces + [proj, biases, own_x, other_x, mod, own_1, other_1, own_2, other_2]
    return call(kernel, outs, me, pair, high, *args, scalars=3, scratch=scratch, us=12)


def norm_backward(mine, there, mid, attn, own_x, mod):
    latents, seq_len, width = own_x.shape[1:]

    def kernel(
        mine_ref, there_ref, mid_ref, attn_ref, x_ref, mod_ref, grad_ref, low_ref, sums_ref
    ):
        for at in range(latents):
            where = slice(at * seq_len, (at + 1) * seq_len)
            grad_h = mine_ref[where].astype(F32) + there_ref[where].astype(F32)
            norm, rate = norm_parts(mid_ref[where])
            grad = x_ref[1, at].astype(F32) + norm_back(
                norm, rate, grad_h * (1.0 + mod_ref[at, 4:5])
            )
            grad_ref[where] = grad
            low_ref[where] = (mod_ref[at, 2:3] * grad).astype(BF16)
            sums_ref[at, 0:1] = jnp.sum(grad * attn_ref[where], axis=0, keepdims=True)
            sums_ref[at, 1:2] = jnp.sum(grad_h, axis=0, keepdims=True)
            sums_ref[at, 2:3] = jnp.sum(grad_h * norm, axis=0, keepdims=True)

    outs = [
        ((latents * seq_len, width), F32),
        ((latents * seq_len, width), BF16),
        ((latents, 3, width), F32),
    ]
    return call(kernel, outs, mine, there, mid, attn, own_x, mod, us=3)


def attend_back(
    me, core, pair, own_grad, other_grad, proj, qkv, attended, near, h_low, weight, own_x, other_x,
    blocks,
):
    latents, seq_len, width = own_x.shape[1:]
    count = 2 * latents
    total, columns = qkv.shape
    group = columns // 3
    seq, high, block = blocks
    rows = block // 2
    third = rows // 3
    size = seq * block
    scale = HD ** (-0.5)

    def kernel(
        me_ref, core_ref, pair_ref, own_ref, other_ref, proj_ref, qkv_ref, att_ref, near_ref,
        h_ref, w_ref, own_x_ref, other_x_ref, keep_ref, send_ref, h_own_ref, h_other_ref,
        sums_ref, cols_ref, grads_ref, whole_ref, rows_ref,
    ):
        proj_rows = proj_ref[me_ref[0]]
        grad_mine, grad_near = 0.0, 0.0
        for at in range(count):
            where = slice(at * seq_len, (at + 1) * seq_len)
            away = (at + latents) % count
            away = slice(away * seq_len, (away + 1) * seq_len)
            lane = at % latents
            x = own_x_ref[0, lane] if at < latents else other_x_ref[0, lane]
            lane = slice(lane * seq_len, (lane + 1) * seq_len)
            grad_attn = own_ref[lane] if at < latents else other_ref[lane]
            grad_mine = grad_mine + dot_lt(att_ref[where], grad_attn)
            grad_near = grad_near + dot_lt(near_ref[away], grad_attn)
            grad_out = dot_rt(grad_attn, proj_rows).astype(BF16)
            pieces = [[], [], []]
            for head in range(group // HD):
                query, key, value = (
                    qkv_ref[where, part * group + head * HD : part * group + (head + 1) * HD]
                    for part in range(3)
                )
                grad_head = grad_out[:, head * HD : (head + 1) * HD]
                probs = softmax(query, key)
                grad_probs = dot_rt(grad_head, value)
                inner = jnp.sum(grad_probs * probs, axis=-1, keepdims=True)
                grad_scores = (probs * (grad_probs - inner)).astype(BF16)
                pieces[0].append((dot(grad_scores, key) * scale).astype(BF16))
                pieces[1].append((dot_lt(grad_scores, query) * scale).astype(BF16))
                pieces[2].append(dot_lt(probs.astype(BF16), grad_head).astype(BF16))
            grad_qkv = jnp.concatenate(sum(pieces, []), axis=1)
            grads_ref[where] = grad_qkv
            grad_h = dot_rt(grad_qkv, w_ref[...])
            norm = norm_parts(x.astype(F32))[0]
            sums_ref[at, 0:1] = jnp.sum(grad_h, axis=0, keepdims=True)
            sums_ref[at, 1:2] = jnp.sum(grad_h * norm, axis=0, keepdims=True)
            if at < latents:
                h_own_ref[lane] = grad_h
            else:
                h_other_ref[lane] = grad_h.astype(BF16)
        cols_ref[...] = jnp.sum(grads_ref[...].astype(F32), axis=0, keepdims=True)
        whole = dot_lt(h_ref[...], grads_ref[...]).astype(BF16)
        whole_ref[...] = whole.reshape(whole_ref.shape)
        half_rows = (high,) + rows_ref.shape[1:]
        rows_ref[pl.ds(core_ref[0] * high, high)] = grad_mine.reshape(half_rows)
        rows_ref[pl.ds((1 - core_ref[0]) * high, high)] = grad_near.reshape(half_rows)
        for to, out_ref in ((pair_ref[0], keep_ref), (1 - pair_ref[0], send_ref)):
            for second in range(high):
                for first in range(seq):
                    lane = slice(first * block, (first + 1) * block)
                    out_ref[second, lane] = whole_ref[first * high + second, to]
                piece = rows_ref[second * 2 + to, core_ref[0]].astype(BF16)
                out_ref[second, size : size + rows] = piece[:, :columns]
                out_ref[second, size + rows :] = jnp.concatenate(
                    [piece[at * third : (at + 1) * third, columns:] for at in range(3)], axis=1
                )

    own_total = latents * seq_len
    outs = [
        ((high, size + rows + third, columns), BF16),
        ((high, size + rows + third, columns), BF16),
        ((own_total, width), F32),
        ((own_total, width), BF16),
        ((count, 2, width), F32),
        ((1, columns), F32),
    ]
    scratch = [
        ((total, columns), BF16),
        ((seq * high, 2, block, columns), BF16),
        ((2 * high, 2, rows, width), F32),
    ]
    return call(
        kernel, outs, me, core, pair, own_grad, other_grad, proj, qkv, attended, near, h_low,
        weight, own_x, other_x, scalars=3, scratch=scratch, us=12,
    )


def join_fc1(me, pair, pieces, high):
    rows, hidden = pieces[0].shape
    wide = hidden // (2 * high)
    team = len(pieces)

    def kernel(me_ref, pair_ref, *refs):
        ins, out_ref, held_ref = refs[:team], refs[team], refs[team + 1]
        for step, piece_ref in enumerate(ins):
            piece = piece_ref[...].astype(F32)
            turned = jnp.concatenate([piece[:, hidden // 2 :], piece[:, : hidden // 2]], axis=1)
            held_ref[jnp.bitwise_xor(me_ref[0], step)] = jnp.where(
                pair_ref[0] == 0, piece, turned
            )
        out = []
        for first in range(team // 2):
            for second in range(high):
                for side in range(2):
                    at = (side * high + second) * wide
                    for core in range(2):
                        out.append(held_ref[first * 2 + core][:, at : at + wide])
        out_ref[...] = jnp.concatenate(out, axis=1)

    outs = [((rows, team * hidden), F32)]
    return call(
        kernel, outs, me, pair, *pieces, scalars=2, scratch=[((team, rows, hidden), F32)], us=2
    )[0]


def join_qkv(me, pieces):
    rows, columns = pieces[0].shape
    group = columns // 3
    team = len(pieces)

    def kernel(me_ref, *refs):
        ins, out_ref, held_ref = refs[:team], refs[team], refs[team + 1]
        for step, piece_ref in enumerate(ins):
            held_ref[jnp.bitwise_xor(me_ref[0], step)] = piece_ref[...].astype(F32)
        out = [
            held_ref[member][:, part * group : (part + 1) * group]
            for part in range(3)
            for member in range(team)
        ]
        out_ref[...] = jnp.concatenate(out, axis=1)

    outs = [((rows, team * columns), F32)]
    return call(
        kernel, outs, me, *pieces, scalars=1, scratch=[((team, rows, columns), F32)], us=2
    )[0]


def local(
    shards,
    split,
    tokens,
    cond,
    w_ada,
    b_ada,
    w_qkv,
    b_query,
    b_value,
    w_proj,
    b_proj,
    w_fc1,
    b_fc1,
    w_fc2,
    b_fc2,
    cotangent,
):
    seq, fsdp = split
    link = Links(shards)
    low_bits = int(math.log2(fsdp))
    core_bit = [0]
    seq_bits = list(range(low_bits, int(math.log2(shards))))[::-1]
    pair_bit, high_bits = [1], list(range(2, low_bits))[::-1]
    team_bits = seq_bits + core_bit
    team = seq * 2
    rest = fsdp // 2
    high = rest // 2
    core, half, me = link.place(core_bit), link.place(seq_bits), link.place(team_bits)
    pair, spot = link.place(pair_bit), link.place(high_bits)
    latents, local_len, width = tokens.shape
    seq_len = seq * local_len
    rows = w_qkv.shape[0]
    hidden_rows = w_fc2.shape[0]
    hidden = hidden_rows * rest
    group = width // team
    columns = 3 * group
    count = 2 * latents
    chips = shards // 2

    direct = [jnp.concatenate([w_fc2, w_proj], axis=0)[None]]
    for bit in high_bits:
        direct.append(link.gather_step(direct[-1], bit))

    cond_float = cond.astype(F32)
    silu_cond = jax.nn.silu(cond_float).astype(BF16)
    mine = latents * rows
    cond_blocks = silu_cond.reshape(latents, seq, fsdp, rows)
    cond_blocks = link.pick(cond_blocks, half, 1).swapaxes(0, 1).reshape(fsdp, mine)
    small = 4 * rows + hidden_rows
    bias_row = sum(
        jnp.pad(bias[None], ((0, 0), (start, mine + small - start - bias.shape[0])))
        for start, bias in (
            (mine, b_query), (mine + rows, b_value), (mine + 2 * rows, b_proj),
            (mine + 3 * rows, b_fc2), (mine + 4 * rows, b_fc1),
        )
    )
    to_all = jnp.pad(cond_blocks, ((0, 0), (0, small))) + bias_row
    from_all = lax.all_to_all(to_all, "fsdp", 0, 0, tiled=True)
    all_cond = from_all[:, :mine].reshape(fsdp * latents, rows)
    biases = from_all[:, mine:]
    bias_q, bias_v = (
        lax.dynamic_slice_in_dim(
            biases[:, at * rows : (at + 1) * rows].reshape(1, -1), core * group, group, 1
        ).astype(F32)
        for at in range(2)
    )
    bias_qkv = jnp.concatenate([bias_q, jnp.zeros_like(bias_q), bias_v], axis=1)
    bias_fc1 = biases[:, 4 * rows :].reshape(high, 2, 2, hidden_rows)
    bias_fc1 = link.flip(link.pick(bias_fc1, core, 2).swapaxes(0, 1), pair_bit)
    bias_fc1 = bias_fc1.reshape(1, hidden).astype(F32)

    acts = jnp.stack([tokens, cotangent]).reshape(-1, 1, local_len, width)
    acts = interleave_call(acts, link.send(acts, seq_bits), half, jnp.int32(0))
    acts = acts.reshape(2, latents, seq_len, width)
    team_qkv = w_qkv.reshape(rows, 3, team, group).transpose(2, 0, 1, 3)
    team_fc1 = w_fc1.reshape(rows, seq, high, 2, 2, hidden_rows).transpose(3, 2, 1, 4, 0, 5)
    team_fc1 = link.flip(team_fc1, pair_bit).transpose(2, 3, 4, 0, 1, 5)
    team_part = jnp.concatenate(
        [team_qkv.reshape(team, rows, columns), team_fc1.reshape(team, rows, hidden)], axis=2
    )
    team_part = link.exchange(after(team_part, from_all), team_bits)
    part = dot(all_cond, w_ada)
    own_columns = (jnp.arange(shards) == link.index)[:, None] * b_ada.astype(F32)[None, :]
    part = after(part + own_columns.reshape(-1), acts, team_part, direct[1])
    part = part.reshape(fsdp * latents, 2, 3 * width)
    part = link.pick(part, core, 1) + link.send(link.pick(part, 1 - core, 1), core_bit)
    part = part.reshape(1, rest, count * 3 * width)
    part = jnp.broadcast_to(part, (seq, rest, count * 3 * width)).reshape(chips, -1)
    sent_part = part
    part = link.all_to_all(part, seq_bits + [*high_bits, *pair_bit])

    team_qkv = team_part[:, :, :columns].reshape(1, seq, 2 * rows, columns)
    team_fc1 = team_part[:, :, columns:].reshape(1, seq, 2 * rows, hidden)
    direct_own = direct[-1]
    direct_other = link.send(direct_own, pair_bit)
    steps = [team_qkv]
    for bit in high_bits:
        ready = (direct_own,) if bit == high_bits[0] else (part,)
        steps.append(link.gather_step(steps[-1], bit, ready))
    qkv_own = steps[-1]
    qkv_other = link.send(qkv_own, pair_bit)
    other_acts = link.send(acts, core_bit)
    fc1_steps = [after(team_fc1, steps[1])]
    for bit in high_bits:
        fc1_steps.append(link.gather_step(fc1_steps[-1], bit, (qkv_own,)))
    fc1_own = fc1_steps[-1]
    fc1_other = link.send(fc1_own, pair_bit)
    part = after(part, fc1_steps[1], other_acts)
    modulation = jnp.sum(part, axis=0).reshape(2, latents, 3, width)
    full_proj = interleave_call(
        direct_own[:, None, hidden_rows:], direct_other[:, None, hidden_rows:], pair, spot
    )
    half_proj = full_proj
    full_proj = link.gather(full_proj.reshape(rest, rows, width), seq_bits, 0)
    full_proj = link.gather(full_proj, core_bit, 2).reshape(team, group, width)
    bias_out = link.gather(after(biases, sent_part)[:, 2 * rows : 4 * rows], seq_bits, 0)
    bias_proj, bias_fc2 = (
        bias_out[:, :, at * rows : (at + 1) * rows].reshape(1, width).astype(F32) for at in range(2)
    )
    wide = max(width, hidden)
    feed_biases = jnp.concatenate(
        [
            jnp.pad(bias, ((0, 0), (0, wide - bias.shape[1])))
            for bias in (bias_proj, bias_fc1, bias_fc2 * (1.0 / team))
        ],
        axis=0,
    )

    mod, h_attn, qkv, attended, my_qkv = attend(
        core, pair, spot, modulation, link.send(modulation, core_bit), acts, other_acts,
        after(qkv_own, half_proj, fc1_own),
        qkv_other, bias_qkv,
    )

    near = link.send(attended, core_bit)
    far = link.send(attended, seq_bits)
    across = link.send(far, core_bit)
    (
        attn, mid, grad_h, other_h, keep_fc1, send_fc1, keep_fc2, send_fc2, branch, other_branch,
        grad_gate_mlp, sums_mlp,
    ) = feed(
        me, pair, spot, [attended, near, far, across], full_proj, feed_biases, acts, other_acts,
        mod, fc1_own, fc1_other, direct_own, direct_other,
    )
    grad_h = (grad_h + link.send(other_h, core_bit).astype(F32)).astype(BF16)
    there_h = link.send(grad_h, seq_bits)
    sent_fc2 = link.send(send_fc2, pair_bit)
    sent_fc1 = link.send(send_fc1, pair_bit)
    sent_branch = link.send(other_branch, core_bit)
    grad_mid, grad_attn, sums_mid = norm_backward(grad_h, there_h, mid, attn, acts, mod)
    other_attn = link.send(grad_attn, core_bit)
    grad_fc2 = after(keep_fc2, grad_attn).astype(F32) + sent_fc2.astype(F32)
    grad_fc2 = grad_fc2.astype(BF16).reshape(high, hidden_rows, width)
    keep_qkv, send_qkv, grad_h_attn, other_h_attn, sums_attn, sums_qkv = attend_back(
        me, core, pair, after(grad_attn, grad_fc2), other_attn, full_proj, qkv, attended, near,
        h_attn, my_qkv, acts, other_acts, (seq, high, 2 * rows),
    )

    late = jnp.concatenate([sums_attn, grad_gate_mlp], axis=1)
    late = late[:latents] + link.send(late[latents:], core_bit)
    grad_fc2 = link.scatter(grad_fc2, high_bits)
    late = after(late, grad_fc2)
    late = late + link.send(late, seq_bits)
    grad_mod = jnp.concatenate([late[:, :2], sums_mid, late[:, 2:]], axis=1)
    grad_mod = grad_mod.reshape(1, -1, 128).astype(BF16)
    grad_mod = jnp.broadcast_to(grad_mod, (fsdp,) + grad_mod.shape[1:])
    sent_mod = grad_mod
    grad_mod = lax.all_to_all(grad_mod, "fsdp", 0, 0, tiled=True)
    grad_mod = grad_mod.reshape(fsdp * latents, 6 * width)

    sent_qkv = link.send(send_qkv, pair_bit)
    grad_silu = dot_rt(after(grad_mod, sent_qkv), w_ada).reshape(1, fsdp, mine)
    grad_silu = jnp.broadcast_to(grad_silu, (seq, fsdp, mine)).reshape(shards, -1)
    grad_ada = dot_lt(all_cond, grad_mod)
    own_ada = b_ada.shape[0]
    grad_b_ada = lax.dynamic_slice_in_dim(grad_mod, link.index * own_ada, own_ada, 1)
    grad_b_ada = jnp.sum(grad_b_ada.astype(F32), axis=0)
    everyone = 1.0 / team
    sums_proj = jnp.sum(grad_attn.astype(F32), axis=0) * (1.0 / seq)
    sums_branch, sums_up = sums_mlp[0, :width] * everyone, sums_mlp[1, :hidden]
    sums_proj, sums_branch, sums_up, sums_qkv = after(
        (sums_proj, sums_branch, sums_up, sums_qkv), sent_mod
    )
    in_team = (jnp.arange(team) == me)[:, None]
    by_owner = [sums_branch.reshape(shards, rows), sums_proj.reshape(shards, rows)]
    for sums in (sums_qkv[:, :group], sums_qkv[:, 2 * group :]):
        by_owner.append(jnp.where(in_team, sums, 0.0).reshape(shards, rows))
    sums_up = link.flip(sums_up.reshape(2, high, hidden_rows), pair_bit).swapaxes(0, 1)
    sums_up = sums_up.reshape(1, rest, 1, hidden_rows)
    in_seq = jnp.arange(seq).reshape(seq, 1, 1, 1) == half
    in_core = jnp.arange(2).reshape(1, 1, 2, 1) == core
    by_owner.append(jnp.where(in_seq & in_core, sums_up, 0.0).reshape(shards, hidden_rows))
    tail = jnp.concatenate([grad_silu] + by_owner, axis=1)
    sent_tail = tail
    tail = lax.all_to_all(tail, AXES, 0, 0, tiled=True)
    grad_fc1 = after(keep_fc1, late).astype(F32) + sent_fc1.astype(F32)
    grad_fc1 = link.scatter(grad_fc1.astype(BF16), high_bits, (sent_tail,)).astype(BF16)
    grad_fc1 = link.exchange_pieces(grad_fc1.reshape(team, rows, hidden), team_bits)
    grad_fc1 = join_fc1(me, pair, grad_fc1, high)
    grad_qkv = after(keep_qkv, sent_mod).astype(F32) + sent_qkv.astype(F32)
    grad_qkv = link.scatter(grad_qkv.astype(BF16), high_bits, (sent_tail,))
    size = team * rows
    grad_proj = grad_qkv[size : size + rows]
    last = grad_qkv[size + rows :].reshape(rows // 3, 3, group).swapaxes(0, 1)
    grad_proj = jnp.concatenate([grad_proj, last.reshape(rows, group)], axis=1)
    grad_qkv = grad_qkv[:size].astype(BF16).reshape(team, rows, columns)
    grad_qkv = join_qkv(me, link.exchange_pieces(grad_qkv, team_bits))

    def own_rows(value):
        value = value.reshape(latents, seq_len, -1)
        return lax.dynamic_slice_in_dim(value, half * local_len, local_len, 1)

    branch = after(branch, other_attn) + sent_branch.astype(F32)
    grad_h_attn = after(grad_h_attn, sent_mod) + link.send(other_h_attn, core_bit).astype(F32)
    both = jnp.stack([branch, grad_h_attn]).reshape(2, latents, seq, local_len, width)
    both = link.scatter(jnp.moveaxis(both, 2, 0), seq_bits, (sent_tail,))
    output = (own_rows(mid) + mod[:latents, 5:6] * both[0]).astype(BF16)
    norm, rate = norm_parts(tokens.astype(F32))
    grad_tokens = norm_back(norm, rate, both[1] * (1.0 + mod[:latents, 1:2]))
    grad_tokens = (own_rows(grad_mid) + grad_tokens).astype(BF16)

    grad_silu = tail[:, :mine].reshape(shards, latents, rows).swapaxes(0, 1)
    grad_silu = grad_silu.reshape(latents, width)
    silu_back = jax.vjp(jax.nn.silu, cond_float)[1]
    grad_cond = silu_back(grad_silu)[0].astype(BF16)
    sums = jnp.sum(tail[:, mine:], axis=0)
    return (
        output,
        grad_tokens,
        grad_cond,
        grad_ada,
        grad_b_ada,
        grad_qkv,
        sums[2 * rows : 3 * rows],
        sums[3 * rows : 4 * rows],
        grad_proj,
        sums[rows : 2 * rows],
        grad_fc1,
        sums[4 * rows :],
        grad_fc2,
        sums[:rows],
    )


def solution(mesh):
    seq, fsdp = mesh.shape["seq"], mesh.shape["fsdp"]
    act = P("fsdp", "seq", None)
    matrix = P(AXES, None)
    vector = P(AXES)
    cond = P("fsdp", None)
    in_specs = (
        act, cond, matrix, vector, matrix, vector, vector, matrix, vector, matrix, vector, matrix,
        vector, act,
    )
    out_specs = (
        act, act, cond, matrix, vector, matrix, vector, vector, matrix, vector, matrix, vector,
        matrix, vector,
    )

    def layer(*args):
        return local(seq * fsdp, (seq, fsdp), *args)

    return jax.shard_map(layer, mesh=mesh, in_specs=in_specs, out_specs=out_specs, check_vma=False)
```

time: 299 us -> 209 us (0.70)
  waiting for transfers between devices: 107 us -> 69.8 us
  Pallas kernels: 0 us -> 25.4 us
  other arithmetic: 43.3 us -> 19.9 us
  local copies, waits for them, and re-layouts: 43.1 us -> 20.8 us
  matrix products: 18.2 us -> 1.36 us
  starting transfers between devices: 84 us -> 67.6 us
    ppermute x67 -> x48, waiting for transfers between devices: 96.1 us -> 63.3 us  [send(): lax.ppermute(value, AXES, [(i, i ^ mask) for i in range(self.devices)])]
    pallas_call x0 -> x8, Pallas kernels: none -> 25.4 us  [call(): pl.pallas_call(kernel, out_shape=[jax.ShapeDtypeStruct(shape, dtype) for...]
    ppermute x67 -> x48, starting transfers between devices: 70.8 us -> 52 us  [send(): lax.ppermute(value, AXES, [(i, i ^ mask) for i in range(self.devices)])]
    dot_general x21 -> x3, matrix products: 18.2 us -> 1.36 us  [contract(): lax.dot_general(left, right, (((left_dim,), (right_dim,)), ((), ())), pre...]
    select_n x16 -> x3, other arithmetic: 13.6 us -> 0.3 us  [the longest x2 0.22 us: flip(): value = jnp.where(self.place([bit]) == 0, value, turned)]
    reduce_sum x18 -> x5, other arithmetic: 10.6 us -> 0.64 us  [the longest x1 0.21 us: norm_back(): return rate * (grad - jnp.mean(grad, axis=-1, keepdims=True) - norm * inner)]
    convert_element_type x19 -> x3, local copies, waits for them, and re-layouts: 8.95 us -> 0.19 us  [the longest x1 0.09 us: local(): bias_out[:, :, at * rows:(at + 1) * rows].reshape(1, width).astype(F32)]
    unnamed x146 -> x65, local copies, waits for them, and re-layouts: 10.6 us -> 4.81 us
  transfers between devices with their start and end apart: 70 -> 52, of which waited for: 27 -> 20; matrix products, arithmetic and copies ran while one was open for 27% -> 15% of each run, Pallas kernels for 0% -> 7%
where the time goes in v3:
time: 209 us; the launch traced here: 207 us
  waiting for transfers between devices  69.8 us (33%)
  starting transfers between devices  67.6 us (32%)
  Pallas kernels  25.4 us (12%)
  local copies, waits for them, and re-layouts  20.8 us (10%)
  other arithmetic  19.9 us (10%)
    ppermute x48, waiting for transfers between devices, send(): lax.ppermute(value, AXES, [(i, i ^ mask) for i in range(self.devices)])  63.3 us
    ppermute x48, starting transfers between devices, send(): lax.ppermute(value, AXES, [(i, i ^ mask) for i in range(self.devices)])  52 us
    pallas_call x8, Pallas kernels, call(): pl.pallas_call(kernel, out_shape=[jax.ShapeDtypeStruct(shape, dtype) for...  25.4 us
    unnamed x65, local copies, waits for them, and re-layouts  4.81 us
  transfers between devices with their start and end apart: 52, of which 20 were waited for; matrix products, arithmetic and copies ran while one was open for 15% of the time, Pallas kernels for 7%

profile of v3, /device:TPU:0, one launch (start us, length us, event | category | flops | bytes accessed | tf_op | source)
XLA Modules:
  0.0 206.6 jit_solution(17443859129381552230)
XLA Ops:
  1.7 4.1 %collective-permute-start.4 = (bf16[1,120,768]{2,1,0:T(8,128)(2,1)S(1)}, bf16[1,120,768]{2,1,0:T(8,128)(2,1)S(1)}, u32[]{:S(2)}, u32[]{:S(2)}) collective-permute-start(bf16[1,120,768]{2,1,0:T(8,128)(2,1)S(1)} %maximum_bitcast_fusion), channel_id=1, source_target_pairs={{0,8},{1,9},{2,10},{3,11},{4,12},{5,13},{6,14},{7,15},{8,0},{9,1},... | collective-permute-start | bytes 552968 | tf_op jit(solution)/shard_map/ppermute | solution.py:77
  8.1 3.9 %all-to-all-start = ((bf16[16,1,216]{2,1,0:T(2,128)(2,1)}), bf16[16,1,216]{2,1,0:T(2,128)(2,1)S(1)}, u32[]{:S(2)}, u32[]{:S(2)}) async-start(bf16[16,1,216]{2,1,0:T(2,128)(2,1)} %copy.74), calls=%async_computation | async-start | bytes 32768 | tf_op jit(solution)/shard_map/all_to_all | solution.py:587
  13.1 1.6 collective-permute-start
  16.6 1.9 all-to-all-done
  19.1 1.6 collective-permute-start.2
  22.0 4.1 %collective-permute-done.20 = bf16[16,48]{1,0:T(8,128)(2,1)S(1)} collective-permute-done((bf16[16,48]{1,0:T(8,128)(2,1)S(1)}, bf16[16,48]{1,0:T(8,128)(2,1)S(1)}, u32[]{:S(2)}, u32[]{:S(2)}) %collective-permute-start.20) | collective-permute-done | bytes 1568 | tf_op jit(solution)/shard_map/ppermute | solution.py:77
  27.0 3.6 %collective-permute-done.3 = bf16[1,24,1344]{2,1,0:T(8,128)(2,1)S(1)} collective-permute-done((bf16[1,24,1344]{2,1,0:T(8,128)(2,1)S(1)}, bf16[1,24,1344]{2,1,0:T(8,128)(2,1)S(1)}, u32[]{:S(2)}, u32[]{:S(2)}) %collective-permute-start.3) | collective-permute-done | bytes 64544 | tf_op jit(solution)/shard_map/ppermute | solution.py:77
  32.9 2.6 %collective-permute-start.7 = (bf16[1,2,48,576]{3,2,1,0:T(8,128)(2,1)S(1)}, bf16[1,2,48,576]{3,2,1,0:T(8,128)(2,1)S(1)}, u32[]{:S(2)}, u32[]{:S(2)}) collective-permute-start(bf16[1,2,48,576]{3,2,1,0:T(8,128)(2,1)S(1)} %bitcast.221), channel_id=1, source_target_pairs={{0,8},{1,9},{2,10},{3,11},{4,12},{5,13},{6,14},{7,15},{8,0},{9,1},... | collective-permute-start | bytes 331784 | tf_op jit(solution)/shard_map/ppermute | solution.py:77
  35.6 1.5 collective-permute-start.6
  38.2 3.7 %all-to-all-start.1 = ((f32[16,1,4608]{2,1,0:T(1,128)}), f32[16,1,4608]{2,1,0:T(1,128)S(1)}, u32[]{:S(2)}, u32[]{:S(2)}) async-start(f32[16,1,4608]{2,1,0:T(1,128)} %all_to_all.30), calls=%async_computation.1 | async-start | bytes 589824 | tf_op jit(solution)/shard_map/all_to_all | solution.py:80
  41.9 8.6 %collective-permute-done.6 = bf16[2,120,768]{2,1,0:T(8,128)(2,1)S(1)} collective-permute-done((bf16[2,120,768]{2,1,0:T(8,128)(2,1)S(1)}, bf16[2,120,768]{2,1,0:T(8,128)(2,1)S(1)}, u32[]{:S(2)}, u32[]{:S(2)}) %collective-permute-start.6) | collective-permute-done | bytes 368672 | tf_op jit(solution)/shard_map/ppermute | solution.py:77
  50.7 1.7 collective-permute-start.12
  52.5 3.5 %collective-permute-start.9 = (bf16[1,2,48,768]{3,2,1,0:T(8,128)(2,1)S(1)}, bf16[1,2,48,768]{3,2,1,0:T(8,128)(2,1)S(1)}, u32[]{:S(2)}, u32[]{:S(2)}) collective-permute-start(bf16[1,2,48,768]{3,2,1,0:T(8,128)(2,1)S(1)} %bitcast.218), channel_id=1, source_target_pairs={{0,8},{1,9},{2,10},{3,11},{4,12},{5,13},{6,14},{7,15},{8,0},{9,1},... | collective-permute-start | bytes 442376 | tf_op jit(solution)/shard_map/ppermute | solution.py:77
  56.0 5.3 %collective-permute-done.8 = bf16[2,2,48,576]{3,2,1,0:T(8,128)(2,1)S(1)} collective-permute-done((bf16[2,2,48,576]{3,2,1,0:T(8,128)(2,1)S(1)}, bf16[2,2,48,576]{3,2,1,0:T(8,128)(2,1)S(1)}, u32[]{:S(2)}, u32[]{:S(2)}) %collective-permute-start.8) | collective-permute-done | bytes 221216 | tf_op jit(solution)/shard_map/ppermute | solution.py:77
  64.4 5.8 %collective-permute-done.12.refs_12_ = bf16[4,120,768]{2,1,0:T(8,128)(2,1)} collective-permute-done((bf16[4,120,768]{2,1,0:T(8,128)(2,1)S(1)}, bf16[4,120,768]{2,1,0:T(8,128)(2,1)}, u32[]{:S(2)}, u32[]{:S(2)}) %collective-permute-start.12) | collective-permute-done | bytes 737312 | tf_op jit(solution)/shard_map/ppermute | solution.py:77
  71.2 1.4 collective-permute-start.18
  74.8 1.4 collective-permute-start.21
  76.2 1.9 collective-permute-done.18
  79.4 3.9 %shard_map.247 = (f32[2,6,768]{2,1,0:T(8,128)S(1)}, bf16[512,768]{1,0:T(8,128)(2,1)S(1)}, bf16[512,576]{1,0:T(8,128)(2,1)S(1)}, bf16[512,192]{1,0:T(8,128)(2,1)S(1)}, bf16[768,576]{1,0:T(8,128)(2,1)S(1)}) custom-call(s32[1]{0:T(128)} %bitcast.3.core_ref, s32[1]{0:T(128)} %bitcast.1.pair_ref, s32[1]{0:T(128)} %bitcast.2.high_ref, ...), custom_call_target="tpu_custom_call" | custom-call | flops 6000000000 | bytes 18000000 | tf_op jit(solution)/shard_map/pallas_call | solution.py:140
  84.2 1.7 collective-permute-start.16
  86.1 6.6 %collective-permute-done.16.refs_2_ = bf16[512,192]{1,0:T(8,128)(2,1)S(1)} collective-permute-done((bf16[512,192]{1,0:T(8,128)(2,1)S(1)}, bf16[512,192]{1,0:T(8,128)(2,1)S(1)}, u32[]{:S(2)}, u32[]{:S(2)}) %collective-permute-start.16) | collective-permute-done | bytes 196640 | tf_op jit(solution)/shard_map/ppermute | solution.py:77
  92.7 1.4 collective-permute-done.17.refs_3_
  94.2 9.0 %shard_map.248 = (f32[256,768]{1,0:T(8,128)}, f32[256,768]{1,0:T(8,128)}, f32[256,768]{1,0:T(8,128)}, bf16[256,768]{1,0:T(8,128)(2,1)S(1)}, bf16[4,96,768]{2,1,0...) custom-call(s32[1]{0:T(128)} %bitcast.me_ref, ...), custom_call_target="tpu_custom_call" | custom-call | flops 12000000000 | bytes 36000000 | tf_op jit(solution)/shard_map/pallas_call | solution.py:140
  103.7 1.3 collective-permute-done.22
  106.3 1.4 collective-permute-start.23
  108.3 1.3 collective-permute-start.26
  111.1 6.4 %collective-permute-done.23.there_ref = bf16[256,768]{1,0:T(8,128)(2,1)S(1)} collective-permute-done((bf16[256,768]{1,0:T(8,128)(2,1)S(1)}, bf16[256,768]{1,0:T(8,128)(2,1)S(1)}, u32[]{:S(2)}, u32[]{:S(2)}) %collective-permute-start.23) | collective-permute-done | bytes 393248 | tf_op jit(solution)/shard_map/ppermute | solution.py:77
  118.6 1.9 shard_map.249
  120.7 4.1 %collective-permute-done.26 = bf16[384,768]{1,0:T(8,128)(2,1)} collective-permute-done((bf16[384,768]{1,0:T(8,128)(2,1)}, bf16[384,768]{1,0:T(8,128)(2,1)}, u32[]{:S(2)}, u32[]{:S(2)}) %collective-permute-start.26) | collective-permute-done | bytes 589856 | tf_op jit(solution)/shard_map/ppermute | solution.py:77
  126.5 3.0 %collective-permute-start.29 = (bf16[96,768]{1,0:T(8,128)(2,1)S(1)}, bf16[96,768]{1,0:T(8,128)(2,1)S(1)}, u32[]{:S(2)}, u32[]{:S(2)}) collective-permute-start(bf16[96,768]{1,0:T(8,128)(2,1)S(1)} %get-tuple-element.134), channel_id=1, source_target_pairs={{0,8},{1,9},{2,10},{3,11},{4,12},{5,13},{6,14},{7,15},{8,0},{9,1},... | collective-permute-start | bytes 442376 | tf_op jit(solution)/shard_map/ppermute | solution.py:77
  130.9 7.8 %shard_map.250 = (bf16[4,128,576]{2,1,0:T(8,128)(2,1)S(1)}, bf16[4,128,576]{2,1,0:T(8,128)(2,1)S(1)}, f32[256,768]{1,0:T(8,128)S(1)}, bf16[256,768]{1,0:T(8,128)...) custom-call(s32[1]{0:T(128)} %bitcast.me_ref, s32[1]{0:T(128)} %bitcast.3.core_ref, s32[1]{0:T(128)} %bitcast.1.pair_ref, ...), custom_call_target="tpu_custom_call" | custom-call | flops 12000000000 | bytes 36000000 | tf_op jit(solution)/shard_map/pallas_call | solution.py:140
  141.5 1.3 collective-permute-start.33
  144.2 1.3 convert_add_fusion.2
  145.5 1.3 collective-permute-done.31
  147.6 4.2 %all-to-all-start.2 = ((bf16[16,36,128]{2,1,0:T(8,128)(2,1)}), bf16[16,36,128]{2,1,0:T(8,128)(2,1)S(1)}, u32[]{:S(2)}, u32[]{:S(2)}) async-start(bf16[16,36,128]{2,1,0:T(8,128)(2,1)} %broadcast_in_dim.170), calls=%async_computation.2 | async-start | bytes 327680 | tf_op jit(solution)/shard_map/all_to_all | solution.py:697
  153.5 1.9 collective-permute-start.42
  155.5 2.4 %collective-permute-start.43 = (bf16[96,768]{1,0:T(8,128)(2,1)S(1)}, bf16[96,768]{1,0:T(8,128)(2,1)}, u32[]{:S(2)}, u32[]{:S(2)}) collective-permute-start(bf16[96,768]{1,0:T(8,128)(2,1)S(1)} %get-tuple-element.130), channel_id=1, source_target_pairs={{0,8},{1,9},{2,10},{3,11},{4,12},{5,13},{6,14},{7,15},{8,0},{9,1},... | collective-permute-start | bytes 442376 | tf_op jit(solution)/shard_map/ppermute | solution.py:77
  158.3 2.4 %all-to-all-done.2 = bf16[16,36,128]{2,1,0:T(8,128)(2,1)S(1)} async-done(((bf16[16,36,128]{2,1,0:T(8,128)(2,1)}), bf16[16,36,128]{2,1,0:T(8,128)(2,1)S(1)}, u32[]{:S(2)}, u32[]{:S(2)}) %all-to-all-start.2) | async-done | bytes 147488 | tf_op jit(solution)/shard_map/all_to_all | solution.py:697
  165.9 3.7 %collective-permute-done.43 = bf16[96,768]{1,0:T(8,128)(2,1)} collective-permute-done((bf16[96,768]{1,0:T(8,128)(2,1)S(1)}, bf16[96,768]{1,0:T(8,128)(2,1)}, u32[]{:S(2)}, u32[]{:S(2)}) %collective-permute-start.43) | collective-permute-done | bytes 147488 | tf_op jit(solution)/shard_map/ppermute | solution.py:77
  172.6 1.4 copy.87
  174.8 3.1 %collective-permute-start.35 = (bf16[128,576]{1,0:T(8,128)(2,1)S(1)}, bf16[128,576]{1,0:T(8,128)(2,1)S(1)}, u32[]{:S(2)}, u32[]{:S(2)}) collective-permute-start(bf16[128,576]{1,0:T(8,128)(2,1)S(1)} %get-tuple-element.127), channel_id=1, source_target_pairs={{0,4},{1,5},{2,6},{3,7},{4,0},{5,1},{6,2},{7,3},{8,12},{9,13},{10,... | collective-permute-start | bytes 442376 | tf_op jit(solution)/shard_map/ppermute | solution.py:77
  177.9 3.8 %all-to-all-start.3 = ((f32[32,1,216]{2,1,0:T(1,128)}), f32[32,1,216]{2,1,0:T(1,128)S(1)}, u32[]{:S(2)}, u32[]{:S(2)}) async-start(f32[32,1,216]{2,1,0:T(1,128)} %all_to_all.34), calls=%async_computation.3 | async-start | bytes 65536 | tf_op jit(solution)/shard_map/all_to_all | solution.py:724
  181.7 2.7 %collective-permute-start.36 = (bf16[128,576]{1,0:T(8,128)(2,1)S(1)}, bf16[128,576]{1,0:T(8,128)(2,1)S(1)}, u32[]{:S(2)}, u32[]{:S(2)}) collective-permute-start(bf16[128,576]{1,0:T(8,128)(2,1)S(1)} %get-tuple-element.126), channel_id=1, source_target_pairs={{0,8},{1,9},{2,10},{3,11},{4,12},{5,13},{6,14},{7,15},{8,0},{9,1},... | collective-permute-start | bytes 442376 | tf_op jit(solution)/shard_map/ppermute | solution.py:77
  184.4 1.5 collective-permute-start.37
  186.8 2.2 %all-to-all-done.3 = f32[32,1,216]{2,1,0:T(1,128)S(1)} async-done(((f32[32,1,216]{2,1,0:T(1,128)}), f32[32,1,216]{2,1,0:T(1,128)S(1)}, u32[]{:S(2)}, u32[]{:S(2)}) %all-to-all-start.3) | async-done | bytes 27680 | tf_op jit(solution)/shard_map/all_to_all | solution.py:724
  191.0 6.2 %collective-permute-done.36 = bf16[128,576]{1,0:T(8,128)(2,1)S(1)} collective-permute-done((bf16[128,576]{1,0:T(8,128)(2,1)S(1)}, bf16[128,576]{1,0:T(8,128)(2,1)S(1)}, u32[]{:S(2)}, u32[]{:S(2)}) %collective-permute-start.36) | collective-permute-done | bytes 147488 | tf_op jit(solution)/shard_map/ppermute | solution.py:77
  197.5 1.7 collective-permute-start.39
  200.1 1.4 collective-permute-done.39.refs_2_
  (292 shorter events, 54.3 us)
Async XLA Ops:
  1.7 29.2 %collective-permute-start.4 = (bf16[1,120,768]{2,1,0:T(8,128)(2,1)S(1)}, bf16[1,120,768]{2,1,0:T(8,128)(2,1)S(1)}, u32[]{:S(2)}, u32[]{:S(2)}) collective-permute-start(bf16[1,120,768]{2,1,0:T(8,128)(2,1)S(1)} %maximum_bitcast_fusion), channel_id=1, source_target_pairs={{0,8},{1,9},{2,10},{3,11},{4,12},{5,13},{6,14},{7,15},{8,0},{9,1},... | collective-permute-start | bytes 552968 | tf_op jit(solution)/shard_map/ppermute | solution.py:77
  8.1 10.4 %all-to-all-start = ((bf16[16,1,216]{2,1,0:T(2,128)(2,1)}), bf16[16,1,216]{2,1,0:T(2,128)(2,1)S(1)}, u32[]{:S(2)}, u32[]{:S(2)}) async-start(bf16[16,1,216]{2,1,0:T(2,128)(2,1)} %copy.74), calls=%async_computation | async-start | bytes 32768 | tf_op jit(solution)/shard_map/all_to_all | solution.py:587
  13.1 17.9 %collective-permute-start = (bf16[2,1,128,768]{3,2,1,0:T(8,128)(2,1)S(1)}, bf16[2,1,128,768]{3,2,1,0:T(8,128)(2,1)S(1)}, u32[]{:S(2)}, u32[]{:S(2)}) collective-permute-start(bf16[2,1,128,768]{3,2,1,0:T(8,128)(2,1)S(1)} %pad_maximum_fusion.1.own_ref), channel_id=1, source_target_pairs={{0,16},{1,17},{2,18},{3,19},{4,20},{5,21},{6,22},{7,23},{8,24},{9,... | collective-permute-start | bytes 1179656 | tf_op jit(solution)/shard_map/ppermute | solution.py:77
  19.0 11.5 %collective-permute-start.1 = (bf16[1,24,1344]{2,1,0:T(8,128)(2,1)S(1)}, bf16[1,24,1344]{2,1,0:T(8,128)(2,1)S(1)}, u32[]{:S(2)}, u32[]{:S(2)}) collective-permute-start(bf16[1,24,1344]{2,1,0:T(8,128)(2,1)S(1)} %get-tuple-element.144), channel_id=1, source_target_pairs={{0,1},{1,0},{2,3},{3,2},{4,5},{5,4},{6,7},{7,6},{8,9},{9,8},{10,11... | collective-permute-start | bytes 193544 | tf_op jit(solution)/shard_map/ppermute | solution.py:77
  19.1 7.8 %collective-permute-start.2 = (bf16[1,24,1344]{2,1,0:T(8,128)(2,1)S(1)}, bf16[1,24,1344]{2,1,0:T(8,128)(2,1)S(1)}, u32[]{:S(2)}, u32[]{:S(2)}) collective-permute-start(bf16[1,24,1344]{2,1,0:T(8,128)(2,1)S(1)} %get-tuple-element.143), channel_id=1, source_target_pairs={{0,16},{1,17},{2,18},{3,19},{4,20},{5,21},{6,22},{7,23},{8,24},{9,... | collective-permute-start | bytes 193544 | tf_op jit(solution)/shard_map/ppermute | solution.py:77
  21.1 5.1 %collective-permute-start.20 = (bf16[16,48]{1,0:T(8,128)(2,1)S(1)}, bf16[16,48]{1,0:T(8,128)(2,1)S(1)}, u32[]{:S(2)}, u32[]{:S(2)}) collective-permute-start(bf16[16,48]{1,0:T(8,128)(2,1)S(1)} %slice.194), channel_id=1, source_target_pairs={{0,16},{1,17},{2,18},{3,19},{4,20},{5,21},{6,22},{7,23},{8,24},{9,... | collective-permute-start | bytes 4616 | tf_op jit(solution)/shard_map/ppermute | solution.py:77
  26.1 4.4 %collective-permute-start.3 = (bf16[1,24,1344]{2,1,0:T(8,128)(2,1)S(1)}, bf16[1,24,1344]{2,1,0:T(8,128)(2,1)S(1)}, u32[]{:S(2)}, u32[]{:S(2)}) collective-permute-start(bf16[1,24,1344]{2,1,0:T(8,128)(2,1)S(1)} %get-tuple-element.142), channel_id=1, source_target_pairs={{0,17},{1,16},{2,19},{3,18},{4,21},{5,20},{6,23},{7,22},{8,25},{9,... | collective-permute-start | bytes 193544 | tf_op jit(solution)/shard_map/ppermute | solution.py:77
  32.4 4.6 %collective-permute-start.5 = (f32[16,2304]{1,0:T(8,128)S(1)}, f32[16,2304]{1,0:T(8,128)S(1)}, u32[]{:S(2)}, u32[]{:S(2)}) collective-permute-start(f32[16,2304]{1,0:T(8,128)S(1)} %bitcast.232), channel_id=1, source_target_pairs={{0,1},{1,0},{2,3},{3,2},{4,5},{5,4},{6,7},{7,6},{8,9},{9,8},{10,11... | collective-permute-start | bytes 442376 | tf_op jit(solution)/shard_map/ppermute | solution.py:77
  32.9 19.4 %collective-permute-start.7 = (bf16[1,2,48,576]{3,2,1,0:T(8,128)(2,1)S(1)}, bf16[1,2,48,576]{3,2,1,0:T(8,128)(2,1)S(1)}, u32[]{:S(2)}, u32[]{:S(2)}) collective-permute-start(bf16[1,2,48,576]{3,2,1,0:T(8,128)(2,1)S(1)} %bitcast.221), channel_id=1, source_target_pairs={{0,8},{1,9},{2,10},{3,11},{4,12},{5,13},{6,14},{7,15},{8,0},{9,1},... | collective-permute-start | bytes 331784 | tf_op jit(solution)/shard_map/ppermute | solution.py:77
  35.6 15.0 %collective-permute-start.6 = (bf16[2,120,768]{2,1,0:T(8,128)(2,1)S(1)}, bf16[2,120,768]{2,1,0:T(8,128)(2,1)S(1)}, u32[]{:S(2)}, u32[]{:S(2)}) collective-permute-start(bf16[2,120,768]{2,1,0:T(8,128)(2,1)S(1)} %pad_maximum_fusion.2), channel_id=1, source_target_pairs={{0,4},{1,5},{2,6},{3,7},{4,0},{5,1},{6,2},{7,3},{8,12},{9,13},{10,... | collective-permute-start | bytes 1105928 | tf_op jit(solution)/shard_map/ppermute | solution.py:77
  37.0 36.5 %collective-permute-start.10 = (bf16[2,1,256,768]{3,2,1,0:T(8,128)(2,1)}, bf16[2,1,256,768]{3,2,1,0:T(8,128)(2,1)}, u32[]{:S(2)}, u32[]{:S(2)}) collective-permute-start(bf16[2,1,256,768]{3,2,1,0:T(8,128)(2,1)} %bitcast.14.own_ref.refs_6_.x_ref.own_x_ref), channel_id=1, source_target_pairs={{0,1},{1,0},{2,3},{3,2},{4,5},{5,4},{6,7},{7,6},{8,9},{9,8},{10,11... | collective-permute-start | bytes 2359304 | tf_op jit(solution)/shard_map/ppermute | solution.py:77
  38.2 17.8 %all-to-all-start.1 = ((f32[16,1,4608]{2,1,0:T(1,128)}), f32[16,1,4608]{2,1,0:T(1,128)S(1)}, u32[]{:S(2)}, u32[]{:S(2)}) async-start(f32[16,1,4608]{2,1,0:T(1,128)} %all_to_all.30), calls=%async_computation.1 | async-start | bytes 589824 | tf_op jit(solution)/shard_map/all_to_all | solution.py:80
  50.7 19.6 %collective-permute-start.12 = (bf16[4,120,768]{2,1,0:T(8,128)(2,1)S(1)}, bf16[4,120,768]{2,1,0:T(8,128)(2,1)}, u32[]{:S(2)}, u32[]{:S(2)}) collective-permute-start(bf16[4,120,768]{2,1,0:T(8,128)(2,1)S(1)} %pad_maximum_fusion.refs_11_), channel_id=1, source_target_pairs={{0,2},{1,3},{2,0},{3,1},{4,6},{5,7},{6,4},{7,5},{8,10},{9,11},{10,... | collective-permute-start | bytes 2211848 | tf_op jit(solution)/shard_map/ppermute | solution.py:77
  52.4 8.9 %collective-permute-start.8 = (bf16[2,2,48,576]{3,2,1,0:T(8,128)(2,1)S(1)}, bf16[2,2,48,576]{3,2,1,0:T(8,128)(2,1)S(1)}, u32[]{:S(2)}, u32[]{:S(2)}) collective-permute-start(bf16[2,2,48,576]{3,2,1,0:T(8,128)(2,1)S(1)} %constant_dynamic-update-slice_fusion), channel_id=1, source_target_pairs={{0,4},{1,5},{2,6},{3,7},{4,0},{5,1},{6,2},{7,3},{8,12},{9,13},{10,... | collective-permute-start | bytes 663560 | tf_op jit(solution)/shard_map/ppermute | solution.py:77
  52.5 9.5 %collective-permute-start.9 = (bf16[1,2,48,768]{3,2,1,0:T(8,128)(2,1)S(1)}, bf16[1,2,48,768]{3,2,1,0:T(8,128)(2,1)S(1)}, u32[]{:S(2)}, u32[]{:S(2)}) collective-permute-start(bf16[1,2,48,768]{3,2,1,0:T(8,128)(2,1)S(1)} %bitcast.218), channel_id=1, source_target_pairs={{0,8},{1,9},{2,10},{3,11},{4,12},{5,13},{6,14},{7,15},{8,0},{9,1},... | collective-permute-start | bytes 442376 | tf_op jit(solution)/shard_map/ppermute | solution.py:77
  62.7 11.1 %collective-permute-start.13 = (bf16[2,2,48,768]{3,2,1,0:T(8,128)(2,1)}, bf16[2,2,48,768]{3,2,1,0:T(8,128)(2,1)}, u32[]{:S(2)}, u32[]{:S(2)}) collective-permute-start(bf16[2,2,48,768]{3,2,1,0:T(8,128)(2,1)} %constant_dynamic-update-slice_fusion.4), channel_id=1, source_target_pairs={{0,4},{1,5},{2,6},{3,7},{4,0},{5,1},{6,2},{7,3},{8,12},{9,13},{10,... | collective-permute-start | bytes 884744 | tf_op jit(solution)/shard_map/ppermute | solution.py:77
  63.3 16.2 %collective-permute-start.14 = (bf16[4,2,48,576]{3,2,1,0:T(8,128)(2,1)S(1)}, bf16[4,2,48,576]{3,2,1,0:T(8,128)(2,1)S(1)}, u32[]{:S(2)}, u32[]{:S(2)}) collective-permute-start(bf16[4,2,48,576]{3,2,1,0:T(8,128)(2,1)S(1)} %constant_dynamic-update-slice_fusion.2.own_w_ref), channel_id=1, source_target_pairs={{0,2},{1,3},{2,0},{3,1},{4,6},{5,7},{6,4},{7,5},{8,10},{9,11},{10,... | collective-permute-start | bytes 1327112 | tf_op jit(solution)/shard_map/ppermute | solution.py:77
  71.2 6.9 %collective-permute-start.18 = (bf16[8,24,768]{2,1,0:T(8,128)(2,1)S(1)}, bf16[8,24,768]{2,1,0:T(8,128)(2,1)}, u32[]{:S(2)}, u32[]{:S(2)}) collective-permute-start(bf16[8,24,768]{2,1,0:T(8,128)(2,1)S(1)} %bitcast.196), channel_id=1, source_target_pairs={{0,16},{1,17},{2,18},{3,19},{4,20},{5,21},{6,22},{7,23},{8,24},{9,... | collective-permute-start | bytes 884744 | tf_op jit(solution)/shard_map/ppermute | solution.py:77
  73.6 5.5 %collective-permute-start.11 = (f32[2,1,3,768]{3,2,1,0:T(4,128)S(1)}, f32[2,1,3,768]{3,2,1,0:T(4,128)S(1)}, u32[]{:S(2)}, u32[]{:S(2)}) collective-permute-start(f32[2,1,3,768]{3,2,1,0:T(4,128)S(1)} %bitcast.198), channel_id=1, source_target_pairs={{0,1},{1,0},{2,3},{3,2},{4,5},{5,4},{6,7},{7,6},{8,9},{9,8},{10,11... | collective-permute-start | bytes 55304 | tf_op jit(solution)/shard_map/ppermute | solution.py:77
  74.8 19.4 %collective-permute-start.21 = (bf16[4,2,48,768]{3,2,1,0:T(8,128)(2,1)S(1)}, bf16[4,2,48,768]{3,2,1,0:T(8,128)(2,1)S(1)}, u32[]{:S(2)}, u32[]{:S(2)}) collective-permute-start(bf16[4,2,48,768]{3,2,1,0:T(8,128)(2,1)S(1)} %constant_dynamic-update-slice_fusion.6.refs_9_), channel_id=1, source_target_pairs={{0,2},{1,3},{2,0},{3,1},{4,6},{5,7},{6,4},{7,5},{8,10},{9,11},{10,... | collective-permute-start | bytes 1769480 | tf_op jit(solution)/shard_map/ppermute | solution.py:77
  79.1 13.6 %collective-permute-start.19 = (bf16[2,8,24,768]{3,2,1,0:T(8,128)(2,1)S(1)}, bf16[2,8,24,768]{3,2,1,0:T(8,128)(2,1)S(1)}, u32[]{:S(2)}, u32[]{:S(2)}) collective-permute-start(bf16[2,8,24,768]{3,2,1,0:T(8,128)(2,1)S(1)} %bitcast_dynamic-update-slice_fusion.2), channel_id=1, source_target_pairs={{0,1},{1,0},{2,3},{3,2},{4,5},{5,4},{6,7},{7,6},{8,9},{9,8},{10,11... | collective-permute-start | bytes 1769480 | tf_op jit(solution)/shard_map/ppermute | solution.py:77
  84.2 8.4 %collective-permute-start.16 = (bf16[512,192]{1,0:T(8,128)(2,1)S(1)}, bf16[512,192]{1,0:T(8,128)(2,1)S(1)}, u32[]{:S(2)}, u32[]{:S(2)}) collective-permute-start(bf16[512,192]{1,0:T(8,128)(2,1)S(1)} %get-tuple-element.73.refs_0_.att_ref), channel_id=1, source_target_pairs={{0,16},{1,17},{2,18},{3,19},{4,20},{5,21},{6,22},{7,23},{8,24},{9,... | collective-permute-start | bytes 589832 | tf_op jit(solution)/shard_map/ppermute | solution.py:77
  85.9 6.8 %collective-permute-start.15 = (bf16[512,192]{1,0:T(8,128)(2,1)S(1)}, bf16[512,192]{1,0:T(8,128)(2,1)S(1)}, u32[]{:S(2)}, u32[]{:S(2)}) collective-permute-start(bf16[512,192]{1,0:T(8,128)(2,1)S(1)} %get-tuple-element.73.refs_0_.att_ref), channel_id=1, source_target_pairs={{0,1},{1,0},{2,3},{3,2},{4,5},{5,4},{6,7},{7,6},{8,9},{9,8},{10,11... | collective-permute-start | bytes 589832 | tf_op jit(solution)/shard_map/ppermute | solution.py:77
  106.3 11.2 %collective-permute-start.23 = (bf16[256,768]{1,0:T(8,128)(2,1)S(1)}, bf16[256,768]{1,0:T(8,128)(2,1)S(1)}, u32[]{:S(2)}, u32[]{:S(2)}) collective-permute-start(bf16[256,768]{1,0:T(8,128)(2,1)S(1)} %add_convert_fusion.3.mine_ref), channel_id=1, source_target_pairs={{0,16},{1,17},{2,18},{3,19},{4,20},{5,21},{6,22},{7,23},{8,24},{9,... | collective-permute-start | bytes 1179656 | tf_op jit(solution)/shard_map/ppermute | solution.py:77
  108.3 16.5 %collective-permute-start.26 = (bf16[384,768]{1,0:T(8,128)(2,1)}, bf16[384,768]{1,0:T(8,128)(2,1)}, u32[]{:S(2)}, u32[]{:S(2)}) collective-permute-start(bf16[384,768]{1,0:T(8,128)(2,1)} %copy-done.6), channel_id=1, source_target_pairs={{0,2},{1,3},{2,0},{3,1},{4,6},{5,7},{6,4},{7,5},{8,10},{9,11},{10,... | collective-permute-start | bytes 1769480 | tf_op jit(solution)/shard_map/ppermute | solution.py:77
  110.3 41.6 %collective-permute-start.41 = (bf16[4,96,768]{2,1,0:T(8,128)(2,1)}, bf16[4,96,768]{2,1,0:T(8,128)(2,1)}, u32[]{:S(2)}, u32[]{:S(2)}) collective-permute-start(bf16[4,96,768]{2,1,0:T(8,128)(2,1)} %copy-done.5), channel_id=1, source_target_pairs={{0,2},{1,3},{2,0},{3,1},{4,6},{5,7},{6,4},{7,5},{8,10},{9,11},{10,... | collective-permute-start | bytes 1769480 | tf_op jit(solution)/shard_map/ppermute | solution.py:77
  111.1 33.1 %collective-permute-start.25 = (bf16[256,768]{1,0:T(8,128)(2,1)S(1)}, bf16[256,768]{1,0:T(8,128)(2,1)}, u32[]{:S(2)}, u32[]{:S(2)}) collective-permute-start(bf16[256,768]{1,0:T(8,128)(2,1)S(1)} %get-tuple-element.82), channel_id=1, source_target_pairs={{0,1},{1,0},{2,3},{3,2},{4,5},{5,4},{6,7},{7,6},{8,9},{9,8},{10,11... | collective-permute-start | bytes 1179656 | tf_op jit(solution)/shard_map/ppermute | solution.py:77
  120.5 9.1 %collective-permute-start.24 = (bf16[256,768]{1,0:T(8,128)(2,1)S(1)}, bf16[256,768]{1,0:T(8,128)(2,1)S(1)}, u32[]{:S(2)}, u32[]{:S(2)}) collective-permute-start(bf16[256,768]{1,0:T(8,128)(2,1)S(1)} %get-tuple-element.86.own_ref), channel_id=1, source_target_pairs={{0,1},{1,0},{2,3},{3,2},{4,5},{5,4},{6,7},{7,6},{8,9},{9,8},{10,11... | collective-permute-start | bytes 1179656 | tf_op jit(solution)/shard_map/ppermute | solution.py:77
  126.3 13.3 %collective-permute-start.28 = (bf16[96,768]{1,0:T(8,128)(2,1)S(1)}, bf16[96,768]{1,0:T(8,128)(2,1)S(1)}, u32[]{:S(2)}, u32[]{:S(2)}) collective-permute-start(bf16[96,768]{1,0:T(8,128)(2,1)S(1)} %get-tuple-element.132), channel_id=1, source_target_pairs={{0,4},{1,5},{2,6},{3,7},{4,0},{5,1},{6,2},{7,3},{8,12},{9,13},{10,... | collective-permute-start | bytes 442376 | tf_op jit(solution)/shard_map/ppermute | solution.py:77
  126.5 13.1 %collective-permute-start.29 = (bf16[96,768]{1,0:T(8,128)(2,1)S(1)}, bf16[96,768]{1,0:T(8,128)(2,1)S(1)}, u32[]{:S(2)}, u32[]{:S(2)}) collective-permute-start(bf16[96,768]{1,0:T(8,128)(2,1)S(1)} %get-tuple-element.134), channel_id=1, source_target_pairs={{0,8},{1,9},{2,10},{3,11},{4,12},{5,13},{6,14},{7,15},{8,0},{9,1},... | collective-permute-start | bytes 442376 | tf_op jit(solution)/shard_map/ppermute | solution.py:77
  129.7 10.0 %collective-permute-start.30 = (bf16[96,768]{1,0:T(8,128)(2,1)S(1)}, bf16[96,768]{1,0:T(8,128)(2,1)S(1)}, u32[]{:S(2)}, u32[]{:S(2)}) collective-permute-start(bf16[96,768]{1,0:T(8,128)(2,1)S(1)} %get-tuple-element.133), channel_id=1, source_target_pairs={{0,12},{1,13},{2,14},{3,15},{4,8},{5,9},{6,10},{7,11},{8,4},{9,5},... | collective-permute-start | bytes 442376 | tf_op jit(solution)/shard_map/ppermute | solution.py:77
  139.6 3.5 %collective-permute-start.27 = (f32[1,3,768]{2,1,0:T(4,128)S(1)}, f32[1,3,768]{2,1,0:T(4,128)S(1)}, u32[]{:S(2)}, u32[]{:S(2)}) collective-permute-start(f32[1,3,768]{2,1,0:T(4,128)S(1)} %pad_maximum_fusion.10), channel_id=1, source_target_pairs={{0,1},{1,0},{2,3},{3,2},{4,5},{5,4},{6,7},{7,6},{8,9},{9,8},{10,11... | collective-permute-start | bytes 27656 | tf_op jit(solution)/shard_map/ppermute | solution.py:77
  141.5 24.0 %collective-permute-start.33 = (bf16[4,128,576]{1,2,0:T(8,128)(2,1)}, bf16[4,128,576]{1,2,0:T(8,128)(2,1)}, u32[]{:S(2)}, u32[]{:S(2)}) collective-permute-start(bf16[4,128,576]{1,2,0:T(8,128)(2,1)} %copy.85), channel_id=1, source_target_pairs={{0,2},{1,3},{2,0},{3,1},{4,6},{5,7},{6,4},{7,5},{8,10},{9,11},{10,... | collective-permute-start | bytes 1769480 | tf_op jit(solution)/shard_map/ppermute | solution.py:77
  142.8 19.6 %collective-permute-start.32 = (bf16[256,768]{1,0:T(8,128)(2,1)}, bf16[256,768]{1,0:T(8,128)(2,1)}, u32[]{:S(2)}, u32[]{:S(2)}) collective-permute-start(bf16[256,768]{1,0:T(8,128)(2,1)} %copy-done.7), channel_id=1, source_target_pairs={{0,1},{1,0},{2,3},{3,2},{4,5},{5,4},{6,7},{7,6},{8,9},{9,8},{10,11... | collective-permute-start | bytes 1179656 | tf_op jit(solution)/shard_map/ppermute | solution.py:77
  143.1 3.8 %collective-permute-start.31 = (f32[1,3,768]{2,1,0:T(4,128)S(1)}, f32[1,3,768]{2,1,0:T(4,128)S(1)}, u32[]{:S(2)}, u32[]{:S(2)}) collective-permute-start(f32[1,3,768]{2,1,0:T(4,128)S(1)} %fusion.25), channel_id=1, source_target_pairs={{0,16},{1,17},{2,18},{3,19},{4,20},{5,21},{6,22},{7,23},{8,24},{9,... | collective-permute-start | bytes 27656 | tf_op jit(solution)/shard_map/ppermute | solution.py:77
  147.6 13.2 %all-to-all-start.2 = ((bf16[16,36,128]{2,1,0:T(8,128)(2,1)}), bf16[16,36,128]{2,1,0:T(8,128)(2,1)S(1)}, u32[]{:S(2)}, u32[]{:S(2)}) async-start(bf16[16,36,128]{2,1,0:T(8,128)(2,1)} %broadcast_in_dim.170), calls=%async_computation.2 | async-start | bytes 327680 | tf_op jit(solution)/shard_map/all_to_all | solution.py:697
  153.5 12.3 %collective-permute-start.42 = (bf16[96,768]{1,0:T(8,128)(2,1)S(1)}, bf16[96,768]{1,0:T(8,128)(2,1)S(1)}, u32[]{:S(2)}, u32[]{:S(2)}) collective-permute-start(bf16[96,768]{1,0:T(8,128)(2,1)S(1)} %get-tuple-element.131), channel_id=1, source_target_pairs={{0,4},{1,5},{2,6},{3,7},{4,0},{5,1},{6,2},{7,3},{8,12},{9,13},{10,... | collective-permute-start | bytes 442376 | tf_op jit(solution)/shard_map/ppermute | solution.py:77
  155.5 14.1 %collective-permute-start.43 = (bf16[96,768]{1,0:T(8,128)(2,1)S(1)}, bf16[96,768]{1,0:T(8,128)(2,1)}, u32[]{:S(2)}, u32[]{:S(2)}) collective-permute-start(bf16[96,768]{1,0:T(8,128)(2,1)S(1)} %get-tuple-element.130), channel_id=1, source_target_pairs={{0,8},{1,9},{2,10},{3,11},{4,12},{5,13},{6,14},{7,15},{8,0},{9,1},... | collective-permute-start | bytes 442376 | tf_op jit(solution)/shard_map/ppermute | solution.py:77
  157.8 11.7 %collective-permute-start.44 = (bf16[96,768]{1,0:T(8,128)(2,1)S(1)}, bf16[96,768]{1,0:T(8,128)(2,1)}, u32[]{:S(2)}, u32[]{:S(2)}) collective-permute-start(bf16[96,768]{1,0:T(8,128)(2,1)S(1)} %get-tuple-element.129), channel_id=1, source_target_pairs={{0,12},{1,13},{2,14},{3,15},{4,8},{5,9},{6,10},{7,11},{8,4},{9,5},... | collective-permute-start | bytes 442376 | tf_op jit(solution)/shard_map/ppermute | solution.py:77
  164.3 39.0 %collective-permute-start.34 = (bf16[2,1,128,768]{3,2,1,0:T(8,128)(2,1)}, bf16[2,1,128,768]{3,2,1,0:T(8,128)(2,1)}, u32[]{:S(2)}, u32[]{:S(2)}) collective-permute-start(bf16[2,1,128,768]{3,2,1,0:T(8,128)(2,1)} %fusion.14), channel_id=1, source_target_pairs={{0,16},{1,17},{2,18},{3,19},{4,20},{5,21},{6,22},{7,23},{8,24},{9,... | collective-permute-start | bytes 1179656 | tf_op jit(solution)/shard_map/ppermute | solution.py:77
  170.6 11.1 %collective-permute-start.45 = (bf16[24,768]{1,0:T(8,128)(2,1)S(1)}, bf16[24,768]{1,0:T(8,128)(2,1)S(1)}, u32[]{:S(2)}, u32[]{:S(2)}) collective-permute-start(bf16[24,768]{1,0:T(8,128)(2,1)S(1)} %get-tuple-element.155), channel_id=1, source_target_pairs={{0,1},{1,0},{2,3},{3,2},{4,5},{5,4},{6,7},{7,6},{8,9},{9,8},{10,11... | collective-permute-start | bytes 110600 | tf_op jit(solution)/shard_map/ppermute | solution.py:77
  170.7 13.7 %collective-permute-start.46 = (bf16[24,768]{1,0:T(8,128)(2,1)S(1)}, bf16[24,768]{1,0:T(8,128)(2,1)S(1)}, u32[]{:S(2)}, u32[]{:S(2)}) collective-permute-start(bf16[24,768]{1,0:T(8,128)(2,1)S(1)} %get-tuple-element.154), channel_id=1, source_target_pairs={{0,16},{1,17},{2,18},{3,19},{4,20},{5,21},{6,22},{7,23},{8,24},{9,... | collective-permute-start | bytes 110600 | tf_op jit(solution)/shard_map/ppermute | solution.py:77
  171.9 14.0 %collective-permute-start.47 = (bf16[24,768]{1,0:T(8,128)(2,1)S(1)}, bf16[24,768]{1,0:T(8,128)(2,1)S(1)}, u32[]{:S(2)}, u32[]{:S(2)}) collective-permute-start(bf16[24,768]{1,0:T(8,128)(2,1)S(1)} %get-tuple-element.153), channel_id=1, source_target_pairs={{0,17},{1,16},{2,19},{3,18},{4,21},{5,20},{6,23},{7,22},{8,25},{9,... | collective-permute-start | bytes 110600 | tf_op jit(solution)/shard_map/ppermute | solution.py:77
  174.8 16.2 %collective-permute-start.35 = (bf16[128,576]{1,0:T(8,128)(2,1)S(1)}, bf16[128,576]{1,0:T(8,128)(2,1)S(1)}, u32[]{:S(2)}, u32[]{:S(2)}) collective-permute-start(bf16[128,576]{1,0:T(8,128)(2,1)S(1)} %get-tuple-element.127), channel_id=1, source_target_pairs={{0,4},{1,5},{2,6},{3,7},{4,0},{5,1},{6,2},{7,3},{8,12},{9,13},{10,... | collective-permute-start | bytes 442376 | tf_op jit(solution)/shard_map/ppermute | solution.py:77
  177.9 11.1 %all-to-all-start.3 = ((f32[32,1,216]{2,1,0:T(1,128)}), f32[32,1,216]{2,1,0:T(1,128)S(1)}, u32[]{:S(2)}, u32[]{:S(2)}) async-start(f32[32,1,216]{2,1,0:T(1,128)} %all_to_all.34), calls=%async_computation.3 | async-start | bytes 65536 | tf_op jit(solution)/shard_map/all_to_all | solution.py:724
  181.7 15.5 %collective-permute-start.36 = (bf16[128,576]{1,0:T(8,128)(2,1)S(1)}, bf16[128,576]{1,0:T(8,128)(2,1)S(1)}, u32[]{:S(2)}, u32[]{:S(2)}) collective-permute-start(bf16[128,576]{1,0:T(8,128)(2,1)S(1)} %get-tuple-element.126), channel_id=1, source_target_pairs={{0,8},{1,9},{2,10},{3,11},{4,12},{5,13},{6,14},{7,15},{8,0},{9,1},... | collective-permute-start | bytes 442376 | tf_op jit(solution)/shard_map/ppermute | solution.py:77
  184.4 12.7 %collective-permute-start.37 = (bf16[128,576]{1,0:T(8,128)(2,1)S(1)}, bf16[128,576]{1,0:T(8,128)(2,1)S(1)}, u32[]{:S(2)}, u32[]{:S(2)}) collective-permute-start(bf16[128,576]{1,0:T(8,128)(2,1)S(1)} %get-tuple-element.125), channel_id=1, source_target_pairs={{0,12},{1,13},{2,14},{3,15},{4,8},{5,9},{6,10},{7,11},{8,4},{9,5},... | collective-permute-start | bytes 442376 | tf_op jit(solution)/shard_map/ppermute | solution.py:77
  197.5 4.0 %collective-permute-start.39 = (bf16[24,576]{1,0:T(8,128)(2,1)S(1)}, bf16[24,576]{1,0:T(8,128)(2,1)S(1)}, u32[]{:S(2)}, u32[]{:S(2)}) collective-permute-start(bf16[24,576]{1,0:T(8,128)(2,1)S(1)} %get-tuple-element.158), channel_id=1, source_target_pairs={{0,16},{1,17},{2,18},{3,19},{4,20},{5,21},{6,22},{7,23},{8,24},{9,... | collective-permute-start | bytes 82952 | tf_op jit(solution)/shard_map/ppermute | solution.py:77
  (32 other events, 186.0 us)

commit v4 on v3

--- a/solution.py
+++ b/solution.py
@@ -121,18 +121,19 @@
     def pick(self, value, spot, axis=0):
         return lax.dynamic_index_in_dim(value, spot, axis, keepdims=False)
 
-    def scatter(self, value, bits, earlier=()):
-        spot = self.place(bits)
-        arrived = []
-        for step in range(1, 1 << len(bits)):
-            arrived.append(self.send(self.pick(value, spot ^ step).astype(BF16), bits, step))
-        total = self.pick(value, spot)
-        if earlier:
-            total = after(total, *earlier)
-        total = total.astype(F32)
-        for part in arrived:
-            total = total + part.astype(F32)
-        return total
+    def scatter(self, value, bits, earlier=(), first=()):
+        for bit in reversed(bits):
+            spot = self.place([bit])
+            value = value.reshape((-1, 2) + value.shape[1:])
+            part = self.send(self.pick(value, 1 - spot, 1).astype(BF16), [bit])
+            value = self.pick(value, spot, 1)
+            ready = earlier if bit == bits[0] else first
+            if ready:
+                value = after(value, *ready)
+            value = value.astype(F32) + part.astype(F32)
+            if bit != bits[0]:
+                value = value.astype(BF16)
+        return value[0]
 
 
 def call(kernel, outs, *args, scalars=0, scratch=(), us=5):
@@ -145,7 +146,7 @@
         scratch_shapes=[pltpu.VMEM(shape, dtype) for shape, dtype in scratch],
         compiler_params=pltpu.CompilerParams(vmem_limit_bytes=48 * 2**20),
         cost_estimate=pl.CostEstimate(
-            flops=us * 10**9, bytes_accessed=us * 3 * 10**6, transcendentals=0
+            flops=us * 10**8, bytes_accessed=us * 3 * 10**5, transcendentals=0
         ),
     )(*arrays)
 
@@ -393,7 +394,7 @@
     group = columns // 3
     seq, high, block = blocks
     rows = block // 2
-    third = rows // 3
+    team = 2 * seq
     size = seq * block
     scale = HD ** (-0.5)
 
@@ -447,19 +448,19 @@
         rows_ref[pl.ds((1 - core_ref[0]) * high, high)] = grad_near.reshape(half_rows)
         for to, out_ref in ((pair_ref[0], keep_ref), (1 - pair_ref[0], send_ref)):
             for second in range(high):
-                for first in range(seq):
-                    lane = slice(first * block, (first + 1) * block)
-                    out_ref[second, lane] = whole_ref[first * high + second, to]
-                piece = rows_ref[second * 2 + to, core_ref[0]].astype(BF16)
-                out_ref[second, size : size + rows] = piece[:, :columns]
-                out_ref[second, size + rows :] = jnp.concatenate(
-                    [piece[at * third : (at + 1) * third, columns:] for at in range(3)], axis=1
+                ours = [whole_ref[first * high + second, to] for first in range(seq)]
+                piece = rows_ref[second * 2 + to, core_ref[0]]
+                beside = jnp.concatenate(
+                    [piece[:, at * group : (at + 1) * group] for at in range(team)], axis=0
+                )
+                out_ref[second] = jnp.concatenate(
+                    [jnp.concatenate(ours, axis=0), beside.astype(BF16)], axis=1
                 )
 
     own_total = latents * seq_len
     outs = [
-        ((high, size + rows + third, columns), BF16),
-        ((high, size + rows + third, columns), BF16),
+        ((high, size, columns + group), BF16),
+        ((high, size, columns + group), BF16),
         ((own_total, width), F32),
         ((own_total, width), BF16),
         ((count, 2, width), F32),
@@ -607,34 +608,34 @@
     team_part = jnp.concatenate(
         [team_qkv.reshape(team, rows, columns), team_fc1.reshape(team, rows, hidden)], axis=2
     )
-    team_part = link.exchange(after(team_part, from_all), team_bits)
-    part = dot(all_cond, w_ada)
+    team_part = link.exchange(team_part, team_bits)
+    part = dot(after(all_cond, team_part), w_ada)
     own_columns = (jnp.arange(shards) == link.index)[:, None] * b_ada.astype(F32)[None, :]
-    part = after(part + own_columns.reshape(-1), acts, team_part, direct[1])
+    part = after(part + own_columns.reshape(-1), direct[1])
     part = part.reshape(fsdp * latents, 2, 3 * width)
+    team_qkv = team_part[:, :, :columns].reshape(1, seq, 2 * rows, columns)
+    team_fc1 = team_part[:, :, columns:].reshape(1, seq, 2 * rows, hidden)
+    steps = [team_qkv, link.gather_step(team_qkv, high_bits[0])]
     part = link.pick(part, core, 1) + link.send(link.pick(part, 1 - core, 1), core_bit)
+    part = after(part, steps[1], acts)
     part = part.reshape(1, rest, count * 3 * width)
     part = jnp.broadcast_to(part, (seq, rest, count * 3 * width)).reshape(chips, -1)
     sent_part = part
     part = link.all_to_all(part, seq_bits + [*high_bits, *pair_bit])
 
-    team_qkv = team_part[:, :, :columns].reshape(1, seq, 2 * rows, columns)
-    team_fc1 = team_part[:, :, columns:].reshape(1, seq, 2 * rows, hidden)
     direct_own = direct[-1]
     direct_other = link.send(direct_own, pair_bit)
-    steps = [team_qkv]
-    for bit in high_bits:
-        ready = (direct_own,) if bit == high_bits[0] else (part,)
-        steps.append(link.gather_step(steps[-1], bit, ready))
+    for bit in high_bits[1:]:
+        steps.append(link.gather_step(steps[-1], bit, (part,)))
     qkv_own = steps[-1]
     qkv_other = link.send(qkv_own, pair_bit)
     other_acts = link.send(acts, core_bit)
-    fc1_steps = [after(team_fc1, steps[1])]
+    fc1_steps = [after(team_fc1, steps[2])]
     for bit in high_bits:
         fc1_steps.append(link.gather_step(fc1_steps[-1], bit, (qkv_own,)))
     fc1_own = fc1_steps[-1]
     fc1_other = link.send(fc1_own, pair_bit)
-    part = after(part, fc1_steps[1], other_acts)
+    part = after(part, qkv_own, other_acts)
     modulation = jnp.sum(part, axis=0).reshape(2, latents, 3, width)
     full_proj = interleave_call(
         direct_own[:, None, hidden_rows:], direct_other[:, None, hidden_rows:], pair, spot
@@ -642,7 +643,7 @@
     half_proj = full_proj
     full_proj = link.gather(full_proj.reshape(rest, rows, width), seq_bits, 0)
     full_proj = link.gather(full_proj, core_bit, 2).reshape(team, group, width)
-    bias_out = link.gather(after(biases, sent_part)[:, 2 * rows : 4 * rows], seq_bits, 0)
+    bias_out = link.gather(after(biases, qkv_own)[:, 2 * rows : 4 * rows], seq_bits, 0)
     bias_proj, bias_fc2 = (
         bias_out[:, :, at * rows : (at + 1) * rows].reshape(1, width).astype(F32) for at in range(2)
     )
@@ -687,18 +688,20 @@
 
     late = jnp.concatenate([sums_attn, grad_gate_mlp], axis=1)
     late = late[:latents] + link.send(late[latents:], core_bit)
-    grad_fc2 = link.scatter(grad_fc2, high_bits)
-    late = after(late, grad_fc2)
     late = late + link.send(late, seq_bits)
     grad_mod = jnp.concatenate([late[:, :2], sums_mid, late[:, 2:]], axis=1)
     grad_mod = grad_mod.reshape(1, -1, 128).astype(BF16)
     grad_mod = jnp.broadcast_to(grad_mod, (fsdp,) + grad_mod.shape[1:])
+    sent_qkv = link.send(send_qkv, pair_bit)
+    grad_qkv = after(keep_qkv, late).astype(F32) + sent_qkv.astype(F32)
+    grad_qkv = grad_qkv.astype(BF16)
+    grad_mod = after(grad_mod, grad_qkv)
     sent_mod = grad_mod
+    grad_fc2 = link.scatter(grad_fc2, high_bits, (sent_mod,), (sums_attn,))
     grad_mod = lax.all_to_all(grad_mod, "fsdp", 0, 0, tiled=True)
     grad_mod = grad_mod.reshape(fsdp * latents, 6 * width)
 
-    sent_qkv = link.send(send_qkv, pair_bit)
-    grad_silu = dot_rt(after(grad_mod, sent_qkv), w_ada).reshape(1, fsdp, mine)
+    grad_silu = dot_rt(grad_mod, w_ada).reshape(1, fsdp, mine)
     grad_silu = jnp.broadcast_to(grad_silu, (seq, fsdp, mine)).reshape(shards, -1)
     grad_ada = dot_lt(all_cond, grad_mod)
     own_ada = b_ada.shape[0]
@@ -720,19 +723,15 @@
     in_core = jnp.arange(2).reshape(1, 1, 2, 1) == core
     by_owner.append(jnp.where(in_seq & in_core, sums_up, 0.0).reshape(shards, hidden_rows))
     tail = jnp.concatenate([grad_silu] + by_owner, axis=1)
-    sent_tail = tail
     tail = lax.all_to_all(tail, AXES, 0, 0, tiled=True)
-    grad_fc1 = after(keep_fc1, late).astype(F32) + sent_fc1.astype(F32)
-    grad_fc1 = link.scatter(grad_fc1.astype(BF16), high_bits, (sent_tail,)).astype(BF16)
+    grad_fc1 = after(keep_fc1, sums_attn).astype(F32) + sent_fc1.astype(F32)
+    grad_fc1 = link.scatter(grad_fc1.astype(BF16), high_bits, (tail,), (grad_qkv,)).astype(BF16)
     grad_fc1 = link.exchange_pieces(grad_fc1.reshape(team, rows, hidden), team_bits)
     grad_fc1 = join_fc1(me, pair, grad_fc1, high)
-    grad_qkv = after(keep_qkv, sent_mod).astype(F32) + sent_qkv.astype(F32)
-    grad_qkv = link.scatter(grad_qkv.astype(BF16), high_bits, (sent_tail,))
-    size = team * rows
-    grad_proj = grad_qkv[size : size + rows]
-    last = grad_qkv[size + rows :].reshape(rows // 3, 3, group).swapaxes(0, 1)
-    grad_proj = jnp.concatenate([grad_proj, last.reshape(rows, group)], axis=1)
-    grad_qkv = grad_qkv[:size].astype(BF16).reshape(team, rows, columns)
+    grad_qkv = link.scatter(grad_qkv, high_bits, (tail,))
+    grad_proj = grad_qkv[:, columns:].reshape(team, rows, group)
+    grad_proj = jnp.concatenate([grad_proj[at] for at in range(team)], axis=1)
+    grad_qkv = grad_qkv[:, :columns].astype(BF16).reshape(team, rows, columns)
     grad_qkv = join_qkv(me, link.exchange_pieces(grad_qkv, team_bits))
 
     def own_rows(value):
@@ -742,7 +741,7 @@
     branch = after(branch, other_attn) + sent_branch.astype(F32)
     grad_h_attn = after(grad_h_attn, sent_mod) + link.send(other_h_attn, core_bit).astype(F32)
     both = jnp.stack([branch, grad_h_attn]).reshape(2, latents, seq, local_len, width)
-    both = link.scatter(jnp.moveaxis(both, 2, 0), seq_bits, (sent_tail,))
+    both = link.scatter(jnp.moveaxis(both, 2, 0), seq_bits, (tail,))
     output = (own_rows(mid) + mod[:latents, 5:6] * both[0]).astype(BF16)
     norm, rate = norm_parts(tokens.astype(F32))
     grad_tokens = norm_back(norm, rate, both[1] * (1.0 + mod[:latents, 1:2]))

time: 209 us -> 205 us (0.981)
  local copies, waits for them, and re-layouts: 20.8 us -> 36.4 us
  waiting for transfers between devices: 69.8 us -> 57.7 us
  starting transfers between devices: 67.6 us -> 58.1 us
  other arithmetic: 19.9 us -> 24.3 us
    ppermute x48 -> x45, starting transfers between devices: 52 us -> 38.9 us  [send(): lax.ppermute(value, AXES, [(i, i ^ mask) for i in range(self.devices)])]
    ppermute x48 -> x45, waiting for transfers between devices: 63.3 us -> 51.6 us  [send(): lax.ppermute(value, AXES, [(i, i ^ mask) for i in range(self.devices)])]
    unnamed x65 -> x118, local copies, waits for them, and re-layouts: 4.81 us -> 13.2 us
    all_to_all x1, waiting for transfers between devices: 0.01 us -> 3.89 us  [all_to_all(): lax.all_to_all(value, AXES, 0, 0, tiled=True, axis_index_groups=self.grou...]
    all_to_all x1, starting transfers between devices: 3.72 us -> 6.76 us  [all_to_all(): lax.all_to_all(value, AXES, 0, 0, tiled=True, axis_index_groups=self.grou...]
    convert_element_type x3 -> x6, other arithmetic: 2.06 us -> 5.09 us  [the longest x3 2.22 us: scatter(): value = value.astype(BF16)]
    squeeze x5 -> x8, local copies, waits for them, and re-layouts: 0.43 us -> 3.1 us  [pick(): return lax.dynamic_index_in_dim(value, spot, axis, keepdims=False)]
    concatenate x2 -> x3, other arithmetic: 0.11 us -> 2.59 us  [gather_step(): return jnp.concatenate([value, part], 0)]
  transfers between devices with their start and end apart: 52 -> 49, of which waited for: 20 -> 18; matrix products, arithmetic and copies ran while one was open for 15% -> 24% of each run, Pallas kernels for 7% -> 7%
where the time goes in v4:
time: 205 us; the launch traced here: 204 us
  starting transfers between devices  58.1 us (28%)
  waiting for transfers between devices  57.7 us (28%)
  local copies, waits for them, and re-layouts  36.4 us (18%)
  other arithmetic  24.3 us (12%)
  Pallas kernels  23.9 us (12%)
    ppermute x45, waiting for transfers between devices, send(): lax.ppermute(value, AXES, [(i, i ^ mask) for i in range(self.devices)])  51.6 us
    ppermute x45, starting transfers between devices, send(): lax.ppermute(value, AXES, [(i, i ^ mask) for i in range(self.devices)])  38.9 us
    pallas_call x8, Pallas kernels, call(): pl.pallas_call(kernel, out_shape=[jax.ShapeDtypeStruct(shape, dtype) for...  23.9 us
    unnamed x118, local copies, waits for them, and re-layouts  13.2 us
    all_to_all x1, starting transfers between devices, all_to_all(): lax.all_to_all(value, AXES, 0, 0, tiled=True, axis_index_groups=self.grou...  6.76 us
    all_to_all x1, starting transfers between devices, local(): from_all = lax.all_to_all(to_all, 'fsdp', 0, 0, tiled=True)  6.17 us
  transfers between devices with their start and end apart: 49, of which 18 were waited for; matrix products, arithmetic and copies ran while one was open for 24% of the time, Pallas kernels for 7%

profile of v4, /device:TPU:0, one launch (start us, length us, event | category | flops | bytes accessed | tf_op | source)
XLA Modules:
  0.0 203.6 jit_solution(1961424898091781048)
XLA Ops:
  0.7 1.2 reshape.521
  4.7 2.6 %collective-permute-start.1 = (bf16[1,24,1344]{2,1,0:T(8,128)(2,1)S(1)}, bf16[1,24,1344]{2,1,0:T(8,128)(2,1)S(1)}, u32[]{:S(2)}, u32[]{:S(2)}) collective-permute-start(bf16[1,24,1344]{2,1,0:T(8,128)(2,1)S(1)} %get-tuple-element.150), channel_id=1, source_target_pairs={{0,16},{1,17},{2,18},{3,19},{4,20},{5,21},{6,22},{7,23},{8,24},{9,... | collective-permute-start | bytes 193544 | tf_op jit(solution)/shard_map/ppermute | solution.py:77
  8.8 6.2 %all-to-all-start = ((bf16[16,1,216]{2,1,0:T(2,128)(2,1)}), bf16[16,1,216]{2,1,0:T(2,128)(2,1)S(1)}, u32[]{:S(2)}, u32[]{:S(2)}) async-start(bf16[16,1,216]{2,1,0:T(2,128)(2,1)} %copy.78), calls=%async_computation | async-start | bytes 32768 | tf_op jit(solution)/shard_map/all_to_all | solution.py:588
  15.0 2.9 %collective-permute-start.3 = (bf16[1,120,768]{2,1,0:T(8,128)(2,1)S(1)}, bf16[1,120,768]{2,1,0:T(8,128)(2,1)S(1)}, u32[]{:S(2)}, u32[]{:S(2)}) collective-permute-start(bf16[1,120,768]{2,1,0:T(8,128)(2,1)S(1)} %maximum_bitcast_fusion), channel_id=1, source_target_pairs={{0,8},{1,9},{2,10},{3,11},{4,12},{5,13},{6,14},{7,15},{8,0},{9,1},... | collective-permute-start | bytes 552968 | tf_op jit(solution)/shard_map/ppermute | solution.py:77
  18.0 1.6 collective-permute-start.6
  22.8 7.5 %collective-permute-done.3 = bf16[1,120,768]{2,1,0:T(8,128)(2,1)S(1)} collective-permute-done((bf16[1,120,768]{2,1,0:T(8,128)(2,1)S(1)}, bf16[1,120,768]{2,1,0:T(8,128)(2,1)S(1)}, u32[]{:S(2)}, u32[]{:S(2)}) %collective-permute-start.3) | collective-permute-done | bytes 184352 | tf_op jit(solution)/shard_map/ppermute | solution.py:77
  34.8 6.8 %all-to-all-start.1 = ((f32[16,1,4608]{2,1,0:T(1,128)}), f32[16,1,4608]{2,1,0:T(1,128)S(1)}, u32[]{:S(2)}, u32[]{:S(2)}) async-start(f32[16,1,4608]{2,1,0:T(1,128)} %all_to_all.30), calls=%async_computation.1 | async-start | bytes 589824 | tf_op jit(solution)/shard_map/all_to_all | solution.py:80
  41.8 1.8 collective-permute-start.7
  43.6 1.9 collective-permute-done.10
  46.6 2.0 %collective-permute-start.11 = (bf16[4,120,768]{2,1,0:T(8,128)(2,1)S(1)}, bf16[4,120,768]{2,1,0:T(8,128)(2,1)}, u32[]{:S(2)}, u32[]{:S(2)}) collective-permute-start(bf16[4,120,768]{2,1,0:T(8,128)(2,1)S(1)} %pad_maximum_fusion.refs_11_), channel_id=1, source_target_pairs={{0,2},{1,3},{2,0},{3,1},{4,6},{5,7},{6,4},{7,5},{8,10},{9,11},{10,... | collective-permute-start | bytes 2211848 | tf_op jit(solution)/shard_map/ppermute | solution.py:77
  48.6 3.9 %all-to-all-done.1 = f32[16,1,4608]{2,1,0:T(1,128)S(1)} async-done(((f32[16,1,4608]{2,1,0:T(1,128)}), f32[16,1,4608]{2,1,0:T(1,128)S(1)}, u32[]{:S(2)}, u32[]{:S(2)}) %all-to-all-start.1) | async-done | bytes 294944 | tf_op jit(solution)/shard_map/all_to_all | solution.py:80
  53.3 1.7 constant_dynamic-update-slice_fusion.1
  54.9 1.7 constant_dynamic-update-slice_fusion.own_w_ref
  56.6 1.3 collective-permute-start.12
  57.9 1.5 collective-permute-start.14
  59.5 1.5 collective-permute-start.20
  61.7 1.5 collective-permute-done.20
  63.9 1.9 collective-permute-done.12
  67.4 1.2 reduce_sum.72
  69.7 1.5 collective-permute-start.18
  72.9 2.7 %collective-permute-done.13 = bf16[2,2,48,768]{3,2,1,0:T(8,128)(2,1)} collective-permute-done((bf16[2,2,48,768]{3,2,1,0:T(8,128)(2,1)}, bf16[2,2,48,768]{3,2,1,0:T(8,128)(2,1)}, u32[]{:S(2)}, u32[]{:S(2)}) %collective-permute-start.13) | collective-permute-done | bytes 294944 | tf_op jit(solution)/shard_map/ppermute | solution.py:77
  76.7 3.7 %shard_map.247 = (f32[2,6,768]{2,1,0:T(8,128)S(1)}, bf16[512,768]{1,0:T(8,128)(2,1)S(1)}, bf16[512,576]{1,0:T(8,128)(2,1)S(1)}, bf16[512,192]{1,0:T(8,128)(2,1)S(1)}, bf16[768,576]{1,0:T(8,128)(2,1)S(1)}) custom-call(s32[1]{0:T(128)} %bitcast.3.core_ref, s32[1]{0:T(128)} %bitcast.1.pair_ref, s32[1]{0:T(128)} %bitcast.2.high_ref, ...), custom_call_target="tpu_custom_call" | custom-call | flops 600000000 | bytes 1800000 | tf_op jit(solution)/shard_map/pallas_call | solution.py:141
  83.1 1.5 collective-permute-start.16
  85.5 1.7 collective-permute-start.21
  87.5 2.9 %collective-permute-done.16.refs_2_ = bf16[512,192]{1,0:T(8,128)(2,1)S(1)} collective-permute-done((bf16[512,192]{1,0:T(8,128)(2,1)S(1)}, bf16[512,192]{1,0:T(8,128)(2,1)S(1)}, u32[]{:S(2)}, u32[]{:S(2)}) %collective-permute-start.16) | collective-permute-done | bytes 196640 | tf_op jit(solution)/shard_map/ppermute | solution.py:77
  92.8 8.5 %collective-permute-done.21.refs_10_ = bf16[4,2,48,768]{3,2,1,0:T(8,128)(2,1)S(1)} collective-permute-done((bf16[4,2,48,768]{3,2,1,0:T(8,128)(2,1)S(1)}, bf16[4,2,48,768]{3,2,1,0:T(8,128)(2,1)S(1)}, u32[]{:S(2)}, u32[]{:S(2)}) %collective-permute-start.21) | collective-permute-done | bytes 589856 | tf_op jit(solution)/shard_map/ppermute | solution.py:77
  101.3 9.0 %shard_map.248 = (f32[256,768]{1,0:T(8,128)}, f32[256,768]{1,0:T(8,128)}, f32[256,768]{1,0:T(8,128)}, bf16[256,768]{1,0:T(8,128)(2,1)}, bf16[4,96,768]{2,1,0:T(8...) custom-call(s32[1]{0:T(128)} %bitcast.me_ref, ...), custom_call_target="tpu_custom_call" | custom-call | flops 1200000000 | bytes 3600000 | tf_op jit(solution)/shard_map/pallas_call | solution.py:141
  115.9 1.7 collective-permute-start.42
  117.6 1.2 add_convert_fusion.3.mine_ref
  120.5 9.7 %collective-permute-done.23.there_ref = bf16[256,768]{1,0:T(8,128)(2,1)S(1)} collective-permute-done((bf16[256,768]{1,0:T(8,128)(2,1)S(1)}, bf16[256,768]{1,0:T(8,128)(2,1)S(1)}, u32[]{:S(2)}, u32[]{:S(2)}) %collective-permute-start.23) | collective-permute-done | bytes 393248 | tf_op jit(solution)/shard_map/ppermute | solution.py:77
  130.2 1.1 copy-done.8
  134.9 8.4 %shard_map.250 = (bf16[4,96,768]{2,1,0:T(8,128)(2,1)S(1)}, bf16[4,96,768]{2,1,0:T(8,128)(2,1)}, f32[256,768]{1,0:T(8,128)S(1)}, bf16[256,768]{1,0:T(8,128)(2,1)S...) custom-call(s32[1]{0:T(128)} %bitcast.me_ref, s32[1]{0:T(128)} %bitcast.3.core_ref, s32[1]{0:T(128)} %bitcast.1.pair_ref, ...), custom_call_target="tpu_custom_call" | custom-call | flops 1200000000 | bytes 3600000 | tf_op jit(solution)/shard_map/pallas_call | solution.py:141
  144.8 1.6 collective-permute-start.44
  147.4 1.3 collective-permute-start.37
  150.4 2.1 %collective-permute-done.27 = f32[1,3,768]{2,1,0:T(4,128)S(1)} collective-permute-done((f32[1,3,768]{2,1,0:T(4,128)S(1)}, f32[1,3,768]{2,1,0:T(4,128)S(1)}, u32[]{:S(2)}, u32[]{:S(2)}) %collective-permute-start.27) | collective-permute-done | bytes 9248 | tf_op jit(solution)/shard_map/ppermute | solution.py:77
  152.5 6.9 %collective-permute-done.28 = bf16[4,96,768]{2,1,0:T(8,128)(2,1)} collective-permute-done((bf16[4,96,768]{2,1,0:T(8,128)(2,1)}, bf16[4,96,768]{2,1,0:T(8,128)(2,1)}, u32[]{:S(2)}, u32[]{:S(2)}) %collective-permute-start.28) | collective-permute-done | bytes 589856 | tf_op jit(solution)/shard_map/ppermute | solution.py:77
  159.4 2.0 add_convert_fusion.2
  162.2 3.7 %all-to-all-start.2 = ((bf16[16,36,128]{2,1,0:T(8,128)(2,1)}), bf16[16,36,128]{2,1,0:T(8,128)(2,1)S(1)}, u32[]{:S(2)}, u32[]{:S(2)}) async-start(bf16[16,36,128]{2,1,0:T(8,128)(2,1)} %broadcast_in_dim.170), calls=%async_computation.2 | async-start | bytes 327680 | tf_op jit(solution)/shard_map/all_to_all | solution.py:701
  168.0 1.1 add_convert_fusion.5
  170.2 2.8 %collective-permute-start.38 = (bf16[1,96,768]{2,1,0:T(8,128)(2,1)}, bf16[1,96,768]{2,1,0:T(8,128)(2,1)S(1)}, u32[]{:S(2)}, u32[]{:S(2)}) collective-permute-start(bf16[1,96,768]{2,1,0:T(8,128)(2,1)} %get-tuple-element.135), channel_id=1, source_target_pairs={{0,8},{1,9},{2,10},{3,11},{4,12},{5,13},{6,14},{7,15},{8,0},{9,1},... | collective-permute-start | bytes 442376 | tf_op jit(solution)/shard_map/ppermute | solution.py:77
  173.8 1.5 collective-permute-start.31
  176.3 1.7 add_bitcast_fusion
  178.9 2.6 %all-to-all-start.3 = ((f32[32,1,216]{2,1,0:T(1,128)}), f32[32,1,216]{2,1,0:T(1,128)S(1)}, u32[]{:S(2)}, u32[]{:S(2)}) async-start(f32[32,1,216]{2,1,0:T(1,128)} %all_to_all.34), calls=%async_computation.3 | async-start | bytes 65536 | tf_op jit(solution)/shard_map/all_to_all | solution.py:726
  183.2 1.8 collective-permute-done.31
  187.1 1.7 all-to-all-done.3
  189.6 1.2 collective-permute-start.41
  194.3 1.2 convert_add_fusion
  200.3 1.7 collective-permute-done.34.refs_2_
  (341 shorter events, 62.9 us)
Async XLA Ops:
  4.1 17.6 %collective-permute-start = (bf16[1,24,1344]{2,1,0:T(8,128)(2,1)S(1)}, bf16[1,24,1344]{2,1,0:T(8,128)(2,1)S(1)}, u32[]{:S(2)}, u32[]{:S(2)}) collective-permute-start(bf16[1,24,1344]{2,1,0:T(8,128)(2,1)S(1)} %get-tuple-element.151), channel_id=1, source_target_pairs={{0,1},{1,0},{2,3},{3,2},{4,5},{5,4},{6,7},{7,6},{8,9},{9,8},{10,11... | collective-permute-start | bytes 193544 | tf_op jit(solution)/shard_map/ppermute | solution.py:77
  4.7 17.1 %collective-permute-start.1 = (bf16[1,24,1344]{2,1,0:T(8,128)(2,1)S(1)}, bf16[1,24,1344]{2,1,0:T(8,128)(2,1)S(1)}, u32[]{:S(2)}, u32[]{:S(2)}) collective-permute-start(bf16[1,24,1344]{2,1,0:T(8,128)(2,1)S(1)} %get-tuple-element.150), channel_id=1, source_target_pairs={{0,16},{1,17},{2,18},{3,19},{4,20},{5,21},{6,22},{7,23},{8,24},{9,... | collective-permute-start | bytes 193544 | tf_op jit(solution)/shard_map/ppermute | solution.py:77
  7.2 14.5 %collective-permute-start.2 = (bf16[1,24,1344]{2,1,0:T(8,128)(2,1)S(1)}, bf16[1,24,1344]{2,1,0:T(8,128)(2,1)S(1)}, u32[]{:S(2)}, u32[]{:S(2)}) collective-permute-start(bf16[1,24,1344]{2,1,0:T(8,128)(2,1)S(1)} %get-tuple-element.149), channel_id=1, source_target_pairs={{0,17},{1,16},{2,19},{3,18},{4,21},{5,20},{6,23},{7,22},{8,25},{9,... | collective-permute-start | bytes 193544 | tf_op jit(solution)/shard_map/ppermute | solution.py:77
  8.8 12.7 %all-to-all-start = ((bf16[16,1,216]{2,1,0:T(2,128)(2,1)}), bf16[16,1,216]{2,1,0:T(2,128)(2,1)S(1)}, u32[]{:S(2)}, u32[]{:S(2)}) async-start(bf16[16,1,216]{2,1,0:T(2,128)(2,1)} %copy.78), calls=%async_computation | async-start | bytes 32768 | tf_op jit(solution)/shard_map/all_to_all | solution.py:588
  15.0 15.3 %collective-permute-start.3 = (bf16[1,120,768]{2,1,0:T(8,128)(2,1)S(1)}, bf16[1,120,768]{2,1,0:T(8,128)(2,1)S(1)}, u32[]{:S(2)}, u32[]{:S(2)}) collective-permute-start(bf16[1,120,768]{2,1,0:T(8,128)(2,1)S(1)} %maximum_bitcast_fusion), channel_id=1, source_target_pairs={{0,8},{1,9},{2,10},{3,11},{4,12},{5,13},{6,14},{7,15},{8,0},{9,1},... | collective-permute-start | bytes 552968 | tf_op jit(solution)/shard_map/ppermute | solution.py:77
  18.0 15.6 %collective-permute-start.6 = (bf16[2,1,128,768]{3,2,1,0:T(8,128)(2,1)S(1)}, bf16[2,1,128,768]{3,2,1,0:T(8,128)(2,1)S(1)}, u32[]{:S(2)}, u32[]{:S(2)}) collective-permute-start(bf16[2,1,128,768]{3,2,1,0:T(8,128)(2,1)S(1)} %pad_maximum_fusion.1.own_ref), channel_id=1, source_target_pairs={{0,16},{1,17},{2,18},{3,19},{4,20},{5,21},{6,22},{7,23},{8,24},{9,... | collective-permute-start | bytes 1179656 | tf_op jit(solution)/shard_map/ppermute | solution.py:77
  22.1 10.5 %collective-permute-start.5 = (bf16[1,2,48,576]{3,2,1,0:T(8,128)(2,1)S(1)}, bf16[1,2,48,576]{3,2,1,0:T(8,128)(2,1)S(1)}, u32[]{:S(2)}, u32[]{:S(2)}) collective-permute-start(bf16[1,2,48,576]{3,2,1,0:T(8,128)(2,1)S(1)} %bitcast.219), channel_id=1, source_target_pairs={{0,8},{1,9},{2,10},{3,11},{4,12},{5,13},{6,14},{7,15},{8,0},{9,1},... | collective-permute-start | bytes 331784 | tf_op jit(solution)/shard_map/ppermute | solution.py:77
  31.7 1.9 collective-permute-start.4
  33.4 12.1 %collective-permute-start.10 = (bf16[2,120,768]{2,1,0:T(8,128)(2,1)}, bf16[2,120,768]{2,1,0:T(8,128)(2,1)}, u32[]{:S(2)}, u32[]{:S(2)}) collective-permute-start(bf16[2,120,768]{2,1,0:T(8,128)(2,1)} %pad_maximum_fusion.2), channel_id=1, source_target_pairs={{0,4},{1,5},{2,6},{3,7},{4,0},{5,1},{6,2},{7,3},{8,12},{9,13},{10,... | collective-permute-start | bytes 1105928 | tf_op jit(solution)/shard_map/ppermute | solution.py:77
  34.8 17.7 %all-to-all-start.1 = ((f32[16,1,4608]{2,1,0:T(1,128)}), f32[16,1,4608]{2,1,0:T(1,128)S(1)}, u32[]{:S(2)}, u32[]{:S(2)}) async-start(f32[16,1,4608]{2,1,0:T(1,128)} %all_to_all.30), calls=%async_computation.1 | async-start | bytes 589824 | tf_op jit(solution)/shard_map/all_to_all | solution.py:80
  41.8 13.2 %collective-permute-start.7 = (bf16[2,2,48,576]{3,2,1,0:T(8,128)(2,1)}, bf16[2,2,48,576]{3,2,1,0:T(8,128)(2,1)}, u32[]{:S(2)}, u32[]{:S(2)}) collective-permute-start(bf16[2,2,48,576]{3,2,1,0:T(8,128)(2,1)} %pad_maximum_fusion.9), channel_id=1, source_target_pairs={{0,4},{1,5},{2,6},{3,7},{4,0},{5,1},{6,2},{7,3},{8,12},{9,13},{10,... | collective-permute-start | bytes 663560 | tf_op jit(solution)/shard_map/ppermute | solution.py:77
  43.6 23.8 %collective-permute-start.8 = (bf16[2,1,256,768]{3,2,1,0:T(8,128)(2,1)S(1)}, bf16[2,1,256,768]{3,2,1,0:T(8,128)(2,1)S(1)}, u32[]{:S(2)}, u32[]{:S(2)}) collective-permute-start(bf16[2,1,256,768]{3,2,1,0:T(8,128)(2,1)S(1)} %bitcast.186), channel_id=1, source_target_pairs={{0,1},{1,0},{2,3},{3,2},{4,5},{5,4},{6,7},{7,6},{8,9},{9,8},{10,11... | collective-permute-start | bytes 2359304 | tf_op jit(solution)/shard_map/ppermute | solution.py:77
  46.6 22.2 %collective-permute-start.11 = (bf16[4,120,768]{2,1,0:T(8,128)(2,1)S(1)}, bf16[4,120,768]{2,1,0:T(8,128)(2,1)}, u32[]{:S(2)}, u32[]{:S(2)}) collective-permute-start(bf16[4,120,768]{2,1,0:T(8,128)(2,1)S(1)} %pad_maximum_fusion.refs_11_), channel_id=1, source_target_pairs={{0,2},{1,3},{2,0},{3,1},{4,6},{5,7},{6,4},{7,5},{8,10},{9,11},{10,... | collective-permute-start | bytes 2211848 | tf_op jit(solution)/shard_map/ppermute | solution.py:77
  56.6 9.1 %collective-permute-start.12 = (bf16[1,2,48,768]{3,2,1,0:T(8,128)(2,1)S(1)}, bf16[1,2,48,768]{3,2,1,0:T(8,128)(2,1)S(1)}, u32[]{:S(2)}, u32[]{:S(2)}) collective-permute-start(bf16[1,2,48,768]{3,2,1,0:T(8,128)(2,1)S(1)} %bitcast.216), channel_id=1, source_target_pairs={{0,8},{1,9},{2,10},{3,11},{4,12},{5,13},{6,14},{7,15},{8,0},{9,1},... | collective-permute-start | bytes 442376 | tf_op jit(solution)/shard_map/ppermute | solution.py:77
  57.9 18.7 %collective-permute-start.14 = (bf16[4,2,48,576]{3,2,1,0:T(8,128)(2,1)}, bf16[4,2,48,576]{3,2,1,0:T(8,128)(2,1)}, u32[]{:S(2)}, u32[]{:S(2)}) collective-permute-start(bf16[4,2,48,576]{3,2,1,0:T(8,128)(2,1)} %constant_dynamic-update-slice_fusion.own_w_ref), channel_id=1, source_target_pairs={{0,2},{1,3},{2,0},{3,1},{4,6},{5,7},{6,4},{7,5},{8,10},{9,11},{10,... | collective-permute-start | bytes 1327112 | tf_op jit(solution)/shard_map/ppermute | solution.py:77
  59.5 3.6 %collective-permute-start.20 = (bf16[16,48]{1,0:T(8,128)(2,1)S(1)}, bf16[16,48]{1,0:T(8,128)(2,1)S(1)}, u32[]{:S(2)}, u32[]{:S(2)}) collective-permute-start(bf16[16,48]{1,0:T(8,128)(2,1)S(1)} %slice.173), channel_id=1, source_target_pairs={{0,16},{1,17},{2,18},{3,19},{4,20},{5,21},{6,22},{7,23},{8,24},{9,... | collective-permute-start | bytes 4616 | tf_op jit(solution)/shard_map/ppermute | solution.py:77
  66.4 9.2 %collective-permute-start.13 = (bf16[2,2,48,768]{3,2,1,0:T(8,128)(2,1)}, bf16[2,2,48,768]{3,2,1,0:T(8,128)(2,1)}, u32[]{:S(2)}, u32[]{:S(2)}) collective-permute-start(bf16[2,2,48,768]{3,2,1,0:T(8,128)(2,1)} %constant_dynamic-update-slice_fusion.2), channel_id=1, source_target_pairs={{0,4},{1,5},{2,6},{3,7},{4,0},{5,1},{6,2},{7,3},{8,12},{9,13},{10,... | collective-permute-start | bytes 884744 | tf_op jit(solution)/shard_map/ppermute | solution.py:77
  68.7 7.9 %collective-permute-start.9 = (f32[2,1,3,768]{3,2,1,0:T(4,128)S(1)}, f32[2,1,3,768]{3,2,1,0:T(4,128)S(1)}, u32[]{:S(2)}, u32[]{:S(2)}) collective-permute-start(f32[2,1,3,768]{3,2,1,0:T(4,128)S(1)} %bitcast.193), channel_id=1, source_target_pairs={{0,1},{1,0},{2,3},{3,2},{4,5},{5,4},{6,7},{7,6},{8,9},{9,8},{10,11... | collective-permute-start | bytes 55304 | tf_op jit(solution)/shard_map/ppermute | solution.py:77
  69.7 14.8 %collective-permute-start.18 = (bf16[8,24,768]{2,1,0:T(8,128)(2,1)S(1)}, bf16[8,24,768]{2,1,0:T(8,128)(2,1)S(1)}, u32[]{:S(2)}, u32[]{:S(2)}) collective-permute-start(bf16[8,24,768]{2,1,0:T(8,128)(2,1)S(1)} %bitcast.191), channel_id=1, source_target_pairs={{0,16},{1,17},{2,18},{3,19},{4,20},{5,21},{6,22},{7,23},{8,24},{9,... | collective-permute-start | bytes 884744 | tf_op jit(solution)/shard_map/ppermute | solution.py:77
  83.1 7.4 %collective-permute-start.16 = (bf16[512,192]{1,0:T(8,128)(2,1)S(1)}, bf16[512,192]{1,0:T(8,128)(2,1)S(1)}, u32[]{:S(2)}, u32[]{:S(2)}) collective-permute-start(bf16[512,192]{1,0:T(8,128)(2,1)S(1)} %get-tuple-element.75.refs_0_.att_ref), channel_id=1, source_target_pairs={{0,16},{1,17},{2,18},{3,19},{4,20},{5,21},{6,22},{7,23},{8,24},{9,... | collective-permute-start | bytes 589832 | tf_op jit(solution)/shard_map/ppermute | solution.py:77
  85.3 6.4 %collective-permute-start.19 = (bf16[2,8,24,768]{3,2,1,0:T(8,128)(2,1)}, bf16[2,8,24,768]{3,2,1,0:T(8,128)(2,1)}, u32[]{:S(2)}, u32[]{:S(2)}) collective-permute-start(bf16[2,8,24,768]{3,2,1,0:T(8,128)(2,1)} %bitcast_dynamic-update-slice_fusion.2), channel_id=1, source_target_pairs={{0,1},{1,0},{2,3},{3,2},{4,5},{5,4},{6,7},{7,6},{8,9},{9,8},{10,11... | collective-permute-start | bytes 1769480 | tf_op jit(solution)/shard_map/ppermute | solution.py:77
  85.5 15.8 %collective-permute-start.21 = (bf16[4,2,48,768]{3,2,1,0:T(8,128)(2,1)S(1)}, bf16[4,2,48,768]{3,2,1,0:T(8,128)(2,1)S(1)}, u32[]{:S(2)}, u32[]{:S(2)}) collective-permute-start(bf16[4,2,48,768]{3,2,1,0:T(8,128)(2,1)S(1)} %constant_dynamic-update-slice_fusion.4.refs_9_), channel_id=1, source_target_pairs={{0,2},{1,3},{2,0},{3,1},{4,6},{5,7},{6,4},{7,5},{8,10},{9,11},{10,... | collective-permute-start | bytes 1769480 | tf_op jit(solution)/shard_map/ppermute | solution.py:77
  87.3 5.5 %collective-permute-start.15 = (bf16[512,192]{1,0:T(8,128)(2,1)S(1)}, bf16[512,192]{1,0:T(8,128)(2,1)S(1)}, u32[]{:S(2)}, u32[]{:S(2)}) collective-permute-start(bf16[512,192]{1,0:T(8,128)(2,1)S(1)} %get-tuple-element.75.refs_0_.att_ref), channel_id=1, source_target_pairs={{0,1},{1,0},{2,3},{3,2},{4,5},{5,4},{6,7},{7,6},{8,9},{9,8},{10,11... | collective-permute-start | bytes 589832 | tf_op jit(solution)/shard_map/ppermute | solution.py:77
  90.5 2.4 %collective-permute-start.17 = (bf16[512,192]{1,0:T(8,128)(2,1)S(1)}, bf16[512,192]{1,0:T(8,128)(2,1)S(1)}, u32[]{:S(2)}, u32[]{:S(2)}) collective-permute-start(bf16[512,192]{1,0:T(8,128)(2,1)S(1)} %collective-permute-done.16.refs_2_), channel_id=1, source_target_pairs={{0,1},{1,0},{2,3},{3,2},{4,5},{5,4},{6,7},{7,6},{8,9},{9,8},{10,11... | collective-permute-start | bytes 589832 | tf_op jit(solution)/shard_map/ppermute | solution.py:77
  114.4 3.3 %collective-permute-start.22 = (bf16[256,768]{1,0:T(8,128)(2,1)}, bf16[256,768]{1,0:T(8,128)(2,1)S(1)}, u32[]{:S(2)}, u32[]{:S(2)}) collective-permute-start(bf16[256,768]{1,0:T(8,128)(2,1)} %get-tuple-element.81), channel_id=1, source_target_pairs={{0,1},{1,0},{2,3},{3,2},{4,5},{5,4},{6,7},{7,6},{8,9},{9,8},{10,11... | collective-permute-start | bytes 1179656 | tf_op jit(solution)/shard_map/ppermute | solution.py:77
  115.9 17.2 %collective-permute-start.42 = (bf16[384,768]{1,0:T(8,128)(2,1)}, bf16[384,768]{1,0:T(8,128)(2,1)S(1)}, u32[]{:S(2)}, u32[]{:S(2)}) collective-permute-start(bf16[384,768]{1,0:T(8,128)(2,1)} %copy-done.22), channel_id=1, source_target_pairs={{0,2},{1,3},{2,0},{3,1},{4,6},{5,7},{6,4},{7,5},{8,10},{9,11},{10,... | collective-permute-start | bytes 1769480 | tf_op jit(solution)/shard_map/ppermute | solution.py:77
  118.9 11.3 %collective-permute-start.23 = (bf16[256,768]{1,0:T(8,128)(2,1)S(1)}, bf16[256,768]{1,0:T(8,128)(2,1)S(1)}, u32[]{:S(2)}, u32[]{:S(2)}) collective-permute-start(bf16[256,768]{1,0:T(8,128)(2,1)S(1)} %add_convert_fusion.3.mine_ref), channel_id=1, source_target_pairs={{0,16},{1,17},{2,18},{3,19},{4,20},{5,21},{6,22},{7,23},{8,24},{9,... | collective-permute-start | bytes 1179656 | tf_op jit(solution)/shard_map/ppermute | solution.py:77
  120.0 26.4 %collective-permute-start.36 = (bf16[4,96,768]{2,1,0:T(8,128)(2,1)}, bf16[4,96,768]{2,1,0:T(8,128)(2,1)S(1)}, u32[]{:S(2)}, u32[]{:S(2)}) collective-permute-start(bf16[4,96,768]{2,1,0:T(8,128)(2,1)} %copy-done.21), channel_id=1, source_target_pairs={{0,2},{1,3},{2,0},{3,1},{4,6},{5,7},{6,4},{7,5},{8,10},{9,11},{10,... | collective-permute-start | bytes 1769480 | tf_op jit(solution)/shard_map/ppermute | solution.py:77
  120.4 28.3 %collective-permute-start.25 = (bf16[256,768]{1,0:T(8,128)(2,1)}, bf16[256,768]{1,0:T(8,128)(2,1)S(1)}, u32[]{:S(2)}, u32[]{:S(2)}) collective-permute-start(bf16[256,768]{1,0:T(8,128)(2,1)} %copy-done.23), channel_id=1, source_target_pairs={{0,1},{1,0},{2,3},{3,2},{4,5},{5,4},{6,7},{7,6},{8,9},{9,8},{10,11... | collective-permute-start | bytes 1179656 | tf_op jit(solution)/shard_map/ppermute | solution.py:77
  133.4 10.6 %collective-permute-start.43 = (bf16[2,96,768]{2,1,0:T(8,128)(2,1)S(1)}, bf16[2,96,768]{2,1,0:T(8,128)(2,1)S(1)}, u32[]{:S(2)}, u32[]{:S(2)}) collective-permute-start(bf16[2,96,768]{2,1,0:T(8,128)(2,1)S(1)} %get-tuple-element.129), channel_id=1, source_target_pairs={{0,4},{1,5},{2,6},{3,7},{4,0},{5,1},{6,2},{7,3},{8,12},{9,13},{10,... | collective-permute-start | bytes 884744 | tf_op jit(solution)/shard_map/ppermute | solution.py:77
  143.3 5.4 %collective-permute-start.26 = (f32[1,3,768]{2,1,0:T(4,128)S(1)}, f32[1,3,768]{2,1,0:T(4,128)S(1)}, u32[]{:S(2)}, u32[]{:S(2)}) collective-permute-start(f32[1,3,768]{2,1,0:T(4,128)S(1)} %pad_maximum_fusion.11), channel_id=1, source_target_pairs={{0,1},{1,0},{2,3},{3,2},{4,5},{5,4},{6,7},{7,6},{8,9},{9,8},{10,11... | collective-permute-start | bytes 27656 | tf_op jit(solution)/shard_map/ppermute | solution.py:77
  143.6 15.8 %collective-permute-start.28 = (bf16[4,96,768]{2,1,0:T(8,128)(2,1)}, bf16[4,96,768]{2,1,0:T(8,128)(2,1)}, u32[]{:S(2)}, u32[]{:S(2)}) collective-permute-start(bf16[4,96,768]{2,1,0:T(8,128)(2,1)} %get-tuple-element.95), channel_id=1, source_target_pairs={{0,2},{1,3},{2,0},{3,1},{4,6},{5,7},{6,4},{7,5},{8,10},{9,11},{10,... | collective-permute-start | bytes 1769480 | tf_op jit(solution)/shard_map/ppermute | solution.py:77
  144.8 31.5 %collective-permute-start.44 = (bf16[1,96,768]{2,1,0:T(8,128)(2,1)}, bf16[1,96,768]{2,1,0:T(8,128)(2,1)}, u32[]{:S(2)}, u32[]{:S(2)}) collective-permute-start(bf16[1,96,768]{2,1,0:T(8,128)(2,1)} %get-tuple-element.133), channel_id=1, source_target_pairs={{0,8},{1,9},{2,10},{3,11},{4,12},{5,13},{6,14},{7,15},{8,0},{9,1},... | collective-permute-start | bytes 442376 | tf_op jit(solution)/shard_map/ppermute | solution.py:77
  147.4 20.5 %collective-permute-start.37 = (bf16[2,96,768]{2,1,0:T(8,128)(2,1)}, bf16[2,96,768]{2,1,0:T(8,128)(2,1)}, u32[]{:S(2)}, u32[]{:S(2)}) collective-permute-start(bf16[2,96,768]{2,1,0:T(8,128)(2,1)} %get-tuple-element.131), channel_id=1, source_target_pairs={{0,4},{1,5},{2,6},{3,7},{4,0},{5,1},{6,2},{7,3},{8,12},{9,13},{10,... | collective-permute-start | bytes 884744 | tf_op jit(solution)/shard_map/ppermute | solution.py:77
  148.7 17.2 %collective-permute-start.29 = (bf16[256,768]{1,0:T(8,128)(2,1)S(1)}, bf16[256,768]{1,0:T(8,128)(2,1)}, u32[]{:S(2)}, u32[]{:S(2)}) collective-permute-start(bf16[256,768]{1,0:T(8,128)(2,1)S(1)} %get-tuple-element.98), channel_id=1, source_target_pairs={{0,1},{1,0},{2,3},{3,2},{4,5},{5,4},{6,7},{7,6},{8,9},{9,8},{10,11... | collective-permute-start | bytes 1179656 | tf_op jit(solution)/shard_map/ppermute | solution.py:77
  148.7 3.8 %collective-permute-start.27 = (f32[1,3,768]{2,1,0:T(4,128)S(1)}, f32[1,3,768]{2,1,0:T(4,128)S(1)}, u32[]{:S(2)}, u32[]{:S(2)}) collective-permute-start(f32[1,3,768]{2,1,0:T(4,128)S(1)} %fusion.30), channel_id=1, source_target_pairs={{0,16},{1,17},{2,18},{3,19},{4,20},{5,21},{6,22},{7,23},{8,24},{9,... | collective-permute-start | bytes 27656 | tf_op jit(solution)/shard_map/ppermute | solution.py:77
  162.2 15.8 %all-to-all-start.2 = ((bf16[16,36,128]{2,1,0:T(8,128)(2,1)}), bf16[16,36,128]{2,1,0:T(8,128)(2,1)S(1)}, u32[]{:S(2)}, u32[]{:S(2)}) async-start(bf16[16,36,128]{2,1,0:T(8,128)(2,1)} %broadcast_in_dim.170), calls=%async_computation.2 | async-start | bytes 327680 | tf_op jit(solution)/shard_map/all_to_all | solution.py:701
  170.2 18.6 %collective-permute-start.38 = (bf16[1,96,768]{2,1,0:T(8,128)(2,1)}, bf16[1,96,768]{2,1,0:T(8,128)(2,1)S(1)}, u32[]{:S(2)}, u32[]{:S(2)}) collective-permute-start(bf16[1,96,768]{2,1,0:T(8,128)(2,1)} %get-tuple-element.135), channel_id=1, source_target_pairs={{0,8},{1,9},{2,10},{3,11},{4,12},{5,13},{6,14},{7,15},{8,0},{9,1},... | collective-permute-start | bytes 442376 | tf_op jit(solution)/shard_map/ppermute | solution.py:77
  173.8 11.2 %collective-permute-start.31 = (bf16[2,96,768]{2,1,0:T(8,128)(2,1)}, bf16[2,96,768]{2,1,0:T(8,128)(2,1)}, u32[]{:S(2)}, u32[]{:S(2)}) collective-permute-start(bf16[2,96,768]{2,1,0:T(8,128)(2,1)} %dynamic-slice_bitcast_fusion.4), channel_id=1, source_target_pairs={{0,4},{1,5},{2,6},{3,7},{4,0},{5,1},{6,2},{7,3},{8,12},{9,13},{10,... | collective-permute-start | bytes 884744 | tf_op jit(solution)/shard_map/ppermute | solution.py:77
  175.2 19.1 %collective-permute-start.30 = (bf16[1,2,1,128,768]{4,3,2,1,0:T(8,128)(2,1)}, bf16[1,2,1,128,768]{4,3,2,1,0:T(8,128)(2,1)}, u32[]{:S(2)}, u32[]{:S(2)}) collective-permute-start(bf16[1,2,1,128,768]{4,3,2,1,0:T(8,128)(2,1)} %fusion.15), channel_id=1, source_target_pairs={{0,16},{1,17},{2,18},{3,19},{4,20},{5,21},{6,22},{7,23},{8,24},{9,... | collective-permute-start | bytes 1179656 | tf_op jit(solution)/shard_map/ppermute | solution.py:77
  178.9 9.9 %all-to-all-start.3 = ((f32[32,1,216]{2,1,0:T(1,128)}), f32[32,1,216]{2,1,0:T(1,128)S(1)}, u32[]{:S(2)}, u32[]{:S(2)}) async-start(f32[32,1,216]{2,1,0:T(1,128)} %all_to_all.34), calls=%async_computation.3 | async-start | bytes 65536 | tf_op jit(solution)/shard_map/all_to_all | solution.py:726
  186.0 11.4 %collective-permute-start.32 = (bf16[1,96,768]{2,1,0:T(8,128)(2,1)S(1)}, bf16[1,96,768]{2,1,0:T(8,128)(2,1)S(1)}, u32[]{:S(2)}, u32[]{:S(2)}) collective-permute-start(bf16[1,96,768]{2,1,0:T(8,128)(2,1)S(1)} %get-tuple-element.141), channel_id=1, source_target_pairs={{0,8},{1,9},{2,10},{3,11},{4,12},{5,13},{6,14},{7,15},{8,0},{9,1},... | collective-permute-start | bytes 442376 | tf_op jit(solution)/shard_map/ppermute | solution.py:77
  188.8 3.9 %collective-permute-start.39 = (bf16[24,768]{1,0:T(8,128)(2,1)S(1)}, bf16[24,768]{1,0:T(8,128)(2,1)S(1)}, u32[]{:S(2)}, u32[]{:S(2)}) collective-permute-start(bf16[24,768]{1,0:T(8,128)(2,1)S(1)} %get-tuple-element.162), channel_id=1, source_target_pairs={{0,1},{1,0},{2,3},{3,2},{4,5},{5,4},{6,7},{7,6},{8,9},{9,8},{10,11... | collective-permute-start | bytes 110600 | tf_op jit(solution)/shard_map/ppermute | solution.py:77
  189.0 4.4 %collective-permute-start.40 = (bf16[24,768]{1,0:T(8,128)(2,1)S(1)}, bf16[24,768]{1,0:T(8,128)(2,1)S(1)}, u32[]{:S(2)}, u32[]{:S(2)}) collective-permute-start(bf16[24,768]{1,0:T(8,128)(2,1)S(1)} %get-tuple-element.161), channel_id=1, source_target_pairs={{0,16},{1,17},{2,18},{3,19},{4,20},{5,21},{6,22},{7,23},{8,24},{9,... | collective-permute-start | bytes 110600 | tf_op jit(solution)/shard_map/ppermute | solution.py:77
  189.6 3.8 %collective-permute-start.41 = (bf16[24,768]{1,0:T(8,128)(2,1)S(1)}, bf16[24,768]{1,0:T(8,128)(2,1)S(1)}, u32[]{:S(2)}, u32[]{:S(2)}) collective-permute-start(bf16[24,768]{1,0:T(8,128)(2,1)S(1)} %get-tuple-element.160), channel_id=1, source_target_pairs={{0,17},{1,16},{2,19},{3,18},{4,21},{5,20},{6,23},{7,22},{8,25},{9,... | collective-permute-start | bytes 110600 | tf_op jit(solution)/shard_map/ppermute | solution.py:77
  197.5 2.7 %collective-permute-start.33 = (bf16[24,576]{1,0:T(8,128)(2,1)S(1)}, bf16[24,576]{1,0:T(8,128)(2,1)S(1)}, u32[]{:S(2)}, u32[]{:S(2)}) collective-permute-start(bf16[24,576]{1,0:T(8,128)(2,1)S(1)} %get-tuple-element.166), channel_id=1, source_target_pairs={{0,1},{1,0},{2,3},{3,2},{4,5},{5,4},{6,7},{7,6},{8,9},{9,8},{10,11... | collective-permute-start | bytes 82952 | tf_op jit(solution)/shard_map/ppermute | solution.py:77
  198.1 3.9 %collective-permute-start.34 = (bf16[24,576]{1,0:T(8,128)(2,1)S(1)}, bf16[24,576]{1,0:T(8,128)(2,1)S(1)}, u32[]{:S(2)}, u32[]{:S(2)}) collective-permute-start(bf16[24,576]{1,0:T(8,128)(2,1)S(1)} %get-tuple-element.165), channel_id=1, source_target_pairs={{0,16},{1,17},{2,18},{3,19},{4,20},{5,21},{6,22},{7,23},{8,24},{9,... | collective-permute-start | bytes 82952 | tf_op jit(solution)/shard_map/ppermute | solution.py:77
  199.2 3.6 %collective-permute-start.35 = (bf16[24,576]{1,0:T(8,128)(2,1)S(1)}, bf16[24,576]{1,0:T(8,128)(2,1)S(1)}, u32[]{:S(2)}, u32[]{:S(2)}) collective-permute-start(bf16[24,576]{1,0:T(8,128)(2,1)S(1)} %get-tuple-element.164), channel_id=1, source_target_pairs={{0,17},{1,16},{2,19},{3,18},{4,21},{5,20},{6,23},{7,22},{8,25},{9,... | collective-permute-start | bytes 82952 | tf_op jit(solution)/shard_map/ppermute | solution.py:77
  (56 other events, 385.7 us)

commit v5 on v4

--- a/solution.py
+++ b/solution.py
@@ -630,7 +630,7 @@
     qkv_own = steps[-1]
     qkv_other = link.send(qkv_own, pair_bit)
     other_acts = link.send(acts, core_bit)
-    fc1_steps = [after(team_fc1, steps[2])]
+    fc1_steps = [after(team_fc1, steps[1])]
     for bit in high_bits:
         fc1_steps.append(link.gather_step(fc1_steps[-1], bit, (qkv_own,)))
     fc1_own = fc1_steps[-1]
@@ -643,7 +643,13 @@
     half_proj = full_proj
     full_proj = link.gather(full_proj.reshape(rest, rows, width), seq_bits, 0)
     full_proj = link.gather(full_proj, core_bit, 2).reshape(team, group, width)
-    bias_out = link.gather(after(biases, qkv_own)[:, 2 * rows : 4 * rows], seq_bits, 0)
+    mod, h_attn, qkv, attended, my_qkv = attend(
+        core, pair, spot, modulation, link.send(modulation, core_bit), acts, other_acts,
+        after(qkv_own, half_proj, fc1_own),
+        qkv_other, bias_qkv,
+    )
+
+    bias_out = link.gather(after(biases, attended)[:, 2 * rows : 4 * rows], seq_bits, 0)
     bias_proj, bias_fc2 = (
         bias_out[:, :, at * rows : (at + 1) * rows].reshape(1, width).astype(F32) for at in range(2)
     )
@@ -654,12 +660,6 @@
             for bias in (bias_proj, bias_fc1, bias_fc2 * (1.0 / team))
         ],
         axis=0,
-    )
-
-    mod, h_attn, qkv, attended, my_qkv = attend(
-        core, pair, spot, modulation, link.send(modulation, core_bit), acts, other_acts,
-        after(qkv_own, half_proj, fc1_own),
-        qkv_other, bias_qkv,
     )
 
     near = link.send(attended, core_bit)

time: 205 us -> 200 us (0.976)
  waiting for transfers between devices: 57.7 us -> 52.1 us
  starting transfers between devices: 58.1 us -> 60.7 us
    ppermute x45, waiting for transfers between devices: 51.6 us -> 45.5 us  [send(): lax.ppermute(value, AXES, [(i, i ^ mask) for i in range(self.devices)])]
    ppermute x45, starting transfers between devices: 38.9 us -> 41.6 us  [send(): lax.ppermute(value, AXES, [(i, i ^ mask) for i in range(self.devices)])]
    unnamed x118 -> x98, local copies, waits for them, and re-layouts: 13.2 us -> 15.7 us
  transfers between devices with their start and end apart: 49 -> 49, of which waited for: 18 -> 20; matrix products, arithmetic and copies ran while one was open for 24% -> 22% of each run, Pallas kernels for 7% -> 7%
where the time goes in v5:
time: 200 us; the launch traced here: 199 us
  starting transfers between devices  60.7 us (30%)
  waiting for transfers between devices  52.1 us (26%)
  local copies, waits for them, and re-layouts  36.2 us (18%)
  Pallas kernels  24 us (12%)
  other arithmetic  22.7 us (11%)
    ppermute x45, waiting for transfers between devices, send(): lax.ppermute(value, AXES, [(i, i ^ mask) for i in range(self.devices)])  45.5 us
    ppermute x45, starting transfers between devices, send(): lax.ppermute(value, AXES, [(i, i ^ mask) for i in range(self.devices)])  41.6 us
    pallas_call x8, Pallas kernels, call(): pl.pallas_call(kernel, out_shape=[jax.ShapeDtypeStruct(shape, dtype) for...  24 us
    unnamed x98, local copies, waits for them, and re-layouts  15.7 us
    all_to_all x1, starting transfers between devices, all_to_all(): lax.all_to_all(value, AXES, 0, 0, tiled=True, axis_index_groups=self.grou...  6.76 us
    all_to_all x1, starting transfers between devices, local(): from_all = lax.all_to_all(to_all, 'fsdp', 0, 0, tiled=True)  6.17 us
  transfers between devices with their start and end apart: 49, of which 20 were waited for; matrix products, arithmetic and copies ran while one was open for 22% of the time, Pallas kernels for 7%

profile of v5, /device:TPU:0, one launch (start us, length us, event | category | flops | bytes accessed | tf_op | source)
XLA Modules:
  0.0 198.8 jit_solution(9348470489792684740)
XLA Ops:
  0.7 1.2 reshape.521
  4.7 2.6 %collective-permute-start.1 = (bf16[1,24,1344]{2,1,0:T(8,128)(2,1)S(1)}, bf16[1,24,1344]{2,1,0:T(8,128)(2,1)S(1)}, u32[]{:S(2)}, u32[]{:S(2)}) collective-permute-start(bf16[1,24,1344]{2,1,0:T(8,128)(2,1)S(1)} %get-tuple-element.150), channel_id=1, source_target_pairs={{0,16},{1,17},{2,18},{3,19},{4,20},{5,21},{6,22},{7,23},{8,24},{9,... | collective-permute-start | bytes 193544 | tf_op jit(solution)/shard_map/ppermute | solution.py:77
  8.2 6.2 %all-to-all-start = ((bf16[16,1,216]{2,1,0:T(2,128)(2,1)}), bf16[16,1,216]{2,1,0:T(2,128)(2,1)S(1)}, u32[]{:S(2)}, u32[]{:S(2)}) async-start(bf16[16,1,216]{2,1,0:T(2,128)(2,1)} %copy.78), calls=%async_computation | async-start | bytes 32768 | tf_op jit(solution)/shard_map/all_to_all | solution.py:588
  14.5 2.9 %collective-permute-start.3 = (bf16[1,120,768]{2,1,0:T(8,128)(2,1)S(1)}, bf16[1,120,768]{2,1,0:T(8,128)(2,1)S(1)}, u32[]{:S(2)}, u32[]{:S(2)}) collective-permute-start(bf16[1,120,768]{2,1,0:T(8,128)(2,1)S(1)} %maximum_bitcast_fusion), channel_id=1, source_target_pairs={{0,8},{1,9},{2,10},{3,11},{4,12},{5,13},{6,14},{7,15},{8,0},{9,1},... | collective-permute-start | bytes 552968 | tf_op jit(solution)/shard_map/ppermute | solution.py:77
  17.4 1.6 collective-permute-start.6
  19.5 1.5 all-to-all-done
  22.3 7.5 %collective-permute-done.3 = bf16[1,120,768]{2,1,0:T(8,128)(2,1)S(1)} collective-permute-done((bf16[1,120,768]{2,1,0:T(8,128)(2,1)S(1)}, bf16[1,120,768]{2,1,0:T(8,128)(2,1)S(1)}, u32[]{:S(2)}, u32[]{:S(2)}) %collective-permute-start.3) | collective-permute-done | bytes 184352 | tf_op jit(solution)/shard_map/ppermute | solution.py:77
  34.2 6.8 %all-to-all-start.1 = ((f32[16,1,4608]{2,1,0:T(1,128)}), f32[16,1,4608]{2,1,0:T(1,128)S(1)}, u32[]{:S(2)}, u32[]{:S(2)}) async-start(f32[16,1,4608]{2,1,0:T(1,128)} %all_to_all.30), calls=%async_computation.1 | async-start | bytes 589824 | tf_op jit(solution)/shard_map/all_to_all | solution.py:80
  42.0 1.7 collective-permute-start.7
  43.7 2.4 %collective-permute-start.12 = (bf16[1,2,48,768]{3,2,1,0:T(8,128)(2,1)}, bf16[1,2,48,768]{3,2,1,0:T(8,128)(2,1)}, u32[]{:S(2)}, u32[]{:S(2)}) collective-permute-start(bf16[1,2,48,768]{3,2,1,0:T(8,128)(2,1)} %bitcast.35), channel_id=1, source_target_pairs={{0,8},{1,9},{2,10},{3,11},{4,12},{5,13},{6,14},{7,15},{8,0},{9,1},... | collective-permute-start | bytes 442376 | tf_op jit(solution)/shard_map/ppermute | solution.py:77
  47.2 1.5 collective-permute-start.11
  48.7 3.3 %all-to-all-done.1 = f32[16,1,4608]{2,1,0:T(1,128)S(1)} async-done(((f32[16,1,4608]{2,1,0:T(1,128)}), f32[16,1,4608]{2,1,0:T(1,128)S(1)}, u32[]{:S(2)}, u32[]{:S(2)}) %all-to-all-start.1) | async-done | bytes 294944 | tf_op jit(solution)/shard_map/all_to_all | solution.py:80
  52.8 1.7 constant_dynamic-update-slice_fusion.1
  54.4 2.1 %collective-permute-done.7 = bf16[2,2,48,576]{3,2,1,0:T(8,128)(2,1)S(1)} collective-permute-done((bf16[2,2,48,576]{3,2,1,0:T(8,128)(2,1)}, bf16[2,2,48,576]{3,2,1,0:T(8,128)(2,1)S(1)}, u32[]{:S(2)}, u32[]{:S(2)}) %collective-permute-start.7) | collective-permute-done | bytes 221216 | tf_op jit(solution)/shard_map/ppermute | solution.py:77
  57.3 1.6 constant_dynamic-update-slice_fusion.3
  58.9 1.6 constant_dynamic-update-slice_fusion.2
  60.5 1.8 collective-permute-start.14
  63.3 1.2 reduce_sum.72
  64.6 4.5 %collective-permute-done.13 = bf16[2,2,48,768]{3,2,1,0:T(8,128)(2,1)} collective-permute-done((bf16[2,2,48,768]{3,2,1,0:T(8,128)(2,1)}, bf16[2,2,48,768]{3,2,1,0:T(8,128)(2,1)}, u32[]{:S(2)}, u32[]{:S(2)}) %collective-permute-start.13) | collective-permute-done | bytes 294944 | tf_op jit(solution)/shard_map/ppermute | solution.py:77
  70.1 2.0 collective-permute-start.21
  73.0 1.5 collective-permute-start.18
  76.1 1.5 collective-permute-done.14.other_w_ref
  77.7 3.7 %shard_map.247 = (f32[2,6,768]{2,1,0:T(8,128)S(1)}, bf16[512,768]{1,0:T(8,128)(2,1)S(1)}, bf16[512,576]{1,0:T(8,128)(2,1)S(1)}, bf16[512,192]{1,0:T(8,128)(2,1)S(1)}, bf16[768,576]{1,0:T(8,128)(2,1)S(1)}) custom-call(s32[1]{0:T(128)} %bitcast.3.core_ref, s32[1]{0:T(128)} %bitcast.1.pair_ref, s32[1]{0:T(128)} %bitcast.2.high_ref, ...), custom_call_target="tpu_custom_call" | custom-call | flops 600000000 | bytes 1800000 | tf_op jit(solution)/shard_map/pallas_call | solution.py:141
  84.0 1.3 collective-permute-start.16
  86.2 5.9 %collective-permute-done.20 = bf16[16,48]{1,0:T(8,128)(2,1)S(1)} collective-permute-done((bf16[16,48]{1,0:T(8,128)(2,1)S(1)}, bf16[16,48]{1,0:T(8,128)(2,1)S(1)}, u32[]{:S(2)}, u32[]{:S(2)}) %collective-permute-start.20) | collective-permute-done | bytes 1568 | tf_op jit(solution)/shard_map/ppermute | solution.py:77
  96.3 9.1 %shard_map.248 = (f32[256,768]{1,0:T(8,128)}, f32[256,768]{1,0:T(8,128)}, f32[256,768]{1,0:T(8,128)}, bf16[256,768]{1,0:T(8,128)(2,1)}, bf16[4,96,768]{2,1,0:T(8...) custom-call(s32[1]{0:T(128)} %bitcast.me_ref, ...), custom_call_target="tpu_custom_call" | custom-call | flops 1200000000 | bytes 3600000 | tf_op jit(solution)/shard_map/pallas_call | solution.py:141
  112.1 1.2 add_convert_fusion.3.mine_ref
  113.4 1.3 collective-permute-start.23
  114.7 1.1 collective-permute-start.36
  115.8 8.8 %collective-permute-done.23.there_ref = bf16[256,768]{1,0:T(8,128)(2,1)S(1)} collective-permute-done((bf16[256,768]{1,0:T(8,128)(2,1)S(1)}, bf16[256,768]{1,0:T(8,128)(2,1)S(1)}, u32[]{:S(2)}, u32[]{:S(2)}) %collective-permute-start.23) | collective-permute-done | bytes 393248 | tf_op jit(solution)/shard_map/ppermute | solution.py:77
  129.3 8.4 %shard_map.250 = (bf16[4,96,768]{2,1,0:T(8,128)(2,1)S(1)}, bf16[4,96,768]{2,1,0:T(8,128)(2,1)}, f32[256,768]{1,0:T(8,128)S(1)}, bf16[256,768]{1,0:T(8,128)(2,1)S...) custom-call(s32[1]{0:T(128)} %bitcast.me_ref, s32[1]{0:T(128)} %bitcast.3.core_ref, s32[1]{0:T(128)} %bitcast.1.pair_ref, ...), custom_call_target="tpu_custom_call" | custom-call | flops 1200000000 | bytes 3600000 | tf_op jit(solution)/shard_map/pallas_call | solution.py:141
  141.3 1.3 collective-permute-start.37
  142.6 1.2 collective-permute-start.27
  144.8 1.6 collective-permute-done.27
  146.4 7.4 %collective-permute-done.28 = bf16[4,96,768]{2,1,0:T(8,128)(2,1)} collective-permute-done((bf16[4,96,768]{2,1,0:T(8,128)(2,1)}, bf16[4,96,768]{2,1,0:T(8,128)(2,1)}, u32[]{:S(2)}, u32[]{:S(2)}) %collective-permute-start.28) | collective-permute-done | bytes 589856 | tf_op jit(solution)/shard_map/ppermute | solution.py:77
  153.9 2.0 %add_convert_fusion.2 = bf16[4,96,768]{2,1,0:T(8,128)(2,1)} fusion(bf16[4,96,768]{2,1,0:T(8,128)(2,1)} %collective-permute-done.28, bf16[4,96,768]{2,1,0:T(8,128)(2,1)S(1)} %copy-done.18), kind=kLoop, calls=%fused_computation.7 | loop fusion | flops 1179648 | bytes 1769472 | tf_op jit(solution)/shard_map/convert_element_type | solution.py:697
  156.6 3.6 %all-to-all-start.2 = ((bf16[16,36,128]{2,1,0:T(8,128)(2,1)}), bf16[16,36,128]{2,1,0:T(8,128)(2,1)S(1)}, u32[]{:S(2)}, u32[]{:S(2)}) async-start(bf16[16,36,128]{2,1,0:T(8,128)(2,1)} %broadcast_in_dim.170), calls=%async_computation.2 | async-start | bytes 327680 | tf_op jit(solution)/shard_map/all_to_all | solution.py:701
  164.6 2.8 %collective-permute-start.38 = (bf16[1,96,768]{2,1,0:T(8,128)(2,1)}, bf16[1,96,768]{2,1,0:T(8,128)(2,1)}, u32[]{:S(2)}, u32[]{:S(2)}) collective-permute-start(bf16[1,96,768]{2,1,0:T(8,128)(2,1)} %get-tuple-element.135), channel_id=1, source_target_pairs={{0,8},{1,9},{2,10},{3,11},{4,12},{5,13},{6,14},{7,15},{8,0},{9,1},... | collective-permute-start | bytes 442376 | tf_op jit(solution)/shard_map/ppermute | solution.py:77
  167.4 1.6 collective-permute-start.31
  169.0 1.2 collective-permute-start.30
  170.5 1.7 add_bitcast_fusion
  173.2 2.6 %all-to-all-start.3 = ((f32[32,1,216]{2,1,0:T(1,128)}), f32[32,1,216]{2,1,0:T(1,128)S(1)}, u32[]{:S(2)}, u32[]{:S(2)}) async-start(f32[32,1,216]{2,1,0:T(1,128)} %all_to_all.34), calls=%async_computation.3 | async-start | bytes 65536 | tf_op jit(solution)/shard_map/all_to_all | solution.py:726
  179.4 1.8 collective-permute-start.32
  181.2 1.8 all-to-all-done.3
  184.8 1.2 collective-permute-start.41
  189.5 1.2 convert_add_fusion
  193.0 1.4 collective-permute-start.34
  195.3 1.5 collective-permute-done.34.refs_2_
  (321 shorter events, 61.9 us)
Async XLA Ops:
  4.1 17.0 %collective-permute-start = (bf16[1,24,1344]{2,1,0:T(8,128)(2,1)S(1)}, bf16[1,24,1344]{2,1,0:T(8,128)(2,1)S(1)}, u32[]{:S(2)}, u32[]{:S(2)}) collective-permute-start(bf16[1,24,1344]{2,1,0:T(8,128)(2,1)S(1)} %get-tuple-element.151), channel_id=1, source_target_pairs={{0,1},{1,0},{2,3},{3,2},{4,5},{5,4},{6,7},{7,6},{8,9},{9,8},{10,11... | collective-permute-start | bytes 193544 | tf_op jit(solution)/shard_map/ppermute | solution.py:77
  4.7 16.5 %collective-permute-start.1 = (bf16[1,24,1344]{2,1,0:T(8,128)(2,1)S(1)}, bf16[1,24,1344]{2,1,0:T(8,128)(2,1)S(1)}, u32[]{:S(2)}, u32[]{:S(2)}) collective-permute-start(bf16[1,24,1344]{2,1,0:T(8,128)(2,1)S(1)} %get-tuple-element.150), channel_id=1, source_target_pairs={{0,16},{1,17},{2,18},{3,19},{4,20},{5,21},{6,22},{7,23},{8,24},{9,... | collective-permute-start | bytes 193544 | tf_op jit(solution)/shard_map/ppermute | solution.py:77
  7.2 13.9 %collective-permute-start.2 = (bf16[1,24,1344]{2,1,0:T(8,128)(2,1)S(1)}, bf16[1,24,1344]{2,1,0:T(8,128)(2,1)S(1)}, u32[]{:S(2)}, u32[]{:S(2)}) collective-permute-start(bf16[1,24,1344]{2,1,0:T(8,128)(2,1)S(1)} %get-tuple-element.149), channel_id=1, source_target_pairs={{0,17},{1,16},{2,19},{3,18},{4,21},{5,20},{6,23},{7,22},{8,25},{9,... | collective-permute-start | bytes 193544 | tf_op jit(solution)/shard_map/ppermute | solution.py:77
  8.2 12.7 %all-to-all-start = ((bf16[16,1,216]{2,1,0:T(2,128)(2,1)}), bf16[16,1,216]{2,1,0:T(2,128)(2,1)S(1)}, u32[]{:S(2)}, u32[]{:S(2)}) async-start(bf16[16,1,216]{2,1,0:T(2,128)(2,1)} %copy.78), calls=%async_computation | async-start | bytes 32768 | tf_op jit(solution)/shard_map/all_to_all | solution.py:588
  14.5 15.3 %collective-permute-start.3 = (bf16[1,120,768]{2,1,0:T(8,128)(2,1)S(1)}, bf16[1,120,768]{2,1,0:T(8,128)(2,1)S(1)}, u32[]{:S(2)}, u32[]{:S(2)}) collective-permute-start(bf16[1,120,768]{2,1,0:T(8,128)(2,1)S(1)} %maximum_bitcast_fusion), channel_id=1, source_target_pairs={{0,8},{1,9},{2,10},{3,11},{4,12},{5,13},{6,14},{7,15},{8,0},{9,1},... | collective-permute-start | bytes 552968 | tf_op jit(solution)/shard_map/ppermute | solution.py:77
  17.4 15.6 %collective-permute-start.6 = (bf16[2,1,128,768]{3,2,1,0:T(8,128)(2,1)S(1)}, bf16[2,1,128,768]{3,2,1,0:T(8,128)(2,1)S(1)}, u32[]{:S(2)}, u32[]{:S(2)}) collective-permute-start(bf16[2,1,128,768]{3,2,1,0:T(8,128)(2,1)S(1)} %pad_maximum_fusion.1.own_ref), channel_id=1, source_target_pairs={{0,16},{1,17},{2,18},{3,19},{4,20},{5,21},{6,22},{7,23},{8,24},{9,... | collective-permute-start | bytes 1179656 | tf_op jit(solution)/shard_map/ppermute | solution.py:77
  21.6 10.4 %collective-permute-start.5 = (bf16[1,2,48,576]{3,2,1,0:T(8,128)(2,1)S(1)}, bf16[1,2,48,576]{3,2,1,0:T(8,128)(2,1)S(1)}, u32[]{:S(2)}, u32[]{:S(2)}) collective-permute-start(bf16[1,2,48,576]{3,2,1,0:T(8,128)(2,1)S(1)} %bitcast.217), channel_id=1, source_target_pairs={{0,8},{1,9},{2,10},{3,11},{4,12},{5,13},{6,14},{7,15},{8,0},{9,1},... | collective-permute-start | bytes 331784 | tf_op jit(solution)/shard_map/ppermute | solution.py:77
  31.1 1.9 collective-permute-start.4
  32.7 13.4 %collective-permute-start.10 = (bf16[2,120,768]{2,1,0:T(8,128)(2,1)}, bf16[2,120,768]{2,1,0:T(8,128)(2,1)}, u32[]{:S(2)}, u32[]{:S(2)}) collective-permute-start(bf16[2,120,768]{2,1,0:T(8,128)(2,1)} %pad_maximum_fusion.2), channel_id=1, source_target_pairs={{0,4},{1,5},{2,6},{3,7},{4,0},{5,1},{6,2},{7,3},{8,12},{9,13},{10,... | collective-permute-start | bytes 1105928 | tf_op jit(solution)/shard_map/ppermute | solution.py:77
  34.2 17.8 %all-to-all-start.1 = ((f32[16,1,4608]{2,1,0:T(1,128)}), f32[16,1,4608]{2,1,0:T(1,128)S(1)}, u32[]{:S(2)}, u32[]{:S(2)}) async-start(f32[16,1,4608]{2,1,0:T(1,128)} %all_to_all.30), calls=%async_computation.1 | async-start | bytes 589824 | tf_op jit(solution)/shard_map/all_to_all | solution.py:80
  42.0 14.6 %collective-permute-start.7 = (bf16[2,2,48,576]{3,2,1,0:T(8,128)(2,1)}, bf16[2,2,48,576]{3,2,1,0:T(8,128)(2,1)S(1)}, u32[]{:S(2)}, u32[]{:S(2)}) collective-permute-start(bf16[2,2,48,576]{3,2,1,0:T(8,128)(2,1)} %pad_maximum_fusion.9), channel_id=1, source_target_pairs={{0,4},{1,5},{2,6},{3,7},{4,0},{5,1},{6,2},{7,3},{8,12},{9,13},{10,... | collective-permute-start | bytes 663560 | tf_op jit(solution)/shard_map/ppermute | solution.py:77
  43.7 15.2 %collective-permute-start.12 = (bf16[1,2,48,768]{3,2,1,0:T(8,128)(2,1)}, bf16[1,2,48,768]{3,2,1,0:T(8,128)(2,1)}, u32[]{:S(2)}, u32[]{:S(2)}) collective-permute-start(bf16[1,2,48,768]{3,2,1,0:T(8,128)(2,1)} %bitcast.35), channel_id=1, source_target_pairs={{0,8},{1,9},{2,10},{3,11},{4,12},{5,13},{6,14},{7,15},{8,0},{9,1},... | collective-permute-start | bytes 442376 | tf_op jit(solution)/shard_map/ppermute | solution.py:77
  46.1 17.2 %collective-permute-start.8 = (bf16[2,1,256,768]{3,2,1,0:T(8,128)(2,1)S(1)}, bf16[2,1,256,768]{3,2,1,0:T(8,128)(2,1)S(1)}, u32[]{:S(2)}, u32[]{:S(2)}) collective-permute-start(bf16[2,1,256,768]{3,2,1,0:T(8,128)(2,1)S(1)} %bitcast.186), channel_id=1, source_target_pairs={{0,1},{1,0},{2,3},{3,2},{4,5},{5,4},{6,7},{7,6},{8,9},{9,8},{10,11... | collective-permute-start | bytes 2359304 | tf_op jit(solution)/shard_map/ppermute | solution.py:77
  47.2 24.9 %collective-permute-start.11 = (bf16[4,120,768]{2,1,0:T(8,128)(2,1)S(1)}, bf16[4,120,768]{2,1,0:T(8,128)(2,1)}, u32[]{:S(2)}, u32[]{:S(2)}) collective-permute-start(bf16[4,120,768]{2,1,0:T(8,128)(2,1)S(1)} %pad_maximum_fusion.refs_11_), channel_id=1, source_target_pairs={{0,2},{1,3},{2,0},{3,1},{4,6},{5,7},{6,4},{7,5},{8,10},{9,11},{10,... | collective-permute-start | bytes 2211848 | tf_op jit(solution)/shard_map/ppermute | solution.py:77
  60.4 8.7 %collective-permute-start.13 = (bf16[2,2,48,768]{3,2,1,0:T(8,128)(2,1)}, bf16[2,2,48,768]{3,2,1,0:T(8,128)(2,1)}, u32[]{:S(2)}, u32[]{:S(2)}) collective-permute-start(bf16[2,2,48,768]{3,2,1,0:T(8,128)(2,1)} %constant_dynamic-update-slice_fusion.2), channel_id=1, source_target_pairs={{0,4},{1,5},{2,6},{3,7},{4,0},{5,1},{6,2},{7,3},{8,12},{9,13},{10,... | collective-permute-start | bytes 884744 | tf_op jit(solution)/shard_map/ppermute | solution.py:77
  60.5 17.2 %collective-permute-start.14 = (bf16[4,2,48,576]{3,2,1,0:T(8,128)(2,1)}, bf16[4,2,48,576]{3,2,1,0:T(8,128)(2,1)}, u32[]{:S(2)}, u32[]{:S(2)}) collective-permute-start(bf16[4,2,48,576]{3,2,1,0:T(8,128)(2,1)} %constant_dynamic-update-slice_fusion.own_w_ref), channel_id=1, source_target_pairs={{0,2},{1,3},{2,0},{3,1},{4,6},{5,7},{6,4},{7,5},{8,10},{9,11},{10,... | collective-permute-start | bytes 1327112 | tf_op jit(solution)/shard_map/ppermute | solution.py:77
  64.5 11.6 %collective-permute-start.9 = (f32[2,1,3,768]{3,2,1,0:T(4,128)S(1)}, f32[2,1,3,768]{3,2,1,0:T(4,128)S(1)}, u32[]{:S(2)}, u32[]{:S(2)}) collective-permute-start(f32[2,1,3,768]{3,2,1,0:T(4,128)S(1)} %bitcast.193), channel_id=1, source_target_pairs={{0,1},{1,0},{2,3},{3,2},{4,5},{5,4},{6,7},{7,6},{8,9},{9,8},{10,11... | collective-permute-start | bytes 55304 | tf_op jit(solution)/shard_map/ppermute | solution.py:77
  70.1 25.3 %collective-permute-start.21 = (bf16[4,2,48,768]{3,2,1,0:T(8,128)(2,1)S(1)}, bf16[4,2,48,768]{3,2,1,0:T(8,128)(2,1)}, u32[]{:S(2)}, u32[]{:S(2)}) collective-permute-start(bf16[4,2,48,768]{3,2,1,0:T(8,128)(2,1)S(1)} %constant_dynamic-update-slice_fusion.4.refs_9_), channel_id=1, source_target_pairs={{0,2},{1,3},{2,0},{3,1},{4,6},{5,7},{6,4},{7,5},{8,10},{9,11},{10,... | collective-permute-start | bytes 1769480 | tf_op jit(solution)/shard_map/ppermute | solution.py:77
  73.0 19.2 %collective-permute-start.18 = (bf16[8,24,768]{2,1,0:T(8,128)(2,1)S(1)}, bf16[8,24,768]{2,1,0:T(8,128)(2,1)S(1)}, u32[]{:S(2)}, u32[]{:S(2)}) collective-permute-start(bf16[8,24,768]{2,1,0:T(8,128)(2,1)S(1)} %bitcast.191), channel_id=1, source_target_pairs={{0,16},{1,17},{2,18},{3,19},{4,20},{5,21},{6,22},{7,23},{8,24},{9,... | collective-permute-start | bytes 884744 | tf_op jit(solution)/shard_map/ppermute | solution.py:77
  84.0 9.2 %collective-permute-start.16 = (bf16[512,192]{1,0:T(8,128)(2,1)S(1)}, bf16[512,192]{1,0:T(8,128)(2,1)S(1)}, u32[]{:S(2)}, u32[]{:S(2)}) collective-permute-start(bf16[512,192]{1,0:T(8,128)(2,1)S(1)} %get-tuple-element.75.refs_0_.att_ref), channel_id=1, source_target_pairs={{0,16},{1,17},{2,18},{3,19},{4,20},{5,21},{6,22},{7,23},{8,24},{9,... | collective-permute-start | bytes 589832 | tf_op jit(solution)/shard_map/ppermute | solution.py:77
  85.3 9.9 %collective-permute-start.15 = (bf16[512,192]{1,0:T(8,128)(2,1)S(1)}, bf16[512,192]{1,0:T(8,128)(2,1)S(1)}, u32[]{:S(2)}, u32[]{:S(2)}) collective-permute-start(bf16[512,192]{1,0:T(8,128)(2,1)S(1)} %get-tuple-element.75.refs_0_.att_ref), channel_id=1, source_target_pairs={{0,1},{1,0},{2,3},{3,2},{4,5},{5,4},{6,7},{7,6},{8,9},{9,8},{10,11... | collective-permute-start | bytes 589832 | tf_op jit(solution)/shard_map/ppermute | solution.py:77
  85.4 6.7 %collective-permute-start.20 = (bf16[16,48]{1,0:T(8,128)(2,1)S(1)}, bf16[16,48]{1,0:T(8,128)(2,1)S(1)}, u32[]{:S(2)}, u32[]{:S(2)}) collective-permute-start(bf16[16,48]{1,0:T(8,128)(2,1)S(1)} %slice.173), channel_id=1, source_target_pairs={{0,16},{1,17},{2,18},{3,19},{4,20},{5,21},{6,22},{7,23},{8,24},{9,... | collective-permute-start | bytes 4616 | tf_op jit(solution)/shard_map/ppermute | solution.py:77
  93.0 2.2 %collective-permute-start.19 = (bf16[2,8,24,768]{3,2,1,0:T(8,128)(2,1)}, bf16[2,8,24,768]{3,2,1,0:T(8,128)(2,1)S(1)}, u32[]{:S(2)}, u32[]{:S(2)}) collective-permute-start(bf16[2,8,24,768]{3,2,1,0:T(8,128)(2,1)} %bitcast_dynamic-update-slice_fusion.2), channel_id=1, source_target_pairs={{0,1},{1,0},{2,3},{3,2},{4,5},{5,4},{6,7},{7,6},{8,9},{9,8},{10,11... | collective-permute-start | bytes 1769480 | tf_op jit(solution)/shard_map/ppermute | solution.py:77
  93.2 2.2 %collective-permute-start.17 = (bf16[512,192]{1,0:T(8,128)(2,1)S(1)}, bf16[512,192]{1,0:T(8,128)(2,1)S(1)}, u32[]{:S(2)}, u32[]{:S(2)}) collective-permute-start(bf16[512,192]{1,0:T(8,128)(2,1)S(1)} %collective-permute-done.16.refs_2_), channel_id=1, source_target_pairs={{0,1},{1,0},{2,3},{3,2},{4,5},{5,4},{6,7},{7,6},{8,9},{9,8},{10,11... | collective-permute-start | bytes 589832 | tf_op jit(solution)/shard_map/ppermute | solution.py:77
  110.2 1.9 collective-permute-start.22
  110.8 16.8 %collective-permute-start.42 = (bf16[384,768]{1,0:T(8,128)(2,1)}, bf16[384,768]{1,0:T(8,128)(2,1)S(1)}, u32[]{:S(2)}, u32[]{:S(2)}) collective-permute-start(bf16[384,768]{1,0:T(8,128)(2,1)} %copy-done.22), channel_id=1, source_target_pairs={{0,2},{1,3},{2,0},{3,1},{4,6},{5,7},{6,4},{7,5},{8,10},{9,11},{10,... | collective-permute-start | bytes 1769480 | tf_op jit(solution)/shard_map/ppermute | solution.py:77
  113.4 11.2 %collective-permute-start.23 = (bf16[256,768]{1,0:T(8,128)(2,1)S(1)}, bf16[256,768]{1,0:T(8,128)(2,1)S(1)}, u32[]{:S(2)}, u32[]{:S(2)}) collective-permute-start(bf16[256,768]{1,0:T(8,128)(2,1)S(1)} %add_convert_fusion.3.mine_ref), channel_id=1, source_target_pairs={{0,16},{1,17},{2,18},{3,19},{4,20},{5,21},{6,22},{7,23},{8,24},{9,... | collective-permute-start | bytes 1179656 | tf_op jit(solution)/shard_map/ppermute | solution.py:77
  114.7 25.6 %collective-permute-start.36 = (bf16[4,96,768]{2,1,0:T(8,128)(2,1)}, bf16[4,96,768]{2,1,0:T(8,128)(2,1)S(1)}, u32[]{:S(2)}, u32[]{:S(2)}) collective-permute-start(bf16[4,96,768]{2,1,0:T(8,128)(2,1)} %copy-done.21), channel_id=1, source_target_pairs={{0,2},{1,3},{2,0},{3,1},{4,6},{5,7},{6,4},{7,5},{8,10},{9,11},{10,... | collective-permute-start | bytes 1769480 | tf_op jit(solution)/shard_map/ppermute | solution.py:77
  115.8 26.8 %collective-permute-start.25 = (bf16[256,768]{1,0:T(8,128)(2,1)}, bf16[256,768]{1,0:T(8,128)(2,1)S(1)}, u32[]{:S(2)}, u32[]{:S(2)}) collective-permute-start(bf16[256,768]{1,0:T(8,128)(2,1)} %copy-done.23), channel_id=1, source_target_pairs={{0,1},{1,0},{2,3},{3,2},{4,5},{5,4},{6,7},{7,6},{8,9},{9,8},{10,11... | collective-permute-start | bytes 1179656 | tf_op jit(solution)/shard_map/ppermute | solution.py:77
  127.9 11.2 %collective-permute-start.43 = (bf16[2,96,768]{2,1,0:T(8,128)(2,1)S(1)}, bf16[2,96,768]{2,1,0:T(8,128)(2,1)S(1)}, u32[]{:S(2)}, u32[]{:S(2)}) collective-permute-start(bf16[2,96,768]{2,1,0:T(8,128)(2,1)S(1)} %get-tuple-element.129), channel_id=1, source_target_pairs={{0,4},{1,5},{2,6},{3,7},{4,0},{5,1},{6,2},{7,3},{8,12},{9,13},{10,... | collective-permute-start | bytes 884744 | tf_op jit(solution)/shard_map/ppermute | solution.py:77
  137.8 4.8 %collective-permute-start.26 = (f32[1,3,768]{2,1,0:T(4,128)S(1)}, f32[1,3,768]{2,1,0:T(4,128)S(1)}, u32[]{:S(2)}, u32[]{:S(2)}) collective-permute-start(f32[1,3,768]{2,1,0:T(4,128)S(1)} %pad_maximum_fusion.11), channel_id=1, source_target_pairs={{0,1},{1,0},{2,3},{3,2},{4,5},{5,4},{6,7},{7,6},{8,9},{9,8},{10,11... | collective-permute-start | bytes 27656 | tf_op jit(solution)/shard_map/ppermute | solution.py:77
  138.0 15.8 %collective-permute-start.28 = (bf16[4,96,768]{2,1,0:T(8,128)(2,1)}, bf16[4,96,768]{2,1,0:T(8,128)(2,1)}, u32[]{:S(2)}, u32[]{:S(2)}) collective-permute-start(bf16[4,96,768]{2,1,0:T(8,128)(2,1)} %get-tuple-element.95), channel_id=1, source_target_pairs={{0,2},{1,3},{2,0},{3,1},{4,6},{5,7},{6,4},{7,5},{8,10},{9,11},{10,... | collective-permute-start | bytes 1769480 | tf_op jit(solution)/shard_map/ppermute | solution.py:77
  139.9 30.6 %collective-permute-start.44 = (bf16[1,96,768]{2,1,0:T(8,128)(2,1)}, bf16[1,96,768]{2,1,0:T(8,128)(2,1)}, u32[]{:S(2)}, u32[]{:S(2)}) collective-permute-start(bf16[1,96,768]{2,1,0:T(8,128)(2,1)} %get-tuple-element.133), channel_id=1, source_target_pairs={{0,8},{1,9},{2,10},{3,11},{4,12},{5,13},{6,14},{7,15},{8,0},{9,1},... | collective-permute-start | bytes 442376 | tf_op jit(solution)/shard_map/ppermute | solution.py:77
  141.3 21.0 %collective-permute-start.37 = (bf16[2,96,768]{2,1,0:T(8,128)(2,1)}, bf16[2,96,768]{2,1,0:T(8,128)(2,1)}, u32[]{:S(2)}, u32[]{:S(2)}) collective-permute-start(bf16[2,96,768]{2,1,0:T(8,128)(2,1)} %get-tuple-element.131), channel_id=1, source_target_pairs={{0,4},{1,5},{2,6},{3,7},{4,0},{5,1},{6,2},{7,3},{8,12},{9,13},{10,... | collective-permute-start | bytes 884744 | tf_op jit(solution)/shard_map/ppermute | solution.py:77
  142.6 17.8 %collective-permute-start.29 = (bf16[256,768]{1,0:T(8,128)(2,1)S(1)}, bf16[256,768]{1,0:T(8,128)(2,1)}, u32[]{:S(2)}, u32[]{:S(2)}) collective-permute-start(bf16[256,768]{1,0:T(8,128)(2,1)S(1)} %get-tuple-element.98), channel_id=1, source_target_pairs={{0,1},{1,0},{2,3},{3,2},{4,5},{5,4},{6,7},{7,6},{8,9},{9,8},{10,11... | collective-permute-start | bytes 1179656 | tf_op jit(solution)/shard_map/ppermute | solution.py:77
  142.6 3.8 %collective-permute-start.27 = (f32[1,3,768]{2,1,0:T(4,128)S(1)}, f32[1,3,768]{2,1,0:T(4,128)S(1)}, u32[]{:S(2)}, u32[]{:S(2)}) collective-permute-start(f32[1,3,768]{2,1,0:T(4,128)S(1)} %fusion.30), channel_id=1, source_target_pairs={{0,16},{1,17},{2,18},{3,19},{4,20},{5,21},{6,22},{7,23},{8,24},{9,... | collective-permute-start | bytes 27656 | tf_op jit(solution)/shard_map/ppermute | solution.py:77
  156.6 15.6 %all-to-all-start.2 = ((bf16[16,36,128]{2,1,0:T(8,128)(2,1)}), bf16[16,36,128]{2,1,0:T(8,128)(2,1)S(1)}, u32[]{:S(2)}, u32[]{:S(2)}) async-start(bf16[16,36,128]{2,1,0:T(8,128)(2,1)} %broadcast_in_dim.170), calls=%async_computation.2 | async-start | bytes 327680 | tf_op jit(solution)/shard_map/all_to_all | solution.py:701
  164.6 18.4 %collective-permute-start.38 = (bf16[1,96,768]{2,1,0:T(8,128)(2,1)}, bf16[1,96,768]{2,1,0:T(8,128)(2,1)}, u32[]{:S(2)}, u32[]{:S(2)}) collective-permute-start(bf16[1,96,768]{2,1,0:T(8,128)(2,1)} %get-tuple-element.135), channel_id=1, source_target_pairs={{0,8},{1,9},{2,10},{3,11},{4,12},{5,13},{6,14},{7,15},{8,0},{9,1},... | collective-permute-start | bytes 442376 | tf_op jit(solution)/shard_map/ppermute | solution.py:77
  167.4 10.9 %collective-permute-start.31 = (bf16[2,96,768]{2,1,0:T(8,128)(2,1)S(1)}, bf16[2,96,768]{2,1,0:T(8,128)(2,1)}, u32[]{:S(2)}, u32[]{:S(2)}) collective-permute-start(bf16[2,96,768]{2,1,0:T(8,128)(2,1)S(1)} %dynamic-slice_bitcast_fusion.4), channel_id=1, source_target_pairs={{0,4},{1,5},{2,6},{3,7},{4,0},{5,1},{6,2},{7,3},{8,12},{9,13},{10,... | collective-permute-start | bytes 884744 | tf_op jit(solution)/shard_map/ppermute | solution.py:77
  169.0 20.5 %collective-permute-start.30 = (bf16[1,2,1,128,768]{4,3,2,1,0:T(8,128)(2,1)}, bf16[1,2,1,128,768]{4,3,2,1,0:T(8,128)(2,1)}, u32[]{:S(2)}, u32[]{:S(2)}) collective-permute-start(bf16[1,2,1,128,768]{4,3,2,1,0:T(8,128)(2,1)} %fusion.15), channel_id=1, source_target_pairs={{0,16},{1,17},{2,18},{3,19},{4,20},{5,21},{6,22},{7,23},{8,24},{9,... | collective-permute-start | bytes 1179656 | tf_op jit(solution)/shard_map/ppermute | solution.py:77
  173.2 9.8 %all-to-all-start.3 = ((f32[32,1,216]{2,1,0:T(1,128)}), f32[32,1,216]{2,1,0:T(1,128)S(1)}, u32[]{:S(2)}, u32[]{:S(2)}) async-start(f32[32,1,216]{2,1,0:T(1,128)} %all_to_all.34), calls=%async_computation.3 | async-start | bytes 65536 | tf_op jit(solution)/shard_map/all_to_all | solution.py:726
  179.4 13.1 %collective-permute-start.32 = (bf16[1,96,768]{2,1,0:T(8,128)(2,1)S(1)}, bf16[1,96,768]{2,1,0:T(8,128)(2,1)S(1)}, u32[]{:S(2)}, u32[]{:S(2)}) collective-permute-start(bf16[1,96,768]{2,1,0:T(8,128)(2,1)S(1)} %get-tuple-element.141), channel_id=1, source_target_pairs={{0,8},{1,9},{2,10},{3,11},{4,12},{5,13},{6,14},{7,15},{8,0},{9,1},... | collective-permute-start | bytes 442376 | tf_op jit(solution)/shard_map/ppermute | solution.py:77
  184.0 3.9 %collective-permute-start.39 = (bf16[24,768]{1,0:T(8,128)(2,1)S(1)}, bf16[24,768]{1,0:T(8,128)(2,1)S(1)}, u32[]{:S(2)}, u32[]{:S(2)}) collective-permute-start(bf16[24,768]{1,0:T(8,128)(2,1)S(1)} %get-tuple-element.162), channel_id=1, source_target_pairs={{0,1},{1,0},{2,3},{3,2},{4,5},{5,4},{6,7},{7,6},{8,9},{9,8},{10,11... | collective-permute-start | bytes 110600 | tf_op jit(solution)/shard_map/ppermute | solution.py:77
  184.2 4.4 %collective-permute-start.40 = (bf16[24,768]{1,0:T(8,128)(2,1)S(1)}, bf16[24,768]{1,0:T(8,128)(2,1)S(1)}, u32[]{:S(2)}, u32[]{:S(2)}) collective-permute-start(bf16[24,768]{1,0:T(8,128)(2,1)S(1)} %get-tuple-element.161), channel_id=1, source_target_pairs={{0,16},{1,17},{2,18},{3,19},{4,20},{5,21},{6,22},{7,23},{8,24},{9,... | collective-permute-start | bytes 110600 | tf_op jit(solution)/shard_map/ppermute | solution.py:77
  184.8 3.8 %collective-permute-start.41 = (bf16[24,768]{1,0:T(8,128)(2,1)S(1)}, bf16[24,768]{1,0:T(8,128)(2,1)S(1)}, u32[]{:S(2)}, u32[]{:S(2)}) collective-permute-start(bf16[24,768]{1,0:T(8,128)(2,1)S(1)} %get-tuple-element.160), channel_id=1, source_target_pairs={{0,17},{1,16},{2,19},{3,18},{4,21},{5,20},{6,23},{7,22},{8,25},{9,... | collective-permute-start | bytes 110600 | tf_op jit(solution)/shard_map/ppermute | solution.py:77
  192.7 2.6 %collective-permute-start.33 = (bf16[24,576]{1,0:T(8,128)(2,1)S(1)}, bf16[24,576]{1,0:T(8,128)(2,1)S(1)}, u32[]{:S(2)}, u32[]{:S(2)}) collective-permute-start(bf16[24,576]{1,0:T(8,128)(2,1)S(1)} %get-tuple-element.166), channel_id=1, source_target_pairs={{0,1},{1,0},{2,3},{3,2},{4,5},{5,4},{6,7},{7,6},{8,9},{9,8},{10,11... | collective-permute-start | bytes 82952 | tf_op jit(solution)/shard_map/ppermute | solution.py:77
  193.0 3.9 %collective-permute-start.34 = (bf16[24,576]{1,0:T(8,128)(2,1)S(1)}, bf16[24,576]{1,0:T(8,128)(2,1)S(1)}, u32[]{:S(2)}, u32[]{:S(2)}) collective-permute-start(bf16[24,576]{1,0:T(8,128)(2,1)S(1)} %get-tuple-element.165), channel_id=1, source_target_pairs={{0,16},{1,17},{2,18},{3,19},{4,20},{5,21},{6,22},{7,23},{8,24},{9,... | collective-permute-start | bytes 82952 | tf_op jit(solution)/shard_map/ppermute | solution.py:77
  194.3 3.6 %collective-permute-start.35 = (bf16[24,576]{1,0:T(8,128)(2,1)S(1)}, bf16[24,576]{1,0:T(8,128)(2,1)S(1)}, u32[]{:S(2)}, u32[]{:S(2)}) collective-permute-start(bf16[24,576]{1,0:T(8,128)(2,1)S(1)} %get-tuple-element.164), channel_id=1, source_target_pairs={{0,17},{1,16},{2,19},{3,18},{4,21},{5,20},{6,23},{7,22},{8,25},{9,... | collective-permute-start | bytes 82952 | tf_op jit(solution)/shard_map/ppermute | solution.py:77
  (46 other events, 295.9 us)
